TPU v7x, 128 devices: a whole 4x4x4 slice. The times are simulated.
128 devices in a mesh: dp: 4 (over x), expert: 16 (over z, y), tensor: 2 (over core).
Axes of the slice: x: 4, y: 4, z: 4, core: 2. Of those that a mesh axis runs over, the one named last changes fastest.
Arguments:
- tokens: bfloat16 [8192, 2048], P(('dp', 'expert')), may hold values from -6 to 6
- expert_ids: int32 [8192, 8], P(('dp', 'expert')), may hold values from 0 to 63, as said below
- gates: float32 [8192, 8], P(('dp', 'expert')), may hold values from 0.05 to 0.5
- token_weight: float32 [8192], P(('dp', 'expert')), may hold values from 0.25 to 4
- w_gate: bfloat16 [64, 2048, 768], P(('dp', 'expert'), None, 'tensor'), may hold values from -0.125 to 0.125
- w_up: bfloat16 [64, 2048, 768], P(('dp', 'expert'), None, 'tensor'), may hold values from -0.125 to 0.125
- w_down: bfloat16 [64, 768, 2048], P(('dp', 'expert'), 'tensor'), may hold values from -0.21875 to 0.21875
- v_gate: bfloat16 [64, 2048, 768], P(('dp', 'expert'), None, 'tensor'), may hold values from -0.125 to 0.125
- v_up: bfloat16 [64, 2048, 768], P(('dp', 'expert'), None, 'tensor'), may hold values from -0.125 to 0.125
- v_down: bfloat16 [64, 768, 2048], P(('dp', 'expert'), 'tensor'), may hold values from -0.21875 to 0.21875
Outputs:
- gv_gate: float32 [64, 2048, 768], P(('dp', 'expert'), None, 'tensor')
- gv_up: float32 [64, 2048, 768], P(('dp', 'expert'), None, 'tensor')
- gv_down: float32 [64, 768, 2048], P(('dp', 'expert'), 'tensor')
- tangent: bfloat16 [8192, 2048], P(('dp', 'expert'), 'tensor')
Inputs may be any that keep to these rules, and one draw needn't show every extreme that they name: `expert_ids`: each row names 8 different experts. Among the 128 rows of one index of dp and expert (aligned blocks of rows) no expert is named more than 48 times, and one expert is named exactly 48 times by the rows of every such block.
All inputs are finite; a program needn't handle non-finite values.
Results may differ from a plain program's by a relative error of at most 0.0063.
Values may be sent and summed in bfloat16 or wider, within the bound.
No kernel may reach another device: no remote copies, remote signals or barrier semaphores. Data moves between devices by JAX's collectives and lax.ppermute only.
A program may use at most 256 MiB of HBM per device.

v0:
```python
import jax
import jax.numpy as jnp
from jax import lax
from jax.sharding import PartitionSpec as P

BLOCK = 128


def product(left, right):
    return jnp.dot(left, right, preferred_element_type=jnp.float32)


def contract_rows(left, right):
    return lax.dot_general(
        left, right, (((0,), (0,)), ((), ())), preferred_element_type=jnp.float32
    )


def silu_parts(pre_gate):
    sigma = jax.nn.sigmoid(pre_gate)
    return (pre_gate * sigma, sigma * (1.0 + pre_gate * (1.0 - sigma)))


def move_rows(outgoing):
    return lax.all_to_all(outgoing, ("dp", "expert"), split_axis=0, concat_axis=0, tiled=True)


def body(tokens, expert_ids, gates, token_weight, w_gate, w_up, w_down, v_gate, v_up, v_down):
    tok_count, width = tokens.shape
    picks = expert_ids.shape[1]
    dp_count = lax.axis_size("dp")
    groups = dp_count * lax.axis_size("expert")
    slot_cap = min(3 * tok_count * picks // groups, tok_count)
    row_count = tok_count * picks
    packed_len = groups * slot_cap
    half = width // lax.axis_size("tensor")
    col_start = lax.axis_index("tensor") * half
    flat_ids = expert_ids.reshape(row_count)
    labels = jnp.arange(groups, dtype=jnp.int32)
    hits = (flat_ids[:, None] == labels[None, :]).astype(jnp.int32)
    earlier = jnp.cumsum(hits, axis=0) - hits
    position = jnp.sum(earlier * hits, axis=1)
    counts = jnp.sum(hits, axis=0)
    slots = flat_ids * slot_cap + position
    owners = jnp.arange(row_count, dtype=jnp.int32) // picks
    send_width = tokens.shape[1]
    outgoing = jnp.zeros((packed_len, send_width), jnp.bfloat16).at[slots].set(tokens[owners])
    arrived, arrived_counts = (
        lax.all_to_all(outgoing, ("dp", "expert"), split_axis=0, concat_axis=0, tiled=True),
        lax.all_to_all(counts, ("dp", "expert"), split_axis=0, concat_axis=0, tiled=True),
    )
    ends = jnp.cumsum(arrived_counts)
    starts = ends - arrived_counts
    total = ends[-1]
    spots = jnp.arange(packed_len, dtype=jnp.int32)
    passed = spots[:, None] >= ends[None, :]
    source = jnp.minimum(jnp.sum(passed.astype(jnp.int32), axis=1), groups - 1)
    start_of = jnp.sum(jnp.where(passed, arrived_counts[None, :], 0), axis=1)
    live = spots < total
    picked = jnp.where(live, source * slot_cap + spots - start_of, 0)
    packed_x = jnp.where(live[:, None], arrived[picked], jnp.zeros((), jnp.bfloat16))
    gate_mat = w_gate[0]
    up_mat = w_up[0]
    down_mat = w_down[0]
    vgate_mat = v_gate[0]
    vup_mat = v_up[0]
    vdown_mat = v_down[0]
    hidden = gate_mat.shape[1]
    block_count = (total + BLOCK - 1) // BLOCK

    def forward(block_index, carry):
        out_rows, gate_store, up_store = carry
        start = block_index * BLOCK
        rows_x = lax.dynamic_slice_in_dim(packed_x, start, BLOCK, 0)
        pre_gate = product(rows_x, gate_mat)
        pre_up = product(rows_x, up_mat)
        d_gate = product(rows_x, vgate_mat)
        d_up = product(rows_x, vup_mat)
        silu_g, slope_g = silu_parts(pre_gate)
        act = (silu_g * pre_up).astype(jnp.bfloat16)
        d_act = (slope_g * d_gate * pre_up + silu_g * d_up).astype(jnp.bfloat16)
        part = (product(d_act, down_mat) + product(act, vdown_mat)).astype(jnp.bfloat16)
        out_rows = lax.dynamic_update_slice_in_dim(out_rows, part, start, 0)
        gate_store = lax.dynamic_update_slice_in_dim(gate_store, pre_gate, start, 0)
        up_store = lax.dynamic_update_slice_in_dim(up_store, pre_up, start, 0)
        return (out_rows, gate_store, up_store)

    initial = (
        jnp.zeros((packed_len, width), jnp.bfloat16),
        jnp.zeros((packed_len, hidden), jnp.float32),
        jnp.zeros((packed_len, hidden), jnp.float32),
    )
    out_rows, gate_store, up_store = lax.fori_loop(0, block_count, forward, initial)
    within = spots % slot_cap
    slot_counts = jnp.repeat(arrived_counts, slot_cap)
    slot_starts = jnp.repeat(starts, slot_cap)
    slot_live = within < slot_counts
    back_index = jnp.where(slot_live, slot_starts + within, 0)
    returning = jnp.where(slot_live[:, None], out_rows[back_index], jnp.zeros((), jnp.bfloat16))
    returned = move_rows(returning)
    mine = returned[slots].astype(jnp.float32).reshape(tok_count, picks, width)
    tangent_part = jnp.sum(gates[:, :, None] * mine, axis=1)
    tangent_full = lax.psum(tangent_part, "tensor")
    tangent = lax.dynamic_slice_in_dim(tangent_full, col_start, half, 1).astype(jnp.bfloat16)
    scaled = token_weight[:, None] * tangent_full
    weighted = (gates.reshape(row_count)[:, None] * scaled[owners]).astype(jnp.bfloat16)
    sending = jnp.zeros((packed_len, weighted.shape[1]), jnp.bfloat16).at[slots].set(weighted)
    arrived_q = move_rows(sending)
    packed_q = jnp.where(live[:, None], arrived_q[picked], jnp.zeros((), jnp.bfloat16))

    def backward(block_index, sums):
        start = block_index * BLOCK
        rows_x = lax.dynamic_slice_in_dim(packed_x, start, BLOCK, 0)
        rows_q = lax.dynamic_slice_in_dim(packed_q, start, BLOCK, 0)
        pre_gate = lax.dynamic_slice_in_dim(gate_store, start, BLOCK, 0)
        pre_up = lax.dynamic_slice_in_dim(up_store, start, BLOCK, 0)
        silu_g, slope_g = silu_parts(pre_gate)
        act = (silu_g * pre_up).astype(jnp.bfloat16)
        back = lax.dot_general(
            rows_q, down_mat, (((1,), (1,)), ((), ())), preferred_element_type=jnp.float32
        )
        grad_gate = (back * pre_up * slope_g).astype(jnp.bfloat16)
        grad_up = (back * silu_g).astype(jnp.bfloat16)
        return (
            sums[0] + contract_rows(rows_x, grad_gate),
            sums[1] + contract_rows(rows_x, grad_up),
            sums[2] + contract_rows(act, rows_q),
        )

    zero_sums = (
        jnp.zeros((width, hidden), jnp.float32),
        jnp.zeros((width, hidden), jnp.float32),
        jnp.zeros((hidden, width), jnp.float32),
    )
    sums = lax.fori_loop(0, block_count, backward, zero_sums)
    factor = 1.0 / (tok_count * picks) ** 0.5
    return ((factor * sums[0])[None], (factor * sums[1])[None], (factor * sums[2])[None], tangent)


def solution(mesh):
    in_specs = (
        P(("dp", "expert"), None),
        P(("dp", "expert"), None),
        P(("dp", "expert"), None),
        P(("dp", "expert")),
        P(("dp", "expert"), None, "tensor"),
        P(("dp", "expert"), None, "tensor"),
        P(("dp", "expert"), "tensor", None),
        P(("dp", "expert"), None, "tensor"),
        P(("dp", "expert"), None, "tensor"),
        P(("dp", "expert"), "tensor", None),
    )
    out_specs = (
        P(("dp", "expert"), None, "tensor"),
        P(("dp", "expert"), None, "tensor"),
        P(("dp", "expert"), "tensor", None),
        P(("dp", "expert"), "tensor"),
    )
    return jax.shard_map(body, mesh=mesh, in_specs=in_specs, out_specs=out_specs, check_vma=False)
```

profile of v0, /device:TPU:114, one launch (start us, length us, event | category | flops | bytes accessed | tf_op | source)
XLA Modules:
  0.0 1512.4 jit_solution(13365426375910505730)
XLA Ops:
  8.2 18.0 %reduce-window.11 = s32[64,8,128]{2,1,0:T(8,128)S(1)} reduce-window(s32[64,8,128]{2,1,0:T(8,128)S(1)} %fusion.48, s32[]{:T(128)} %constant.57.clone.1), window={size=1x1x128 pad=0_0x0_0x127_0}, to_apply=%region_2.3 | reduce-window | flops 8323072 | bytes 524292 | tf_op jit(solution)/shard_map/reduce-window.1
  27.7 10.0 all-to-all-start
  38.6 27.3 %scatter_custom_fusion = bf16[3072,2048]{1,0:T(8,128)(2,1)} fusion(s32[1024]{0:T(1024)S(1)} %bitcast.78, bf16[]{:T(256)} %constant.93.clone.1, bf16[128,2048]{1,0:T(8,128)(2,1)S(1)} %copy-done, s32[1024]{0:T(1024)S(1)} %broadcast_clamp_fusion.3), kind=kCustom, calls=%fused_computation.63 | custom fusion | bytes 12582914 | tf_op jit(solution)/shard_map/scatter | solution.py:47
  65.9 10.5 all-to-all-start.1
  81.2 162.9 %all-to-all-done.1 = bf16[64,48,2048]{2,1,0:T(8,128)(2,1)} async-done(((bf16[64,48,2048]{2,1,0:T(8,128)(2,1)}), bf16[64,48,2048]{2,1,0:T(8,128)(2,1)}, u32[]{:S(2)}, u32[]{:S(2)}) %all-to-all-start.1) | async-done | bytes 12582944 | tf_op jit(solution)/shard_map/all_to_all | solution.py:49
  244.1 30.0 %gather_fusion = bf16[3072,2048]{1,0:T(8,128)(2,1)} fusion(bf16[3072,2048]{1,0:T(8,128)(2,1)} %bitcast.9, s32[3072]{0:T(1024)S(1)} %broadcast_clamp_fusion.1), kind=kCustom, calls=%fused_computation.1 | custom fusion | bytes 25178112 | tf_op jit(solution)/shard_map/gather | solution.py:61
  274.1 11.0 broadcast_select_fusion.1
  285.1 6.2 broadcast.251
  296.3 290.2 %while.28 = (s32[]{:T(128)}, bf16[3072,2048]{1,0:T(8,128)(2,1)}, f32[3072,384]{1,0:T(8,128)}, f32[3072,384]{1,0:T(8,128)}, s32[]{:T(128)}, /*index=5*/bf16[3072,...) while((s32[]{:T(128)}, bf16[3072,2048]{1,0:T(8,128)(2,1)}, ...), condition=%wide.region_9.10_spmd, body=%wide.region_8.9_spmd.sunk | while | flops 1209565184 | bytes 22612204 | solution.py:93
  586.4 30.0 %gather_fusion.1 = bf16[3072,2048]{1,0:T(8,128)(2,1)} fusion(bf16[3072,2048]{1,0:T(8,128)(2,1)} %get-tuple-element.124, s32[3072]{0:T(1024)S(1)} %broadcast_clamp_fusion), kind=kCustom, calls=%fused_computation.2 | custom fusion | bytes 25178112 | tf_op jit(solution)/shard_map/gather | solution.py:99
  616.5 10.7 broadcast_select_fusion.2
  627.2 8.8 all-to-all-start.2
  636.3 169.7 %all-to-all-done.2 = bf16[64,48,2048]{2,1,0:T(8,128)(2,1)} async-done(((bf16[64,48,2048]{2,1,0:T(8,128)(2,1)}), bf16[64,48,2048]{2,1,0:T(8,128)(2,1)}, u32[]{:S(2)}, u32[]{:S(2)}) %all-to-all-start.2) | async-done | bytes 12582944 | tf_op jit(solution)/shard_map/all_to_all | solution.py:25
  806.0 15.0 gather_fusion.2
  821.0 7.4 fusion.39
  828.5 32.4 %all-reduce.2.cloned.1.call-done = f32[128,2048]{1,0:T(8,128)} async-done(((f32[128,2048]{1,0:T(8,128)}), f32[128,2048]{1,0:T(8,128)}) %all-reduce.2.cloned.1.call-update) | async-done | bytes 1048592 | tf_op jit(solution)/shard_map/psum | solution.py:103
  862.3 21.8 %scatter_custom_fusion.1 = bf16[3072,2048]{1,0:T(8,128)(2,1)} fusion(s32[1024]{0:T(1024)S(1)} %bitcast.80, bf16[]{:T(256)} %constant.93.clone.1, f32[1024]{0:T(1024)S(1)} %mul.133, f32[128,2048]{1,0:T(8,128)S(1)} %broadcast_multiply_fusion, s32[1024]{0:T(1024)S(1)} %broadcast_clamp_fusion.3), kind=kCustom, calls=%fused_computation.61 | custom fusion | flops 4194304 | bytes 13639682 | tf_op jit(solution)/shard_map/scatter | solution.py:107
  884.1 10.6 all-to-all-start.3
  896.5 189.6 %all-to-all-done.3 = bf16[64,48,2048]{2,1,0:T(8,128)(2,1)} async-done(((bf16[64,48,2048]{2,1,0:T(8,128)(2,1)}), bf16[64,48,2048]{2,1,0:T(8,128)(2,1)}, u32[]{:S(2)}, u32[]{:S(2)}) %all-to-all-start.3) | async-done | bytes 12582944 | tf_op jit(solution)/shard_map/all_to_all | solution.py:25
  1086.1 30.0 %gather_fusion.3 = bf16[3072,2048]{1,0:T(8,128)(2,1)} fusion(bf16[3072,2048]{1,0:T(8,128)(2,1)} %bitcast.24, s32[3072]{0:T(1024)S(1)} %broadcast_clamp_fusion.1), kind=kCustom, calls=%fused_computation.5 | custom fusion | bytes 25178112 | tf_op jit(solution)/shard_map/gather | solution.py:109
  1116.1 11.0 broadcast_select_fusion
  1132.9 363.1 %while.29 = (s32[]{:T(128)}, f32[2048,384]{1,0:T(8,128)}, f32[2048,384]{1,0:T(8,128)}, f32[384,2048]{1,0:T(8,128)}, s32[]{:T(128)}, /*index=5*/bf16[3072,2048]{1...) while((s32[]{:T(128)}, f32[2048,384]{1,0:T(8,128)}, ...), condition=%wide.region_14.15_spmd, body=%wide.region_13.14_spmd.sunk | while | flops 808747008 | bytes 24120504 | solution.py:135
  1139.0 4.5 convolution_add_fusion.7
  1143.5 4.5 convolution_add_fusion.9
  1158.6 4.5 convolution_add_fusion.9
  1169.2 4.5 convolution_add_fusion.7
  1173.7 4.5 convolution_add_fusion.9
  1184.4 4.5 convolution_add_fusion.7
  1188.9 4.5 convolution_add_fusion.9
  1199.5 4.5 convolution_add_fusion.7
  1204.0 4.5 convolution_add_fusion.9
  1214.6 4.5 convolution_add_fusion.7
  1219.1 4.5 convolution_add_fusion.9
  1229.7 4.5 convolution_add_fusion.7
  1234.3 4.5 convolution_add_fusion.9
  1244.9 4.5 convolution_add_fusion.7
  1249.4 4.5 convolution_add_fusion.9
  1260.0 4.5 convolution_add_fusion.7
  1264.5 4.5 convolution_add_fusion.9
  1275.1 4.5 convolution_add_fusion.7
  1279.6 4.5 convolution_add_fusion.9
  1290.3 4.5 convolution_add_fusion.7
  1294.8 4.5 convolution_add_fusion.9
  1305.4 4.5 convolution_add_fusion.7
  1309.9 4.5 convolution_add_fusion.9
  1325.0 4.5 convolution_add_fusion.9
  1335.6 4.5 convolution_add_fusion.7
  1340.2 4.5 convolution_add_fusion.9
  1350.8 4.5 convolution_add_fusion.7
  1355.3 4.5 convolution_add_fusion.9
  1365.9 4.5 convolution_add_fusion.7
  1370.4 4.5 convolution_add_fusion.9
  1381.0 4.5 convolution_add_fusion.7
  1385.5 4.5 convolution_add_fusion.9
  1400.7 4.5 convolution_add_fusion.9
  1411.3 4.5 convolution_add_fusion.7
  1415.8 4.5 convolution_add_fusion.9
  1430.9 4.5 convolution_add_fusion.9
  1441.5 4.5 convolution_add_fusion.7
  1446.0 4.5 convolution_add_fusion.9
  1461.2 4.5 convolution_add_fusion.9
  1476.3 4.5 convolution_add_fusion.9
  1491.4 4.5 convolution_add_fusion.9
  1500.1 5.1 multiply_bitcast_fusion.1
  (284 shorter events, 492.9 us)
Async XLA Ops:
  7.2 31.4 %copy-start = (bf16[128,2048]{1,0:T(8,128)(2,1)S(1)}, bf16[128,2048]{1,0:T(8,128)(2,1)}, u32[]{:S(2)}) copy-start(bf16[128,2048]{1,0:T(8,128)(2,1)} %param.14) | copy-start | bytes 1572868
  27.7 38.2 %all-to-all-start = ((s32[64,1,1]{2,1,0:T(1,128)}), s32[64,1,1]{2,1,0:T(1,128)S(1)}, u32[]{:S(2)}, u32[]{:S(2)}) async-start(s32[64,1,1]{2,1,0:T(1,128)} %copy.43), calls=%async_computation | async-start | bytes 65536 | tf_op jit(solution)/shard_map/all_to_all | solution.py:50
  65.9 178.2 %all-to-all-start.1 = ((bf16[64,48,2048]{2,1,0:T(8,128)(2,1)}), bf16[64,48,2048]{2,1,0:T(8,128)(2,1)}, u32[]{:S(2)}, u32[]{:S(2)}) async-start(bf16[64,48,2048]{2,1,0:T(8,128)(2,1)} %bitcast.63), calls=%async_computation.1 | async-start | bytes 25165824 | tf_op jit(solution)/shard_map/all_to_all | solution.py:49
  291.3 5.0 copy-start.2
  296.3 5.5 copy-start.6
  308.3 5.5 copy-start.6
  320.4 5.5 copy-start.6
  332.5 5.5 copy-start.6
  344.6 5.5 copy-start.6
  356.7 5.5 copy-start.6
  368.8 5.5 copy-start.6
  380.8 5.5 copy-start.6
  392.9 5.5 copy-start.6
  405.0 5.5 copy-start.6
  417.1 5.5 copy-start.6
  429.2 5.5 copy-start.6
  441.3 5.5 copy-start.6
  453.4 5.5 copy-start.6
  465.5 5.5 copy-start.6
  477.5 5.5 copy-start.6
  489.6 5.5 copy-start.6
  501.7 5.5 copy-start.6
  513.9 5.5 copy-start.6
  526.0 5.5 copy-start.6
  538.0 5.5 copy-start.6
  550.2 5.5 copy-start.6
  562.3 5.5 copy-start.6
  574.3 5.5 copy-start.6
  627.2 9.0 copy-start.4
  627.2 178.8 %all-to-all-start.2 = ((bf16[64,48,2048]{2,1,0:T(8,128)(2,1)}), bf16[64,48,2048]{2,1,0:T(8,128)(2,1)}, u32[]{:S(2)}, u32[]{:S(2)}) async-start(bf16[64,48,2048]{2,1,0:T(8,128)(2,1)} %broadcast_select_fusion.2), calls=%async_computation.2 | async-start | bytes 25165824 | tf_op jit(solution)/shard_map/all_to_all | solution.py:25
  635.9 225.0 %all-reduce.2.cloned.1.call-start = ((), (), s32[]{:S(2)}) async-start(), calls=%async_computation.4 | async-start | bytes 2097152 | tf_op jit(solution)/shard_map/psum | solution.py:103
  821.0 40.0 %copy-start.5 = (f32[128]{0:T(128)S(1)}, f32[128]{0:T(128)}, u32[]{:S(2)}) copy-start(f32[128]{0:T(128)} %param.17) | copy-start | bytes 1540
  884.1 202.0 %all-to-all-start.3 = ((bf16[64,48,2048]{2,1,0:T(8,128)(2,1)}), bf16[64,48,2048]{2,1,0:T(8,128)(2,1)}, u32[]{:S(2)}, u32[]{:S(2)}) async-start(bf16[64,48,2048]{2,1,0:T(8,128)(2,1)} %bitcast.64), calls=%async_computation.3 | async-start | bytes 25165824 | tf_op jit(solution)/shard_map/all_to_all | solution.py:25
  1496.0 4.1 copy-start.3
  1500.1 5.1 copy-start.1
Sparse Core Ops, SparseCore 0:
  828.6 32.3 all-reduce.1
where the time goes:
time: 1530 us; the launch traced here: 1510 us
  matrix products  653 us (43%)
  waiting for transfers between devices  555 us (36%)
  local copies, waits for them, and re-layouts  155 us (10%)
  other arithmetic  94.7 us (6%)
  starting transfers between devices  40 us (3%)
  between operations  15.4 us (1%)
    all_to_all x2, waiting for transfers between devices, move_rows(): lax.all_to_all(outgoing, ('dp', 'expert'), split_axis=0, concat_axis=0, t...  359 us
    dot_general x72, matrix products, contract_rows(): lax.dot_general(left, right, (((0,), (0,)), ((), ())), preferred_element_...  324 us
    dot_general x120, matrix products, product(): return jnp.dot(left, right, preferred_element_type=jnp.float32)  290 us
    all_to_all x1, waiting for transfers between devices, body(): lax.all_to_all(outgoing, ('dp', 'expert'), split_axis=0, concat_axis=0, t...  163 us
    dot_general x24, matrix products, backward(): lax.dot_general(rows_q, down_mat, (((1,), (1,)), ((), ())), preferred_ele...  39.3 us
    psum x1, waiting for transfers between devices, body(): tangent_full = lax.psum(tangent_part, 'tensor')  32.4 us
  transfers between devices with their start and end apart: 5, of which 4 were waited for; matrix products, arithmetic and copies ran while one was open for 2% of the time, Pallas kernels for 0%

commit v1 on v0

v1 whole, which is shorter than its diff:
```python
import jax
import jax.numpy as jnp
from jax import lax
from jax.experimental import pallas as pl
from jax.experimental.pallas import tpu as pltpu
from jax.sharding import PartitionSpec as P

BF = jnp.bfloat16
F32 = jnp.float32
GROUP = ("dp", "expert")
VMEM_LIMIT = 60 * 1024 * 1024
TILE = 256


def params():
    return pltpu.CompilerParams(
        dimension_semantics=("arbitrary",), vmem_limit_bytes=VMEM_LIMIT
    )


def cost(flops, nbytes):
    return pl.CostEstimate(flops=flops, bytes_accessed=nbytes, transcendentals=0)


def fixed(shape):
    return pl.BlockSpec(
        shape, lambda i: (0,) * len(shape), pipeline_mode=pl.Buffered(buffer_count=1)
    )


def smem():
    return pl.BlockSpec(memory_space=pltpu.SMEM)


def mm(left, right):
    return jnp.dot(left, right, preferred_element_type=F32)


def mm_t(left, right):
    return lax.dot_general(left, right, (((1,), (1,)), ((), ())), preferred_element_type=F32)


def mm_rows(left, right):
    return lax.dot_general(left, right, (((0,), (0,)), ((), ())), preferred_element_type=F32)


def spread(rows, per):
    count, toks = rows.shape
    return jnp.broadcast_to(rows[:, None, :], (count, per, toks)).reshape(count * per, toks)


def slot_match(pos, base, per):
    count, toks = pos.shape
    slot = lax.broadcasted_iota(jnp.int32, (count, per, toks), 1).reshape(count * per, toks)
    return spread(pos, per) == (slot + base).astype(F32)


def route_pack(base, ids_t, gates_t, tokens, experts, per):
    picks, toks = ids_t.shape
    width = tokens.shape[1]
    step = TILE // per
    steps = experts // step

    def kernel(base_ref, ids_ref, gates_ref, tok_ref, x_ref, pos_ref, gm_ref):
        i = pl.program_id(0)

        @pl.when(i == 0)
        def _():
            label = lax.broadcasted_iota(jnp.int32, (experts, toks), 0)
            hits = jnp.zeros((experts, toks), F32)
            gm = jnp.zeros((experts, toks), F32)
            for k in range(picks):
                match = ids_ref[k : k + 1, :] == label
                hits = jnp.where(match, 1.0, hits)
                gm = jnp.where(match, gates_ref[k : k + 1, :], gm)
            row = lax.broadcasted_iota(jnp.int32, (toks, toks), 0)
            col = lax.broadcasted_iota(jnp.int32, (toks, toks), 1)
            before = jnp.where(row < col, 1.0, 0.0).astype(BF)
            pos = mm(hits.astype(BF), before)
            pos_ref[...] = jnp.where(hits > 0.5, pos, -1.0)
            gm_ref[...] = gm

        pos = pos_ref[pl.ds(pl.multiple_of(i * step, step), step), :]
        hot = jnp.where(slot_match(pos, base_ref[0], per), 1.0, 0.0).astype(BF)
        x_ref[...] = mm(hot, tok_ref[...]).astype(BF)

    return pl.pallas_call(
        kernel,
        grid=(steps,),
        in_specs=[smem(), fixed((picks, toks)), fixed((picks, toks)), fixed((toks, width))],
        out_specs=[
            pl.BlockSpec((TILE, width), lambda i: (i, 0)),
            pl.BlockSpec((experts, toks), lambda i: (0, 0)),
            pl.BlockSpec((experts, toks), lambda i: (0, 0)),
        ],
        out_shape=[
            jax.ShapeDtypeStruct((experts * per, width), BF),
            jax.ShapeDtypeStruct((experts, toks), F32),
            jax.ShapeDtypeStruct((experts, toks), F32),
        ],
        compiler_params=params(),
        cost_estimate=cost(2 * experts * per * toks * width, 2 * experts * per * width),
        name="route_pack",
    )(base, ids_t, gates_t, tokens)


def pack(base, pos, tokens, per):
    experts, toks = pos.shape
    width = tokens.shape[1]
    step = TILE // per

    def kernel(base_ref, pos_ref, tok_ref, x_ref):
        hot = jnp.where(slot_match(pos_ref[...], base_ref[0], per), 1.0, 0.0).astype(BF)
        x_ref[...] = mm(hot, tok_ref[...]).astype(BF)

    return pl.pallas_call(
        kernel,
        grid=(experts // step,),
        in_specs=[smem(), pl.BlockSpec((step, toks), lambda i: (i, 0)), fixed((toks, width))],
        out_specs=pl.BlockSpec((TILE, width), lambda i: (i, 0)),
        out_shape=jax.ShapeDtypeStruct((experts * per, width), BF),
        compiler_params=params(),
        cost_estimate=cost(2 * experts * per * toks * width, 2 * experts * per * width),
        name="pack",
    )(base, pos, tokens)


def forward(rows, mats, hidden):
    count, width = rows.shape

    def kernel(x_ref, w_ref, ad_ref, silu_ref, us_ref):
        pre = mm(x_ref[...], w_ref[...])
        gate = pre[:, :hidden]
        up = pre[:, hidden : 2 * hidden]
        d_gate = pre[:, 2 * hidden : 3 * hidden]
        d_up = pre[:, 3 * hidden :]
        sigma = jax.nn.sigmoid(gate)
        silu = gate * sigma
        us = sigma * (1.0 + gate * (1.0 - sigma)) * up
        ad_ref[:, :hidden] = (silu * up).astype(BF)
        ad_ref[:, hidden:] = (us * d_gate + silu * d_up).astype(BF)
        silu_ref[...] = silu
        us_ref[...] = us

    return pl.pallas_call(
        kernel,
        grid=(count // TILE,),
        in_specs=[pl.BlockSpec((TILE, width), lambda i: (i, 0)), fixed((width, 4 * hidden))],
        out_specs=[
            pl.BlockSpec((TILE, 2 * hidden), lambda i: (i, 0)),
            pl.BlockSpec((TILE, hidden), lambda i: (i, 0)),
            pl.BlockSpec((TILE, hidden), lambda i: (i, 0)),
        ],
        out_shape=[
            jax.ShapeDtypeStruct((count, 2 * hidden), BF),
            jax.ShapeDtypeStruct((count, hidden), F32),
            jax.ShapeDtypeStruct((count, hidden), F32),
        ],
        compiler_params=params(),
        cost_estimate=cost(8 * count * width * hidden, 2 * count * width + 12 * count * hidden),
        name="forward",
    )(rows, mats)


def part_rows(ad_own, ad_other, down_own, down_other):
    count, inner = ad_own.shape
    width = down_own.shape[1]

    def kernel(a_ref, b_ref, wa_ref, wb_ref, out_ref):
        out_ref[...] = (mm(a_ref[...], wa_ref[...]) + mm(b_ref[...], wb_ref[...])).astype(BF)

    return pl.pallas_call(
        kernel,
        grid=(count // TILE,),
        in_specs=[
            pl.BlockSpec((TILE, inner), lambda i: (i, 0)),
            pl.BlockSpec((TILE, inner), lambda i: (i, 0)),
            fixed((inner, width)),
            fixed((inner, width)),
        ],
        out_specs=pl.BlockSpec((TILE, width), lambda i: (i, 0)),
        out_shape=jax.ShapeDtypeStruct((count, width), BF),
        compiler_params=params(),
        cost_estimate=cost(4 * count * width * inner, 2 * count * width + 4 * inner * width),
        name="part_rows",
    )(ad_own, ad_other, down_own, down_other)


def split_gates(pos, gm, base, per):
    weight = jnp.where(slot_match(pos, base, per), spread(gm, per), 0.0)
    high = weight.astype(BF)
    low = (weight - high.astype(F32)).astype(BF)
    return high, low


def combine(base, pos, gm, rows, start, per):
    experts, toks = pos.shape
    width = rows.shape[1]
    step = TILE // per
    steps = experts // step
    first = start is None

    def kernel(base_ref, pos_ref, gm_ref, rows_ref, *rest):
        start_ref = None if first else rest[0]
        out_ref, acc_ref = rest[-2:]
        i = pl.program_id(0)
        high, low = split_gates(pos_ref[...], gm_ref[...], base_ref[0], per)
        term = mm_rows(jnp.concatenate([high, low], axis=1), rows_ref[...])

        @pl.when(i == 0)
        def _():
            acc_ref[...] = term

        @pl.when(i > 0)
        def _():
            acc_ref[...] += term

        @pl.when(i == steps - 1)
        def _():
            total = acc_ref[:toks, :] + acc_ref[toks:, :]
            out_ref[...] = total if first else total + start_ref[...]

    extra = [] if first else [start]
    return pl.pallas_call(
        kernel,
        grid=(steps,),
        in_specs=[
            smem(),
            pl.BlockSpec((step, toks), lambda i: (i, 0)),
            pl.BlockSpec((step, toks), lambda i: (i, 0)),
            pl.BlockSpec((TILE, width), lambda i: (i, 0)),
        ]
        + [fixed((toks, width)) for _ in extra],
        out_specs=pl.BlockSpec((toks, width), lambda i: (0, 0)),
        out_shape=jax.ShapeDtypeStruct((toks, width), F32),
        scratch_shapes=[pltpu.VMEM((2 * toks, width), F32)],
        compiler_params=params(),
        cost_estimate=cost(4 * experts * per * toks * width, 2 * experts * per * width),
        name="combine",
    )(base, pos, gm, rows, *extra)


def weigh_pack(base, pos, gm, weight, own, other, per, half):
    experts, toks = pos.shape
    width = own.shape[1]
    step = TILE // per

    def kernel(base_ref, pos_ref, gm_ref, tw_ref, own_ref, other_ref, q_ref, *rest):
        high_ref, low_ref = rest[-2:]

        @pl.when(pl.program_id(0) == 0)
        def _():
            if half:
                cols = pl.ds(pl.multiple_of(base_ref[1] * half, half), half)
                rest[0][...] = (own_ref[:, cols] + other_ref[:, cols]).astype(BF)
            scaled = tw_ref[...] * (own_ref[...] + other_ref[...])
            high = scaled.astype(BF)
            high_ref[...] = high
            low_ref[...] = (scaled - high.astype(F32)).astype(BF)

        g_high, g_low = split_gates(pos_ref[...], gm_ref[...], base_ref[0], per)
        q_ref[...] = (
            mm(g_high, high_ref[...]) + mm(g_low, high_ref[...]) + mm(g_high, low_ref[...])
        ).astype(BF)

    out_specs = [pl.BlockSpec((TILE, width), lambda i: (i, 0))]
    out_shape = [jax.ShapeDtypeStruct((experts * per, width), BF)]
    if half:
        out_specs.append(pl.BlockSpec((toks, half), lambda i: (0, 0)))
        out_shape.append(jax.ShapeDtypeStruct((toks, half), BF))
    return pl.pallas_call(
        kernel,
        grid=(experts // step,),
        in_specs=[
            smem(),
            pl.BlockSpec((step, toks), lambda i: (i, 0)),
            pl.BlockSpec((step, toks), lambda i: (i, 0)),
            fixed((toks, 1)),
            fixed((toks, width)),
            fixed((toks, width)),
        ],
        out_specs=out_specs,
        out_shape=out_shape,
        scratch_shapes=[pltpu.VMEM((toks, width), BF), pltpu.VMEM((toks, width), BF)],
        compiler_params=params(),
        cost_estimate=cost(6 * experts * per * toks * width, 2 * experts * per * width),
        name="weigh_pack",
    )(base, pos, gm, weight, own, other)


def backward(own, other, down, sums, factor):
    count, width = own[0].shape
    hidden = down.shape[0]
    steps = count // TILE
    last = factor is not None
    piece = 256

    def kernel(*refs):
        own_refs, other_refs = refs[:5], refs[5:10]
        down_ref = refs[10]
        i = pl.program_id(0)
        if last:
            in_g, in_d = refs[11:13]
            gate_out, up_out, down_out, acc_g = refs[13:]
            acc_d = down_out.at[0]
        else:
            acc_g, acc_d = refs[11:]

        def terms(tile):
            q_ref, x_ref, ad_ref, silu_ref, us_ref = tile
            q = q_ref[...]
            back = mm_t(q, down_ref[...])
            grads = jnp.concatenate(
                [(back * us_ref[...]).astype(BF), (back * silu_ref[...]).astype(BF)], axis=1
            )
            return mm_rows(grads, x_ref[...]), mm_rows(ad_ref[:, :hidden], q)

        @pl.when(i == 0)
        def _():
            term_g, term_d = terms(own_refs)
            acc_g[...] = term_g + in_g[...] if last else term_g
            acc_d[...] = term_d + in_d[...] if last else term_d

        @pl.when((i > 0) & (i < steps))
        def _():
            term_g, term_d = terms(own_refs)
            acc_g[...] += term_g
            acc_d[...] += term_d

        @pl.when(i >= steps)
        def _():
            term_g, term_d = terms(other_refs)
            acc_g[...] += term_g
            acc_d[...] += term_d

        if last:

            @pl.when(i == 2 * steps - 1)
            def _():
                for start in range(0, width, piece):
                    cols = slice(start, start + piece)
                    gate_out[0, cols, :] = factor * acc_g[:hidden, cols].T
                    up_out[0, cols, :] = factor * acc_g[hidden:, cols].T
                acc_d[...] = factor * acc_d[...]

    def tiles(arrays, index):
        return [pl.BlockSpec((TILE, a.shape[1]), lambda i: (index(i), 0)) for a in arrays]

    in_specs = (
        tiles(own, lambda i: jnp.minimum(i, steps - 1))
        + tiles(other, lambda i: jnp.maximum(i - steps, 0))
        + [fixed((hidden, width))]
    )
    scratch = []
    if last:
        in_specs += [fixed((2 * hidden, width)), fixed((hidden, width))]
        shapes = [(1, width, hidden), (1, width, hidden), (1, hidden, width)]
        scratch = [pltpu.VMEM((2 * hidden, width), F32)]
    else:
        shapes = [(2 * hidden, width), (hidden, width)]
    return pl.pallas_call(
        kernel,
        grid=(2 * steps,),
        in_specs=in_specs,
        out_specs=[fixed(shape) for shape in shapes],
        out_shape=[jax.ShapeDtypeStruct(shape, F32) for shape in shapes],
        scratch_shapes=scratch,
        compiler_params=params(),
        cost_estimate=cost(16 * count * width * hidden, 8 * count * width),
        name="backward",
    )(*own, *other, down, *sums)


def exchange(rows):
    return lax.all_to_all(rows, GROUP, split_axis=0, concat_axis=0, tiled=True)


def body(tokens, expert_ids, gates, token_weight, w_gate, w_up, w_down, v_gate, v_up, v_down):
    toks, width = tokens.shape
    picks = expert_ids.shape[1]
    experts = lax.axis_size("dp") * lax.axis_size("expert")
    cores = lax.axis_size("tensor")
    hidden = w_gate.shape[2]
    per_core = min(3 * toks * picks // experts, toks) // cores
    per_a = 2 * per_core // 3
    per_b = per_core - per_a
    core = lax.axis_index("tensor")
    factor = 1.0 / (toks * picks) ** 0.5

    def swap(rows):
        return lax.ppermute(rows, "tensor", [(0, 1), (1, 0)])

    base_a = jnp.stack([core * per_core, core]).astype(jnp.int32)
    base_b = jnp.stack([core * per_core + per_a, core]).astype(jnp.int32)

    packed_a, pos, gm = route_pack(base_a, expert_ids.T, gates.T, tokens, experts, per_a)
    x_a = exchange(packed_a)
    packed_b = pack(base_b, pos, tokens, per_b)
    mats = jnp.concatenate([w_gate[0], w_up[0], v_gate[0], v_up[0]], axis=1)
    down_own = jnp.concatenate([v_down[0], w_down[0]], axis=0)
    down_other = swap(down_own)

    def run_forward(x_own):
        x_other = swap(x_own)
        mine = forward(x_own, mats, hidden)
        theirs = forward(x_other, mats, hidden)
        part = part_rows(mine[0], swap(theirs[0]), down_own, down_other)
        return part, (x_own, *mine), (x_other, *theirs)

    x_b = exchange(packed_b)
    part_a, mine_a, theirs_a = run_forward(x_a)
    ret_a = exchange(part_a)
    part_b, mine_b, theirs_b = run_forward(x_b)
    ret_b = exchange(part_b)
    own = combine(base_a, pos, gm, ret_a, None, per_a)
    own = combine(base_b, pos, gm, ret_b, own, per_b)
    other = swap(own)
    weight = token_weight[:, None]
    send_a, tangent = weigh_pack(base_a, pos, gm, weight, own, other, per_a, width // cores)
    q_a = exchange(send_a)
    (send_b,) = weigh_pack(base_b, pos, gm, weight, own, other, per_b, 0)
    q_b = exchange(send_b)
    down = w_down[0]
    sums = backward((q_a, *mine_a), (swap(q_a), *theirs_a), down, (), None)
    gv_gate, gv_up, gv_down = backward(
        (q_b, *mine_b), (swap(q_b), *theirs_b), down, sums, factor
    )
    return gv_gate, gv_up, gv_down, tangent


def solution(mesh):
    rows = P(GROUP, None)
    cols = P(GROUP, None, "tensor")
    down = P(GROUP, "tensor", None)
    in_specs = (rows, rows, rows, P(GROUP), cols, cols, down, cols, cols, down)
    out_specs = (cols, cols, down, P(GROUP, "tensor"))
    return jax.shard_map(body, mesh=mesh, in_specs=in_specs, out_specs=out_specs, check_vma=False)
```

time: 1530 us -> 400 us (0.26)
  the two profiles are of different devices: /device:TPU:114 before, /device:TPU:1 now
where the time goes in v1:
time: 400 us; the launch traced here: 399 us
  blocking collectives  157 us (39%)
  Pallas kernels  132 us (33%)
  waiting for transfers between devices  54 us (14%)
  starting transfers between devices  42.4 us (11%)
  other arithmetic  8.32 us (2%)
  local copies, waits for them, and re-layouts  4.88 us (1%)
    all_to_all x3, blocking collectives, exchange(): return lax.all_to_all(rows, GROUP, split_axis=0, concat_axis=0, tiled=True)  157 us
    all_to_all x3, waiting for transfers between devices, exchange(): return lax.all_to_all(rows, GROUP, split_axis=0, concat_axis=0, tiled=True)  48.3 us
    pallas_call x2, Pallas kernels, backward(): pl.pallas_call(kernel, grid=(2 * steps,), in_specs=in_specs, out_specs=[f...  46.8 us
    pallas_call x4, Pallas kernels, forward(): pl.pallas_call(kernel, grid=(count // TILE,), in_specs=[pl.BlockSpec((TIL...  37.4 us
    all_to_all x3, starting transfers between devices, exchange(): return lax.all_to_all(rows, GROUP, split_axis=0, concat_axis=0, tiled=True)  30.3 us
    pallas_call x2, Pallas kernels, part_rows(): pl.pallas_call(kernel, grid=(count // TILE,), in_specs=[pl.BlockSpec((TIL...  19 us
    ppermute x8, starting transfers between devices, swap(): return lax.ppermute(rows, 'tensor', [(0, 1), (1, 0)])  12.1 us
    pallas_call x2, Pallas kernels, weigh_pack(): pl.pallas_call(kernel, grid=(experts // step,), in_specs=[smem(), pl.Bloc...  11.9 us
  transfers between devices with their start and end apart: 11, of which 5 were waited for; matrix products, arithmetic and copies ran while one was open for 2% of the time, Pallas kernels for 24%

profile of v1, /device:TPU:1, one launch (start us, length us, event | category | flops | bytes accessed | tf_op | source)
XLA Modules:
  0.0 399.2 jit_solution(11254855464834459097)
XLA Ops:
  0.6 0.7 pad_add_fusion.1.base_ref
  1.3 4.5 %route_pack.1 = (bf16[1024,2048]{1,0:T(8,128)(2,1)}, f32[64,128]{1,0:T(8,128)}, f32[64,128]{1,0:T(8,128)}) custom-call(s32[2]{0:T(128)} %pad_add_fusion.1.base_ref, s32[8,128]{1,0:T(8,128)} %bitcast.45, f32[8,128]{1,0:T(8,128)} %bitcast.46, bf16[128,2048]{1,0:T(8,128)(2,1)} %tok_ref.3), custom_call_target="tpu_custom_call" | custom-call | flops 536870912 | bytes 4194304 | tf_op jit(solution)/shard_map/route_pack/pallas_call | solution.py:87
  5.8 0.0 copy-start.3
  5.8 0.0 copy-start.6
  5.8 62.2 %all_to_all.66 = bf16[64,16,2048]{2,1,0:T(8,128)(2,1)} all-to-all(bf16[64,16,2048]{2,1,0:T(8,128)(2,1)} %bitcast.36), channel_id=1, replica_groups=mesh['dp'=4,'expert'=16,'tensor'=2] {'dp','expert'}, dimensions={0} | all-to-all | bytes 8388608 | tf_op jit(solution)/shard_map/all_to_all | solution.py:375
  67.9 3.5 collective-permute-start.3
  71.5 0.0 copy-done.3
  71.5 0.0 copy-done.6
  71.5 0.0 copy-start.4
  71.5 0.0 copy-start.5
  71.5 2.1 pad_maximum_fusion.1.wa_ref
  73.6 0.0 collective-permute-start.2
  73.6 0.0 copy-done.4
  73.6 0.9 copy-done.5
  74.5 5.0 %pad_maximum_fusion.w_ref = bf16[2048,1536]{1,0:T(8,128)(2,1)} fusion(bf16[2048,384]{1,0:T(8,128)(2,1)S(1)} %bitcast.39, bf16[2048,384]{1,0:T(8,128)(2,1)S(1)} %bitcast.40, bf16[2048,384]{1,0:T(8,128)(2,1)} %bitcast.41, bf16[2048,384]{1,0:T(8,128)(2,1)} %bitcast.42), kind=kLoop, calls=%fused_computation | loop fusion | flops 25165824 | bytes 12582912 | tf_op jit(solution)/shard_map/concatenate | solution.py:399
  79.5 0.0 collective-permute-done.3.x_ref.refs_6_
  79.5 11.2 %forward.7 = (bf16[1024,768]{1,0:T(8,128)(2,1)}, f32[1024,384]{1,0:T(8,128)}, f32[1024,384]{1,0:T(8,128)}) custom-call(bf16[1024,2048]{1,0:T(8,128)(2,1)} %collective-permute-done.3.x_ref.refs_6_, bf16[2048,1536]{1,0:T(8,128)(2,1)} %pad_maximum_fusion.w_ref), custom_call_target="tpu_custom_call" | custom-call | flops 6442450944 | bytes 8912896 | tf_op jit(solution)/shard_map/forward/pallas_call | solution.py:145
  90.7 0.0 collective-permute-start.4
  90.7 0.6 pad_add_fusion.base_ref
  91.3 2.9 pack.1
  94.2 6.0 %all-to-all-start = ((bf16[64,8,2048]{2,1,0:T(8,128)(2,1)}), bf16[64,8,2048]{2,1,0:T(8,128)(2,1)S(1)}, u32[]{:S(2)}, u32[]{:S(2)}) async-start(bf16[64,8,2048]{2,1,0:T(8,128)(2,1)} %bitcast.29), calls=%async_computation | async-start | bytes 4194304 | tf_op jit(solution)/shard_map/all_to_all | solution.py:375
  100.2 11.2 %forward.6 = (bf16[1024,768]{1,0:T(8,128)(2,1)}, f32[1024,384]{1,0:T(8,128)}, f32[1024,384]{1,0:T(8,128)}) custom-call(bf16[1024,2048]{1,0:T(8,128)(2,1)} %bitcast.17.x_ref.refs_1_, bf16[2048,1536]{1,0:T(8,128)(2,1)} %pad_maximum_fusion.w_ref), custom_call_target="tpu_custom_call" | custom-call | flops 6442450944 | bytes 8912896 | tf_op jit(solution)/shard_map/forward/pallas_call | solution.py:145
  111.4 0.0 collective-permute-done.2.wb_ref
  111.4 0.0 collective-permute-done.4.b_ref
  111.5 11.3 %part_rows.3 = bf16[1024,2048]{1,0:T(8,128)(2,1)} custom-call(bf16[1024,768]{1,0:T(8,128)(2,1)} %get-tuple-element.31.a_ref.refs_2_, bf16[1024,768]{1,0:T(8,128)(2,1)} %collective-permute-done.4.b_ref, bf16[768,2048]{1,0:T(8,128)(2,1)} %pad_maximum_fusion.1.wa_ref, bf16[768,2048]{1,0:T(8,128)(2,1)} %collective-permute-done.2.wb_ref), custom_call_target="tpu_custom_call" | custom-call | flops 6442450944 | bytes 10485760 | tf_op jit(solution)/shard_map/part_rows/pallas_call | solution.py:172
  122.8 4.9 %all-to-all-done = bf16[64,8,2048]{2,1,0:T(8,128)(2,1)S(1)} async-done(((bf16[64,8,2048]{2,1,0:T(8,128)(2,1)}), bf16[64,8,2048]{2,1,0:T(8,128)(2,1)S(1)}, u32[]{:S(2)}, u32[]{:S(2)}) %all-to-all-start) | async-done | bytes 2097184 | tf_op jit(solution)/shard_map/all_to_all | solution.py:375
  127.7 0.0 copy-start
  127.7 7.6 %all-to-all-start.3 = ((bf16[64,16,2048]{2,1,0:T(8,128)(2,1)}), bf16[64,16,2048]{2,1,0:T(8,128)(2,1)}, u32[]{:S(2)}, u32[]{:S(2)}) async-start(bf16[64,16,2048]{2,1,0:T(8,128)(2,1)} %bitcast.35), calls=%async_computation.3 | async-start | bytes 8388608 | tf_op jit(solution)/shard_map/all_to_all | solution.py:375
  135.3 0.0 copy-done
  135.4 1.5 collective-permute-start
  136.9 3.9 collective-permute-done.x_ref.refs_6_
  140.8 7.5 %forward.5 = (bf16[512,768]{1,0:T(8,128)(2,1)}, f32[512,384]{1,0:T(8,128)}, f32[512,384]{1,0:T(8,128)}) custom-call(bf16[512,2048]{1,0:T(8,128)(2,1)} %collective-permute-done.x_ref.refs_6_, bf16[2048,1536]{1,0:T(8,128)(2,1)} %pad_maximum_fusion.w_ref), custom_call_target="tpu_custom_call" | custom-call | flops 3221225472 | bytes 4456448 | tf_op jit(solution)/shard_map/forward/pallas_call | solution.py:145
  148.3 0.4 collective-permute-start.1
  148.7 7.5 %forward.4 = (bf16[512,768]{1,0:T(8,128)(2,1)}, f32[512,384]{1,0:T(8,128)}, f32[512,384]{1,0:T(8,128)}) custom-call(bf16[512,2048]{1,0:T(8,128)(2,1)} %bitcast.25, bf16[2048,1536]{1,0:T(8,128)(2,1)} %pad_maximum_fusion.w_ref), custom_call_target="tpu_custom_call" | custom-call | flops 3221225472 | bytes 4456448 | tf_op jit(solution)/shard_map/forward/pallas_call | solution.py:145
  156.2 0.0 collective-permute-done.1.b_ref
  156.2 0.0 copy-start.9
  156.2 0.9 copy-done.9
  157.1 7.7 %part_rows.2 = bf16[512,2048]{1,0:T(8,128)(2,1)} custom-call(bf16[512,768]{1,0:T(8,128)(2,1)} %get-tuple-element.28.a_ref.refs_2_, bf16[512,768]{1,0:T(8,128)(2,1)} %copy-done.9, bf16[768,2048]{1,0:T(8,128)(2,1)} %pad_maximum_fusion.1.wa_ref, bf16[768,2048]{1,0:T(8,128)(2,1)} %collective-permute-done.2.wb_ref), custom_call_target="tpu_custom_call" | custom-call | flops 3221225472 | bytes 8388608 | tf_op jit(solution)/shard_map/part_rows/pallas_call | solution.py:172
  164.8 21.8 %all-to-all-done.3 = bf16[64,16,2048]{2,1,0:T(8,128)(2,1)} async-done(((bf16[64,16,2048]{2,1,0:T(8,128)(2,1)}), bf16[64,16,2048]{2,1,0:T(8,128)(2,1)}, u32[]{:S(2)}, u32[]{:S(2)}) %all-to-all-start.3) | async-done | bytes 4194336 | tf_op jit(solution)/shard_map/all_to_all | solution.py:375
  186.5 16.7 %all-to-all-start.1 = ((bf16[64,8,2048]{2,1,0:T(8,128)(2,1)}), bf16[64,8,2048]{2,1,0:T(8,128)(2,1)S(1)}, u32[]{:S(2)}, u32[]{:S(2)}) async-start(bf16[64,8,2048]{2,1,0:T(8,128)(2,1)} %bitcast.38), calls=%async_computation.1 | async-start | bytes 4194304 | tf_op jit(solution)/shard_map/all_to_all | solution.py:375
  203.2 5.6 %combine.2.rest_0_ = f32[128,2048]{1,0:T(8,128)} custom-call(s32[2]{0:T(128)} %pad_add_fusion.1.base_ref, f32[64,128]{1,0:T(8,128)} %get-tuple-element.26.pos_ref, f32[64,128]{1,0:T(8,128)} %get-tuple-element.27.gm_ref, bf16[1024,2048]{1,0:T(8,128)(2,1)} %bitcast.19.rows_ref), custom_call_target="tpu_custom_call" | custom-call | flops 1073741824 | bytes 4194304 | tf_op jit(solution)/shard_map/combine/pallas_call | solution.py:224
  208.8 0.0 copy-start.8
  208.8 21.7 %all-to-all-done.1 = bf16[64,8,2048]{2,1,0:T(8,128)(2,1)S(1)} async-done(((bf16[64,8,2048]{2,1,0:T(8,128)(2,1)}), bf16[64,8,2048]{2,1,0:T(8,128)(2,1)S(1)}, u32[]{:S(2)}, u32[]{:S(2)}) %all-to-all-start.1) | async-done | bytes 2097184 | tf_op jit(solution)/shard_map/all_to_all | solution.py:375
  230.5 0.0 copy-start.2
  230.5 1.3 copy-done.2
  231.8 4.0 %combine.3.own_ref = f32[128,2048]{1,0:T(8,128)} custom-call(s32[2]{0:T(128)} %pad_add_fusion.base_ref, f32[64,128]{1,0:T(8,128)} %get-tuple-element.26.pos_ref, f32[64,128]{1,0:T(8,128)} %get-tuple-element.27.gm_ref, bf16[512,2048]{1,0:T(8,128)(2,1)} %bitcast.30, f32[128,2048]{1,0:T(8,128)} %combine.2.rest_0_), custom_call_target="tpu_custom_call" | custom-call | flops 536870912 | bytes 2097152 | tf_op jit(solution)/shard_map/combine/pallas_call | solution.py:224
  235.9 3.2 collective-permute-start.5
  239.1 0.0 copy-done.8
  239.1 0.7 copy.14.tw_ref
  239.8 1.8 collective-permute-done.5.other_ref
  241.6 0.0 copy-start.7
  241.6 1.0 copy-done.7
  242.6 7.0 %weigh_pack.3 = (bf16[1024,2048]{1,0:T(8,128)(2,1)}, bf16[128,1024]{1,0:T(8,128)(2,1)}) custom-call(s32[2]{0:T(128)} %pad_add_fusion.1.base_ref, f32[64,128]{1,0:T(8,128)} %get-tuple-element.26.pos_ref, f32[64,128]{1,0:T(8,128)} %get-tuple-element.27.gm_ref, f32[128,1]{1,0:T(8,128)} %copy.14.tw_ref, f32[128,2048]{1,0:T(8,128)} %combine.3.own_ref, ...), custom_call_target="tpu_custom_call" | custom-call | flops 1610612736 | bytes 4194304 | tf_op jit(solution)/shard_map/weigh_pack/pallas_call | solution.py:271
  249.6 56.7 %all_to_all.67 = bf16[64,16,2048]{2,1,0:T(8,128)(2,1)} all-to-all(bf16[64,16,2048]{2,1,0:T(8,128)(2,1)} %bitcast.37), channel_id=1, replica_groups=mesh['dp'=4,'expert'=16,'tensor'=2] {'dp','expert'}, dimensions={0} | all-to-all | bytes 8388608 | tf_op jit(solution)/shard_map/all_to_all | solution.py:375
  306.3 1.8 collective-permute-start.7
  308.1 5.0 %weigh_pack.2 = bf16[512,2048]{1,0:T(8,128)(2,1)} custom-call(s32[2]{0:T(128)} %pad_add_fusion.base_ref, f32[64,128]{1,0:T(8,128)} %get-tuple-element.26.pos_ref, f32[64,128]{1,0:T(8,128)} %get-tuple-element.27.gm_ref, f32[128,1]{1,0:T(8,128)} %copy.14.tw_ref, f32[128,2048]{1,0:T(8,128)} %combine.3.own_ref, f32[128,2048]{1,0:T(8,128)} %copy-done.7), custom_call_target="tpu_custom_call" | custom-call | flops 805306368 | bytes 2097152 | tf_op jit(solution)/shard_map/weigh_pack/pallas_call | solution.py:271
  313.1 37.7 %all_to_all.68 = bf16[64,8,2048]{2,1,0:T(8,128)(2,1)S(1)} all-to-all(bf16[64,8,2048]{2,1,0:T(8,128)(2,1)} %bitcast.31), channel_id=1, replica_groups=mesh['dp'=4,'expert'=16,'tensor'=2] {'dp','expert'}, dimensions={0} | all-to-all | bytes 4194304 | tf_op jit(solution)/shard_map/all_to_all | solution.py:375
  350.7 0.0 copy-start.1
  350.7 1.6 collective-permute-start.6
  352.3 0.0 collective-permute-done.7.refs_5_
  352.3 25.5 %backward.2 = (f32[768,2048]{1,0:T(8,128)}, f32[384,2048]{1,0:T(8,128)}) custom-call(bf16[1024,2048]{1,0:T(8,128)(2,1)} %bitcast.23.refs_0_, bf16[1024,2048]{1,0:T(8,128)(2,1)} %bitcast.17.x_ref.refs_1_, bf16[1024,768]{1,0:T(8,128)(2,1)} %get-tuple-element.31.a_ref.refs_2_, f32[1024,384]{1,0:T(8,128)} %get-tuple-element.38.refs_3_, ...), custom_call_target="tpu_custom_call" | custom-call | flops 12884901888 | bytes 16777216 | tf_op jit(solution)/shard_map/backward/pallas_call | solution.py:361
  377.8 0.0 copy-done.1
  377.8 0.0 collective-permute-done.6.refs_5_
  377.8 21.3 %backward.3 = (f32[1,2048,384]{2,1,0:T(8,128)}, f32[1,2048,384]{2,1,0:T(8,128)}, f32[1,384,2048]{2,1,0:T(8,128)}) custom-call(bf16[512,2048]{1,0:T(8,128)(2,1)} %bitcast.28, bf16[512,2048]{1,0:T(8,128)(2,1)} %bitcast.26, bf16[512,768]{1,0:T(8,128)(2,1)} %get-tuple-element.28.a_ref.refs_2_, f32[512,384]{1,0:T(8,128)} %get-tuple-element.33.refs_3_, ...), custom_call_target="tpu_custom_call" | custom-call | flops 6442450944 | bytes 8388608 | tf_op jit(solution)/shard_map/backward/pallas_call | solution.py:361
Async XLA Ops:
  5.8 65.7 %copy-start.3 = (bf16[1,384,2048]{2,1,0:T(8,128)(2,1)S(1)}, bf16[1,384,2048]{2,1,0:T(8,128)(2,1)}, u32[]{:S(2)}) copy-start(bf16[1,384,2048]{2,1,0:T(8,128)(2,1)} %param.16) | copy-start | bytes 4718596
  5.8 65.7 %copy-start.6 = (bf16[1,384,2048]{2,1,0:T(8,128)(2,1)S(1)}, bf16[1,384,2048]{2,1,0:T(8,128)(2,1)}, u32[]{:S(2)}) copy-start(bf16[1,384,2048]{2,1,0:T(8,128)(2,1)} %param.19) | copy-start | bytes 4718596
  67.9 11.5 %collective-permute-start.3 = (bf16[1024,2048]{1,0:T(8,128)(2,1)}, bf16[1024,2048]{1,0:T(8,128)(2,1)}, u32[]{:S(2)}, u32[]{:S(2)}) collective-permute-start(bf16[1024,2048]{1,0:T(8,128)(2,1)} %bitcast.17.x_ref.refs_1_), channel_id=1, source_target_pairs={{0,1},{1,0},{2,3},{3,2},{4,5},{5,4},{6,7},{7,6},{8,9},{9,8},{10,11... | collective-permute-start | bytes 12582920 | tf_op jit(solution)/shard_map/ppermute | solution.py:391
  71.5 2.1 copy-start.4
  71.5 3.0 copy-start.5
  73.6 37.9 %collective-permute-start.2 = (bf16[768,2048]{1,0:T(8,128)(2,1)}, bf16[768,2048]{1,0:T(8,128)(2,1)}, u32[]{:S(2)}, u32[]{:S(2)}) collective-permute-start(bf16[768,2048]{1,0:T(8,128)(2,1)} %pad_maximum_fusion.1.wa_ref), channel_id=1, source_target_pairs={{0,1},{1,0},{2,3},{3,2},{4,5},{5,4},{6,7},{7,6},{8,9},{9,8},{10,11... | collective-permute-start | bytes 9437192 | tf_op jit(solution)/shard_map/ppermute | solution.py:391
  90.7 20.8 %collective-permute-start.4 = (bf16[1024,768]{1,0:T(8,128)(2,1)}, bf16[1024,768]{1,0:T(8,128)(2,1)}, u32[]{:S(2)}, u32[]{:S(2)}) collective-permute-start(bf16[1024,768]{1,0:T(8,128)(2,1)} %get-tuple-element.32.refs_7_), channel_id=1, source_target_pairs={{0,1},{1,0},{2,3},{3,2},{4,5},{5,4},{6,7},{7,6},{8,9},{9,8},{10,11... | collective-permute-start | bytes 4718600 | tf_op jit(solution)/shard_map/ppermute | solution.py:391
  94.2 33.5 %all-to-all-start = ((bf16[64,8,2048]{2,1,0:T(8,128)(2,1)}), bf16[64,8,2048]{2,1,0:T(8,128)(2,1)S(1)}, u32[]{:S(2)}, u32[]{:S(2)}) async-start(bf16[64,8,2048]{2,1,0:T(8,128)(2,1)} %bitcast.29), calls=%async_computation | async-start | bytes 4194304 | tf_op jit(solution)/shard_map/all_to_all | solution.py:375
  127.7 7.7 %copy-start = (bf16[64,8,2048]{2,1,0:T(8,128)(2,1)}, bf16[64,8,2048]{2,1,0:T(8,128)(2,1)S(1)}, u32[]{:S(2)}) copy-start(bf16[64,8,2048]{2,1,0:T(8,128)(2,1)S(1)} %all-to-all-done) | copy-start | bytes 6291460
  127.7 58.8 %all-to-all-start.3 = ((bf16[64,16,2048]{2,1,0:T(8,128)(2,1)}), bf16[64,16,2048]{2,1,0:T(8,128)(2,1)}, u32[]{:S(2)}, u32[]{:S(2)}) async-start(bf16[64,16,2048]{2,1,0:T(8,128)(2,1)} %bitcast.35), calls=%async_computation.3 | async-start | bytes 8388608 | tf_op jit(solution)/shard_map/all_to_all | solution.py:375
  135.4 5.4 %collective-permute-start = (bf16[512,2048]{1,0:T(8,128)(2,1)S(1)}, bf16[512,2048]{1,0:T(8,128)(2,1)}, u32[]{:S(2)}, u32[]{:S(2)}) collective-permute-start(bf16[512,2048]{1,0:T(8,128)(2,1)S(1)} %bitcast.24), channel_id=1, source_target_pairs={{0,1},{1,0},{2,3},{3,2},{4,5},{5,4},{6,7},{7,6},{8,9},{9,8},{10,11... | collective-permute-start | bytes 6291464 | tf_op jit(solution)/shard_map/ppermute | solution.py:391
  148.3 7.9 %collective-permute-start.1 = (bf16[512,768]{1,0:T(8,128)(2,1)}, bf16[512,768]{1,0:T(8,128)(2,1)S(1)}, u32[]{:S(2)}, u32[]{:S(2)}) collective-permute-start(bf16[512,768]{1,0:T(8,128)(2,1)} %get-tuple-element.29.refs_7_), channel_id=1, source_target_pairs={{0,1},{1,0},{2,3},{3,2},{4,5},{5,4},{6,7},{7,6},{8,9},{9,8},{10,11... | collective-permute-start | bytes 2359304 | tf_op jit(solution)/shard_map/ppermute | solution.py:391
  156.2 0.9 copy-start.9
  186.5 44.0 %all-to-all-start.1 = ((bf16[64,8,2048]{2,1,0:T(8,128)(2,1)}), bf16[64,8,2048]{2,1,0:T(8,128)(2,1)S(1)}, u32[]{:S(2)}, u32[]{:S(2)}) async-start(bf16[64,8,2048]{2,1,0:T(8,128)(2,1)} %bitcast.38), calls=%async_computation.1 | async-start | bytes 4194304 | tf_op jit(solution)/shard_map/all_to_all | solution.py:375
  208.8 30.2 %copy-start.8 = (f32[128]{0:T(128)S(1)}, f32[128]{0:T(128)}, u32[]{:S(2)}) copy-start(f32[128]{0:T(128)} %param.13) | copy-start | bytes 1540
  230.5 1.3 copy-start.2
  235.9 5.7 %collective-permute-start.5 = (f32[128,2048]{1,0:T(8,128)}, f32[128,2048]{1,0:T(8,128)S(1)}, u32[]{:S(2)}, u32[]{:S(2)}) collective-permute-start(f32[128,2048]{1,0:T(8,128)} %combine.3.own_ref), channel_id=1, source_target_pairs={{0,1},{1,0},{2,3},{3,2},{4,5},{5,4},{6,7},{7,6},{8,9},{9,8},{10,11... | collective-permute-start | bytes 3145736 | tf_op jit(solution)/shard_map/ppermute | solution.py:391
  241.6 1.0 copy-start.7
  306.3 46.0 %collective-permute-start.7 = (bf16[1024,2048]{1,0:T(8,128)(2,1)}, bf16[1024,2048]{1,0:T(8,128)(2,1)}, u32[]{:S(2)}, u32[]{:S(2)}) collective-permute-start(bf16[1024,2048]{1,0:T(8,128)(2,1)} %bitcast.23.refs_0_), channel_id=1, source_target_pairs={{0,1},{1,0},{2,3},{3,2},{4,5},{5,4},{6,7},{7,6},{8,9},{9,8},{10,11... | collective-permute-start | bytes 12582920 | tf_op jit(solution)/shard_map/ppermute | solution.py:391
  350.7 27.1 %copy-start.1 = (bf16[64,8,2048]{2,1,0:T(8,128)(2,1)}, bf16[64,8,2048]{2,1,0:T(8,128)(2,1)S(1)}, u32[]{:S(2)}) copy-start(bf16[64,8,2048]{2,1,0:T(8,128)(2,1)S(1)} %all_to_all.68) | copy-start | bytes 6291460
  350.7 27.1 %collective-permute-start.6 = (bf16[512,2048]{1,0:T(8,128)(2,1)S(1)}, bf16[512,2048]{1,0:T(8,128)(2,1)}, u32[]{:S(2)}, u32[]{:S(2)}) collective-permute-start(bf16[512,2048]{1,0:T(8,128)(2,1)S(1)} %bitcast.27), channel_id=1, source_target_pairs={{0,1},{1,0},{2,3},{3,2},{4,5},{5,4},{6,7},{7,6},{8,9},{9,8},{10,11... | collective-permute-start | bytes 6291464 | tf_op jit(solution)/shard_map/ppermute | solution.py:391

commit v2 on v1

--- a/solution.py
+++ b/solution.py
@@ -10,6 +10,7 @@
 GROUP = ("dp", "expert")
 VMEM_LIMIT = 60 * 1024 * 1024
 TILE = 256
+PIECE = 256
 
 
 def params():
@@ -19,7 +20,7 @@
 
 
 def cost(flops, nbytes):
-    return pl.CostEstimate(flops=flops, bytes_accessed=nbytes, transcendentals=0)
+    return pl.CostEstimate(flops=flops // 16, bytes_accessed=nbytes // 16, transcendentals=0)
 
 
 def fixed(shape):
@@ -246,7 +247,7 @@
     step = TILE // per
 
     def kernel(base_ref, pos_ref, gm_ref, tw_ref, own_ref, other_ref, q_ref, *rest):
-        high_ref, low_ref = rest[-2:]
+        split_ref = rest[-1]
 
         @pl.when(pl.program_id(0) == 0)
         def _():
@@ -255,13 +256,14 @@
                 rest[0][...] = (own_ref[:, cols] + other_ref[:, cols]).astype(BF)
             scaled = tw_ref[...] * (own_ref[...] + other_ref[...])
             high = scaled.astype(BF)
-            high_ref[...] = high
-            low_ref[...] = (scaled - high.astype(F32)).astype(BF)
-
-        g_high, g_low = split_gates(pos_ref[...], gm_ref[...], base_ref[0], per)
-        q_ref[...] = (
-            mm(g_high, high_ref[...]) + mm(g_low, high_ref[...]) + mm(g_high, low_ref[...])
-        ).astype(BF)
+            split_ref[:toks, :] = high
+            split_ref[toks:, :] = (scaled - high.astype(F32)).astype(BF)
+
+        match = slot_match(pos_ref[...], base_ref[0], per)
+        hot = jnp.where(match, 1.0, 0.0).astype(BF)
+        gate = jnp.sum(jnp.where(match, spread(gm_ref[...], per), 0.0), axis=1, keepdims=True)
+        row = mm(jnp.concatenate([hot, hot], axis=1), split_ref[...])
+        q_ref[...] = (gate * row).astype(BF)
 
     out_specs = [pl.BlockSpec((TILE, width), lambda i: (i, 0))]
     out_shape = [jax.ShapeDtypeStruct((experts * per, width), BF)]
@@ -281,94 +283,82 @@
         ],
         out_specs=out_specs,
         out_shape=out_shape,
-        scratch_shapes=[pltpu.VMEM((toks, width), BF), pltpu.VMEM((toks, width), BF)],
+        scratch_shapes=[pltpu.VMEM((2 * toks, width), BF)],
         compiler_params=params(),
         cost_estimate=cost(6 * experts * per * toks * width, 2 * experts * per * width),
         name="weigh_pack",
     )(base, pos, gm, weight, own, other)
 
 
-def backward(own, other, down, sums, factor):
+def gradients(q, silu, us, down):
+    count, width = q.shape
+    hidden = down.shape[0]
+    tile = min(TILE, count)
+
+    def kernel(q_ref, silu_ref, us_ref, down_ref, g_ref):
+        back = mm_t(q_ref[...], down_ref[...])
+        g_ref[:, :hidden] = (back * us_ref[...]).astype(BF)
+        g_ref[:, hidden:] = (back * silu_ref[...]).astype(BF)
+
+    return pl.pallas_call(
+        kernel,
+        grid=(count // tile,),
+        in_specs=[
+            pl.BlockSpec((tile, width), lambda i: (i, 0)),
+            pl.BlockSpec((tile, hidden), lambda i: (i, 0)),
+            pl.BlockSpec((tile, hidden), lambda i: (i, 0)),
+            fixed((hidden, width)),
+        ],
+        out_specs=pl.BlockSpec((tile, 2 * hidden), lambda i: (i, 0)),
+        out_shape=jax.ShapeDtypeStruct((count, 2 * hidden), BF),
+        compiler_params=params(),
+        cost_estimate=cost(2 * count * width * hidden, 2 * count * width),
+        name="gradients",
+    )(q, silu, us, down)
+
+
+def outer_sums(own, other, start, factor, hidden):
     count, width = own[0].shape
-    hidden = down.shape[0]
-    steps = count // TILE
-    last = factor is not None
-    piece = 256
+    piece = PIECE
 
     def kernel(*refs):
-        own_refs, other_refs = refs[:5], refs[5:10]
-        down_ref = refs[10]
-        i = pl.program_id(0)
-        if last:
-            in_g, in_d = refs[11:13]
-            gate_out, up_out, down_out, acc_g = refs[13:]
-            acc_d = down_out.at[0]
-        else:
-            acc_g, acc_d = refs[11:]
-
-        def terms(tile):
-            q_ref, x_ref, ad_ref, silu_ref, us_ref = tile
-            q = q_ref[...]
-            back = mm_t(q, down_ref[...])
-            grads = jnp.concatenate(
-                [(back * us_ref[...]).astype(BF), (back * silu_ref[...]).astype(BF)], axis=1
-            )
-            return mm_rows(grads, x_ref[...]), mm_rows(ad_ref[:, :hidden], q)
-
-        @pl.when(i == 0)
-        def _():
-            term_g, term_d = terms(own_refs)
-            acc_g[...] = term_g + in_g[...] if last else term_g
-            acc_d[...] = term_d + in_d[...] if last else term_d
-
-        @pl.when((i > 0) & (i < steps))
-        def _():
-            term_g, term_d = terms(own_refs)
-            acc_g[...] += term_g
-            acc_d[...] += term_d
-
-        @pl.when(i >= steps)
-        def _():
-            term_g, term_d = terms(other_refs)
-            acc_g[...] += term_g
-            acc_d[...] += term_d
-
-        if last:
-
-            @pl.when(i == 2 * steps - 1)
-            def _():
-                for start in range(0, width, piece):
-                    cols = slice(start, start + piece)
-                    gate_out[0, cols, :] = factor * acc_g[:hidden, cols].T
-                    up_out[0, cols, :] = factor * acc_g[hidden:, cols].T
-                acc_d[...] = factor * acc_d[...]
-
-    def tiles(arrays, index):
-        return [pl.BlockSpec((TILE, a.shape[1]), lambda i: (index(i), 0)) for a in arrays]
-
-    in_specs = (
-        tiles(own, lambda i: jnp.minimum(i, steps - 1))
-        + tiles(other, lambda i: jnp.maximum(i - steps, 0))
-        + [fixed((hidden, width))]
-    )
-    scratch = []
-    if last:
-        in_specs += [fixed((2 * hidden, width)), fixed((hidden, width))]
-        shapes = [(1, width, hidden), (1, width, hidden), (1, hidden, width)]
-        scratch = [pltpu.VMEM((2 * hidden, width), F32)]
-    else:
-        shapes = [(2 * hidden, width), (hidden, width)]
-    return pl.pallas_call(
-        kernel,
-        grid=(2 * steps,),
-        in_specs=in_specs,
-        out_specs=[fixed(shape) for shape in shapes],
+        gate_out, up_out, down_out = refs[-3:]
+        gate_up, down = 0.0, 0.0
+        for q_ref, x_ref, g_ref, act_ref in (refs[:4], refs[4:8]):
+            gate_up += mm_rows(x_ref[...], g_ref[...])
+            down += mm_rows(act_ref[...], q_ref[...])
+        terms = [gate_up[:, :hidden], gate_up[:, hidden:], down]
+        for out, term, begin in zip((gate_out, up_out, down_out), terms, refs[8:11] if start else [None] * 3):
+            out[0] = factor * term + begin[0] if start else factor * term
+
+    def specs():
+        return [
+            pl.BlockSpec((count, piece), lambda i: (0, i)),
+            pl.BlockSpec((count, piece), lambda i: (0, i)),
+            fixed((count, 2 * hidden)),
+            pl.BlockSpec(
+                (count, hidden), lambda i: (0, 0), pipeline_mode=pl.Buffered(buffer_count=1)
+            ),
+        ]
+
+    def results():
+        return [
+            pl.BlockSpec((1, piece, hidden), lambda i: (0, i, 0)),
+            pl.BlockSpec((1, piece, hidden), lambda i: (0, i, 0)),
+            pl.BlockSpec((1, hidden, piece), lambda i: (0, 0, i)),
+        ]
+
+    shapes = [(1, width, hidden), (1, width, hidden), (1, hidden, width)]
+    return pl.pallas_call(
+        kernel,
+        grid=(width // piece,),
+        in_specs=specs() + specs() + (results() if start else []),
+        out_specs=results(),
         out_shape=[jax.ShapeDtypeStruct(shape, F32) for shape in shapes],
-        scratch_shapes=scratch,
-        compiler_params=params(),
-        cost_estimate=cost(16 * count * width * hidden, 8 * count * width),
-        name="backward",
-    )(*own, *other, down, *sums)
+        compiler_params=params(),
+        cost_estimate=cost(12 * count * width * hidden, 8 * count * width),
+        name="outer_sums",
+    )(*own, *other, *start)
 
 
 def exchange(rows):
@@ -398,6 +388,8 @@
     packed_b = pack(base_b, pos, tokens, per_b)
     mats = jnp.concatenate([w_gate[0], w_up[0], v_gate[0], v_up[0]], axis=1)
     down_own = jnp.concatenate([v_down[0], w_down[0]], axis=0)
+    x_a, packed_b, mats, down_own = lax.optimization_barrier((x_a, packed_b, mats, down_own))
+    x_b = exchange(packed_b)
     down_other = swap(down_own)
 
     def run_forward(x_own):
@@ -407,24 +399,34 @@
         part = part_rows(mine[0], swap(theirs[0]), down_own, down_other)
         return part, (x_own, *mine), (x_other, *theirs)
 
-    x_b = exchange(packed_b)
     part_a, mine_a, theirs_a = run_forward(x_a)
+    x_b, part_a = lax.optimization_barrier((x_b, part_a))
     ret_a = exchange(part_a)
     part_b, mine_b, theirs_b = run_forward(x_b)
+    ret_a, part_b = lax.optimization_barrier((ret_a, part_b))
     ret_b = exchange(part_b)
     own = combine(base_a, pos, gm, ret_a, None, per_a)
+    ret_b, own = lax.optimization_barrier((ret_b, own))
     own = combine(base_b, pos, gm, ret_b, own, per_b)
     other = swap(own)
     weight = token_weight[:, None]
     send_a, tangent = weigh_pack(base_a, pos, gm, weight, own, other, per_a, width // cores)
     q_a = exchange(send_a)
     (send_b,) = weigh_pack(base_b, pos, gm, weight, own, other, per_b, 0)
+    q_a, send_b = lax.optimization_barrier((q_a, send_b))
     q_b = exchange(send_b)
     down = w_down[0]
-    sums = backward((q_a, *mine_a), (swap(q_a), *theirs_a), down, (), None)
-    gv_gate, gv_up, gv_down = backward(
-        (q_b, *mine_b), (swap(q_b), *theirs_b), down, sums, factor
-    )
+
+    def run_backward(q_own, mine, theirs, start):
+        q_other = swap(q_own)
+        sides = []
+        for q, (x, ad, silu, us) in ((q_own, mine), (q_other, theirs)):
+            sides.append((q, x, gradients(q, silu, us, down), ad))
+        return outer_sums(*sides, start, factor, hidden)
+
+    sums = run_backward(q_a, mine_a, theirs_a, ())
+    q_b, sums = lax.optimization_barrier((q_b, sums))
+    gv_gate, gv_up, gv_down = run_backward(q_b, mine_b, theirs_b, sums)
     return gv_gate, gv_up, gv_down, tangent
 
 

time: 400 us -> 371 us (0.927)
  blocking collectives: 157 us -> 0 us
  waiting for transfers between devices: 54 us -> 143 us
  starting transfers between devices: 42.4 us -> 75.6 us
  Pallas kernels: 132 us -> 136 us
    all_to_all x3 -> x0, blocking collectives: 157 us -> none  [exchange(): return lax.all_to_all(rows, GROUP, split_axis=0, concat_axis=0, tiled=True)]
    all_to_all x3 -> x6, waiting for transfers between devices: 48.3 us -> 137 us  [exchange(): return lax.all_to_all(rows, GROUP, split_axis=0, concat_axis=0, tiled=True)]
    all_to_all x3 -> x6, starting transfers between devices: 30.3 us -> 65.4 us  [exchange(): return lax.all_to_all(rows, GROUP, split_axis=0, concat_axis=0, tiled=True)]
    pallas_call x2 -> x6, Pallas kernels: 46.8 us -> 53.3 us  [the longest x2 31 us: outer_sums(): pl.pallas_call(kernel, grid=(width // piece,), in_specs=specs() + specs()...]
  transfers between devices with their start and end apart: 11 -> 14, of which waited for: 5 -> 6; matrix products, arithmetic and copies ran while one was open for 2% -> 2% of each run, Pallas kernels for 24% -> 28%
where the time goes in v2:
time: 371 us; the launch traced here: 370 us
  waiting for transfers between devices  143 us (39%)
  Pallas kernels  136 us (37%)
  starting transfers between devices  75.6 us (20%)
  local copies, waits for them, and re-layouts  8.39 us (2%)
  other arithmetic  6.28 us (2%)
    all_to_all x6, waiting for transfers between devices, exchange(): return lax.all_to_all(rows, GROUP, split_axis=0, concat_axis=0, tiled=True)  137 us
    all_to_all x6, starting transfers between devices, exchange(): return lax.all_to_all(rows, GROUP, split_axis=0, concat_axis=0, tiled=True)  65.4 us
    pallas_call x4, Pallas kernels, forward(): pl.pallas_call(kernel, grid=(count // TILE,), in_specs=[pl.BlockSpec((TIL...  37.4 us
    pallas_call x2, Pallas kernels, outer_sums(): pl.pallas_call(kernel, grid=(width // piece,), in_specs=specs() + specs()...  31 us
    pallas_call x4, Pallas kernels, gradients(): pl.pallas_call(kernel, grid=(count // tile,), in_specs=[pl.BlockSpec((til...  22.3 us
    pallas_call x2, Pallas kernels, part_rows(): pl.pallas_call(kernel, grid=(count // TILE,), in_specs=[pl.BlockSpec((TIL...  19.1 us
    ppermute x8, starting transfers between devices, swap(): return lax.ppermute(rows, 'tensor', [(0, 1), (1, 0)])  10.2 us
    pallas_call x2, Pallas kernels, combine(): pl.pallas_call(kernel, grid=(steps,), in_specs=[smem(), pl.BlockSpec((ste...  9.67 us
  transfers between devices with their start and end apart: 14, of which 6 were waited for; matrix products, arithmetic and copies ran while one was open for 2% of the time, Pallas kernels for 28%

profile of v2, /device:TPU:1, one launch (start us, length us, event | category | flops | bytes accessed | tf_op | source)
XLA Modules:
  0.0 370.0 jit_solution(16220444258386765976)
XLA Ops:
  0.6 0.7 pad_add_fusion.base_ref
  1.3 4.6 %route_pack.1 = (bf16[1024,2048]{1,0:T(8,128)(2,1)}, f32[64,128]{1,0:T(8,128)}, f32[64,128]{1,0:T(8,128)}) custom-call(s32[2]{0:T(128)} %pad_add_fusion.base_ref, s32[8,128]{1,0:T(8,128)} %bitcast.44, f32[8,128]{1,0:T(8,128)} %bitcast.45, bf16[128,2048]{1,0:T(8,128)(2,1)} %tok_ref.3), custom_call_target="tpu_custom_call" | custom-call | flops 33554432 | bytes 262144 | tf_op jit(solution)/shard_map/route_pack/pallas_call | solution.py:88
  5.9 12.4 %all-to-all-start = ((bf16[64,16,2048]{2,1,0:T(8,128)(2,1)}), bf16[64,16,2048]{2,1,0:T(8,128)(2,1)}, u32[]{:S(2)}, u32[]{:S(2)}) async-start(bf16[64,16,2048]{2,1,0:T(8,128)(2,1)} %bitcast.37), calls=%async_computation | async-start | bytes 8388608 | tf_op jit(solution)/shard_map/all_to_all | solution.py:365
  18.3 0.0 copy-start
  18.3 0.6 pad_add_fusion.1.base_ref
  18.9 2.9 pack.1
  21.8 0.0 copy-start.7
  21.8 0.0 copy-start.8
  21.8 0.0 copy-start.9
  21.9 1.9 pad_maximum_fusion.1.wa_ref
  23.7 1.1 copy-done.7
  24.8 0.5 copy-done.8
  25.3 0.5 copy-done.9
  25.8 3.1 pad_maximum_fusion.w_ref
  28.9 41.0 %all-to-all-done = bf16[64,16,2048]{2,1,0:T(8,128)(2,1)} async-done(((bf16[64,16,2048]{2,1,0:T(8,128)(2,1)}), bf16[64,16,2048]{2,1,0:T(8,128)(2,1)}, u32[]{:S(2)}, u32[]{:S(2)}) %all-to-all-start) | async-done | bytes 4194336 | tf_op jit(solution)/shard_map/all_to_all | solution.py:365
  69.9 2.6 collective-permute-start
  72.5 0.0 collective-permute-start.2
  72.5 15.2 %all-to-all-start.1 = ((bf16[64,8,2048]{2,1,0:T(8,128)(2,1)}), bf16[64,8,2048]{2,1,0:T(8,128)(2,1)}, u32[]{:S(2)}, u32[]{:S(2)}) async-start(bf16[64,8,2048]{2,1,0:T(8,128)(2,1)} %bitcast.34), calls=%async_computation.1 | async-start | bytes 4194304 | tf_op jit(solution)/shard_map/all_to_all | solution.py:365
  87.7 0.0 collective-permute-done.x_ref.refs_5_
  87.7 11.2 %forward.5 = (bf16[1024,768]{1,0:T(8,128)(2,1)}, f32[1024,384]{1,0:T(8,128)}, f32[1024,384]{1,0:T(8,128)}) custom-call(bf16[1024,2048]{1,0:T(8,128)(2,1)} %collective-permute-done.x_ref.refs_5_, bf16[2048,1536]{1,0:T(8,128)(2,1)} %pad_maximum_fusion.w_ref), custom_call_target="tpu_custom_call" | custom-call | flops 402653184 | bytes 557056 | tf_op jit(solution)/shard_map/forward/pallas_call | solution.py:146
  98.9 0.8 collective-permute-start.1
  99.7 11.2 %forward.4 = (bf16[1024,768]{1,0:T(8,128)(2,1)}, f32[1024,384]{1,0:T(8,128)}, f32[1024,384]{1,0:T(8,128)}) custom-call(bf16[1024,2048]{1,0:T(8,128)(2,1)} %bitcast.7.x_ref.refs_1_, bf16[2048,1536]{1,0:T(8,128)(2,1)} %pad_maximum_fusion.w_ref), custom_call_target="tpu_custom_call" | custom-call | flops 402653184 | bytes 557056 | tf_op jit(solution)/shard_map/forward/pallas_call | solution.py:146
  110.9 0.0 collective-permute-done.2.wb_ref
  110.9 0.0 collective-permute-done.1.b_ref
  110.9 11.4 %part_rows.2 = bf16[1024,2048]{1,0:T(8,128)(2,1)} custom-call(bf16[1024,768]{1,0:T(8,128)(2,1)} %get-tuple-element.49.a_ref.refs_3_, bf16[1024,768]{1,0:T(8,128)(2,1)} %collective-permute-done.1.b_ref, bf16[768,2048]{1,0:T(8,128)(2,1)} %pad_maximum_fusion.1.wa_ref, bf16[768,2048]{1,0:T(8,128)(2,1)} %collective-permute-done.2.wb_ref), custom_call_target="tpu_custom_call" | custom-call | flops 402653184 | bytes 655360 | tf_op jit(solution)/shard_map/part_rows/pallas_call | solution.py:173
  122.3 0.0 all-to-all-done.1
  122.3 11.2 %all-to-all-start.2 = ((bf16[64,16,2048]{2,1,0:T(8,128)(2,1)}), bf16[64,16,2048]{2,1,0:T(8,128)(2,1)}, u32[]{:S(2)}, u32[]{:S(2)}) async-start(bf16[64,16,2048]{2,1,0:T(8,128)(2,1)} %bitcast.32), calls=%async_computation.2 | async-start | bytes 8388608 | tf_op jit(solution)/shard_map/all_to_all | solution.py:365
  133.5 0.5 collective-permute-start.3
  134.0 4.0 %collective-permute-done.3.x_ref.refs_5_ = bf16[512,2048]{1,0:T(8,128)(2,1)S(1)} collective-permute-done((bf16[512,2048]{1,0:T(8,128)(2,1)}, bf16[512,2048]{1,0:T(8,128)(2,1)S(1)}, u32[]{:S(2)}, u32[]{:S(2)}) %collective-permute-start.3) | collective-permute-done | bytes 2097184 | tf_op jit(solution)/shard_map/ppermute | solution.py:381
  138.0 1.4 copy-done.3
  139.4 7.5 %forward.7 = (bf16[512,768]{1,0:T(8,128)(2,1)}, f32[512,384]{1,0:T(8,128)}, f32[512,384]{1,0:T(8,128)}) custom-call(bf16[512,2048]{1,0:T(8,128)(2,1)} %copy-done.3, bf16[2048,1536]{1,0:T(8,128)(2,1)} %pad_maximum_fusion.w_ref), custom_call_target="tpu_custom_call" | custom-call | flops 201326592 | bytes 278528 | tf_op jit(solution)/shard_map/forward/pallas_call | solution.py:146
  146.9 0.4 collective-permute-start.4
  147.3 7.5 %forward.6 = (bf16[512,768]{1,0:T(8,128)(2,1)}, f32[512,384]{1,0:T(8,128)}, f32[512,384]{1,0:T(8,128)}) custom-call(bf16[512,2048]{1,0:T(8,128)(2,1)} %bitcast.15.x_ref.refs_1_, bf16[2048,1536]{1,0:T(8,128)(2,1)} %pad_maximum_fusion.w_ref), custom_call_target="tpu_custom_call" | custom-call | flops 201326592 | bytes 278528 | tf_op jit(solution)/shard_map/forward/pallas_call | solution.py:146
  154.8 0.0 collective-permute-done.4.b_ref
  154.8 0.0 copy-start.11
  154.8 0.9 copy-done.11
  155.7 7.7 %part_rows.3 = bf16[512,2048]{1,0:T(8,128)(2,1)} custom-call(bf16[512,768]{1,0:T(8,128)(2,1)} %get-tuple-element.54.a_ref.refs_3_, bf16[512,768]{1,0:T(8,128)(2,1)} %copy-done.11, bf16[768,2048]{1,0:T(8,128)(2,1)} %pad_maximum_fusion.1.wa_ref, bf16[768,2048]{1,0:T(8,128)(2,1)} %collective-permute-done.2.wb_ref), custom_call_target="tpu_custom_call" | custom-call | flops 201326592 | bytes 524288 | tf_op jit(solution)/shard_map/part_rows/pallas_call | solution.py:173
  163.3 24.1 %all-to-all-done.2 = bf16[64,16,2048]{2,1,0:T(8,128)(2,1)} async-done(((bf16[64,16,2048]{2,1,0:T(8,128)(2,1)}), bf16[64,16,2048]{2,1,0:T(8,128)(2,1)}, u32[]{:S(2)}, u32[]{:S(2)}) %all-to-all-start.2) | async-done | bytes 4194336 | tf_op jit(solution)/shard_map/all_to_all | solution.py:365
  187.5 11.3 %all-to-all-start.3 = ((bf16[64,8,2048]{2,1,0:T(8,128)(2,1)}), bf16[64,8,2048]{2,1,0:T(8,128)(2,1)S(1)}, u32[]{:S(2)}, u32[]{:S(2)}) async-start(bf16[64,8,2048]{2,1,0:T(8,128)(2,1)} %bitcast.33), calls=%async_computation.3 | async-start | bytes 4194304 | tf_op jit(solution)/shard_map/all_to_all | solution.py:365
  198.8 5.7 %combine.2.rest_0_ = f32[128,2048]{1,0:T(8,128)} custom-call(s32[2]{0:T(128)} %pad_add_fusion.base_ref, f32[64,128]{1,0:T(8,128)} %get-tuple-element.43.pos_ref, f32[64,128]{1,0:T(8,128)} %get-tuple-element.44.gm_ref, bf16[1024,2048]{1,0:T(8,128)(2,1)} %bitcast.17.rows_ref), custom_call_target="tpu_custom_call" | custom-call | flops 67108864 | bytes 262144 | tf_op jit(solution)/shard_map/combine/pallas_call | solution.py:225
  204.5 21.2 %all-to-all-done.3 = bf16[64,8,2048]{2,1,0:T(8,128)(2,1)S(1)} async-done(((bf16[64,8,2048]{2,1,0:T(8,128)(2,1)}), bf16[64,8,2048]{2,1,0:T(8,128)(2,1)S(1)}, u32[]{:S(2)}, u32[]{:S(2)}) %all-to-all-start.3) | async-done | bytes 2097184 | tf_op jit(solution)/shard_map/all_to_all | solution.py:365
  225.7 1.3 copy-done.4
  227.0 4.0 %combine.3.own_ref = f32[128,2048]{1,0:T(8,128)} custom-call(s32[2]{0:T(128)} %pad_add_fusion.1.base_ref, f32[64,128]{1,0:T(8,128)} %get-tuple-element.43.pos_ref, f32[64,128]{1,0:T(8,128)} %get-tuple-element.44.gm_ref, bf16[512,2048]{1,0:T(8,128)(2,1)} %bitcast.36, f32[128,2048]{1,0:T(8,128)} %combine.2.rest_0_), custom_call_target="tpu_custom_call" | custom-call | flops 33554432 | bytes 131072 | tf_op jit(solution)/shard_map/combine/pallas_call | solution.py:225
  231.0 3.7 %collective-permute-start.5 = (f32[128,2048]{1,0:T(8,128)}, f32[128,2048]{1,0:T(8,128)S(1)}, u32[]{:S(2)}, u32[]{:S(2)}) collective-permute-start(f32[128,2048]{1,0:T(8,128)} %combine.3.own_ref), channel_id=1, source_target_pairs={{0,1},{1,0},{2,3},{3,2},{4,5},{5,4},{6,7},{7,6},{8,9},{9,8},{10,11... | collective-permute-start | bytes 3145736 | tf_op jit(solution)/shard_map/ppermute | solution.py:381
  234.7 0.7 copy.14.tw_ref
  235.5 1.7 collective-permute-done.5.other_ref
  237.2 1.0 copy-done.5
  238.2 5.6 %weigh_pack.2 = (bf16[1024,2048]{1,0:T(8,128)(2,1)}, bf16[128,1024]{1,0:T(8,128)(2,1)}) custom-call(s32[2]{0:T(128)} %pad_add_fusion.base_ref, f32[64,128]{1,0:T(8,128)} %get-tuple-element.43.pos_ref, f32[64,128]{1,0:T(8,128)} %get-tuple-element.44.gm_ref, f32[128,1]{1,0:T(8,128)} %copy.14.tw_ref, f32[128,2048]{1,0:T(8,128)} %combine.3.own_ref, ...), custom_call_target="tpu_custom_call" | custom-call | flops 100663296 | bytes 262144 | tf_op jit(solution)/shard_map/weigh_pack/pallas_call | solution.py:273
  243.8 5.7 %all-to-all-start.4 = ((bf16[64,16,2048]{2,1,0:T(8,128)(2,1)}), bf16[64,16,2048]{2,1,0:T(8,128)(2,1)}, u32[]{:S(2)}, u32[]{:S(2)}) async-start(bf16[64,16,2048]{2,1,0:T(8,128)(2,1)} %bitcast.38), calls=%async_computation.4 | async-start | bytes 8388608 | tf_op jit(solution)/shard_map/all_to_all | solution.py:365
  249.5 3.9 %weigh_pack.3 = bf16[512,2048]{1,0:T(8,128)(2,1)} custom-call(s32[2]{0:T(128)} %pad_add_fusion.1.base_ref, f32[64,128]{1,0:T(8,128)} %get-tuple-element.43.pos_ref, f32[64,128]{1,0:T(8,128)} %get-tuple-element.44.gm_ref, f32[128,1]{1,0:T(8,128)} %copy.14.tw_ref, f32[128,2048]{1,0:T(8,128)} %combine.3.own_ref, f32[128,2048]{1,0:T(8,128)} %copy-done.5), custom_call_target="tpu_custom_call" | custom-call | flops 50331648 | bytes 131072 | tf_op jit(solution)/shard_map/weigh_pack/pallas_call | solution.py:273
  253.4 50.5 %all-to-all-done.4 = bf16[64,16,2048]{2,1,0:T(8,128)(2,1)} async-done(((bf16[64,16,2048]{2,1,0:T(8,128)(2,1)}), bf16[64,16,2048]{2,1,0:T(8,128)(2,1)}, u32[]{:S(2)}, u32[]{:S(2)}) %all-to-all-start.4) | async-done | bytes 4194336 | tf_op jit(solution)/shard_map/all_to_all | solution.py:365
  303.9 1.8 collective-permute-start.6
  305.7 9.6 %all-to-all-start.5 = ((bf16[64,8,2048]{2,1,0:T(8,128)(2,1)}), bf16[64,8,2048]{2,1,0:T(8,128)(2,1)S(1)}, u32[]{:S(2)}, u32[]{:S(2)}) async-start(bf16[64,8,2048]{2,1,0:T(8,128)(2,1)} %bitcast.35), calls=%async_computation.5 | async-start | bytes 4194304 | tf_op jit(solution)/shard_map/all_to_all | solution.py:365
  315.3 6.8 %gradients.4.refs_2_ = bf16[1024,768]{1,0:T(8,128)(2,1)} custom-call(bf16[1024,2048]{1,0:T(8,128)(2,1)} %bitcast.21.q_ref.refs_0_, f32[1024,384]{1,0:T(8,128)} %get-tuple-element.63.silu_ref, f32[1024,384]{1,0:T(8,128)} %get-tuple-element.64.us_ref, bf16[384,2048]{1,0:T(8,128)(2,1)} %bitcast.24), custom_call_target="tpu_custom_call" | custom-call | flops 100663296 | bytes 262144 | tf_op jit(solution)/shard_map/gradients/pallas_call | solution.py:303
  322.1 0.0 collective-permute-done.6.q_ref.refs_4_
  322.1 6.8 %gradients.5.refs_6_ = bf16[1024,768]{1,0:T(8,128)(2,1)} custom-call(bf16[1024,2048]{1,0:T(8,128)(2,1)} %collective-permute-done.6.q_ref.refs_4_, f32[1024,384]{1,0:T(8,128)} %get-tuple-element.65.silu_ref, f32[1024,384]{1,0:T(8,128)} %get-tuple-element.66.us_ref, bf16[384,2048]{1,0:T(8,128)(2,1)} %bitcast.25), custom_call_target="tpu_custom_call" | custom-call | flops 100663296 | bytes 262144 | tf_op jit(solution)/shard_map/gradients/pallas_call | solution.py:303
  328.9 16.5 %outer_sums.2 = (f32[1,2048,384]{2,1,0:T(8,128)}, f32[1,2048,384]{2,1,0:T(8,128)}, f32[1,384,2048]{2,1,0:T(8,128)}) custom-call(bf16[1024,2048]{1,0:T(8,128)(2,1)} %bitcast.21.q_ref.refs_0_, bf16[1024,2048]{1,0:T(8,128)(2,1)} %bitcast.7.x_ref.refs_1_, bf16[1024,768]{1,0:T(8,128)(2,1)} %gradients.4.refs_2_, ...), custom_call_target="tpu_custom_call" | custom-call | flops 603979776 | bytes 1048576 | tf_op jit(solution)/shard_map/outer_sums/pallas_call | solution.py:352
  345.5 0.0 all-to-all-done.5
  345.5 0.4 collective-permute-start.7
  345.9 1.0 copy-done.2
  346.8 4.3 %gradients.6.refs_2_ = bf16[512,768]{1,0:T(8,128)(2,1)} custom-call(bf16[512,2048]{1,0:T(8,128)(2,1)} %bitcast.30, f32[512,384]{1,0:T(8,128)} %get-tuple-element.71.silu_ref, f32[512,384]{1,0:T(8,128)} %get-tuple-element.72.us_ref, bf16[384,2048]{1,0:T(8,128)(2,1)} %bitcast.26), custom_call_target="tpu_custom_call" | custom-call | flops 50331648 | bytes 131072 | tf_op jit(solution)/shard_map/gradients/pallas_call | solution.py:303
  351.1 0.0 collective-permute-done.7.q_ref.refs_4_
  351.2 4.3 %gradients.7.refs_6_ = bf16[512,768]{1,0:T(8,128)(2,1)} custom-call(bf16[512,2048]{1,0:T(8,128)(2,1)} %collective-permute-done.7.q_ref.refs_4_, f32[512,384]{1,0:T(8,128)} %get-tuple-element.73.silu_ref, f32[512,384]{1,0:T(8,128)} %get-tuple-element.74.us_ref, bf16[384,2048]{1,0:T(8,128)(2,1)} %bitcast.27), custom_call_target="tpu_custom_call" | custom-call | flops 50331648 | bytes 131072 | tf_op jit(solution)/shard_map/gradients/pallas_call | solution.py:303
  355.5 14.4 %outer_sums.3 = (f32[1,2048,384]{2,1,0:T(8,128)}, f32[1,2048,384]{2,1,0:T(8,128)}, f32[1,384,2048]{2,1,0:T(8,128)}) custom-call(bf16[512,2048]{1,0:T(8,128)(2,1)} %bitcast.31, bf16[512,2048]{1,0:T(8,128)(2,1)} %bitcast.15.x_ref.refs_1_, bf16[512,768]{1,0:T(8,128)(2,1)} %gradients.6.refs_2_, bf16[512,768]{1,0:T(8,128)(2,1)} %get-tuple-element.54.a_ref.refs_3_, ...), custom_call_target="tpu_custom_call" | custom-call | flops 301989888 | bytes 524288 | tf_op jit(solution)/shard_map/outer_sums/pallas_call | solution.py:352
  (13 shorter events, 0.0 us)
Async XLA Ops:
  5.9 15.9 %copy-start.10 = (bf16[1,384,2048]{2,1,0:T(8,128)(2,1)S(1)}, bf16[1,384,2048]{2,1,0:T(8,128)(2,1)}, u32[]{:S(2)}) copy-start(bf16[1,384,2048]{2,1,0:T(8,128)(2,1)} %param.19) | copy-start | bytes 4718596
  5.9 64.0 %all-to-all-start = ((bf16[64,16,2048]{2,1,0:T(8,128)(2,1)}), bf16[64,16,2048]{2,1,0:T(8,128)(2,1)}, u32[]{:S(2)}, u32[]{:S(2)}) async-start(bf16[64,16,2048]{2,1,0:T(8,128)(2,1)} %bitcast.37), calls=%async_computation | async-start | bytes 8388608 | tf_op jit(solution)/shard_map/all_to_all | solution.py:365
  18.3 3.5 copy-start
  21.8 1.9 copy-start.6
  21.8 3.0 copy-start.7
  21.8 3.5 copy-start.8
  21.8 3.9 %copy-start.9 = (bf16[1,2048,384]{2,1,0:T(8,128)(2,1)S(1)}, bf16[1,2048,384]{2,1,0:T(8,128)(2,1)}, u32[]{:S(2)}) copy-start(bf16[1,2048,384]{2,1,0:T(8,128)(2,1)} %param.14) | copy-start | bytes 4718596
  25.8 46.7 %copy-start.1 = (bf16[768,2048]{1,0:T(8,128)(2,1)S(1)}, bf16[768,2048]{1,0:T(8,128)(2,1)}, u32[]{:S(2)}) copy-start(bf16[768,2048]{1,0:T(8,128)(2,1)} %pad_maximum_fusion.1.wa_ref) | copy-start | bytes 9437188
  69.9 17.9 %collective-permute-start = (bf16[1024,2048]{1,0:T(8,128)(2,1)}, bf16[1024,2048]{1,0:T(8,128)(2,1)}, u32[]{:S(2)}, u32[]{:S(2)}) collective-permute-start(bf16[1024,2048]{1,0:T(8,128)(2,1)} %bitcast.7.x_ref.refs_1_), channel_id=1, source_target_pairs={{0,1},{1,0},{2,3},{3,2},{4,5},{5,4},{6,7},{7,6},{8,9},{9,8},{10,11... | collective-permute-start | bytes 12582920 | tf_op jit(solution)/shard_map/ppermute | solution.py:381
  72.5 38.4 %collective-permute-start.2 = (bf16[768,2048]{1,0:T(8,128)(2,1)S(1)}, bf16[768,2048]{1,0:T(8,128)(2,1)}, u32[]{:S(2)}, u32[]{:S(2)}) collective-permute-start(bf16[768,2048]{1,0:T(8,128)(2,1)S(1)} %copy-done.1), channel_id=1, source_target_pairs={{0,1},{1,0},{2,3},{3,2},{4,5},{5,4},{6,7},{7,6},{8,9},{9,8},{10,11... | collective-permute-start | bytes 9437192 | tf_op jit(solution)/shard_map/ppermute | solution.py:381
  72.5 49.8 %all-to-all-start.1 = ((bf16[64,8,2048]{2,1,0:T(8,128)(2,1)}), bf16[64,8,2048]{2,1,0:T(8,128)(2,1)}, u32[]{:S(2)}, u32[]{:S(2)}) async-start(bf16[64,8,2048]{2,1,0:T(8,128)(2,1)} %bitcast.34), calls=%async_computation.1 | async-start | bytes 4194304 | tf_op jit(solution)/shard_map/all_to_all | solution.py:365
  98.9 12.0 %collective-permute-start.1 = (bf16[1024,768]{1,0:T(8,128)(2,1)}, bf16[1024,768]{1,0:T(8,128)(2,1)}, u32[]{:S(2)}, u32[]{:S(2)}) collective-permute-start(bf16[1024,768]{1,0:T(8,128)(2,1)} %get-tuple-element.50.refs_7_), channel_id=1, source_target_pairs={{0,1},{1,0},{2,3},{3,2},{4,5},{5,4},{6,7},{7,6},{8,9},{9,8},{10,11... | collective-permute-start | bytes 4718600 | tf_op jit(solution)/shard_map/ppermute | solution.py:381
  122.3 65.2 %all-to-all-start.2 = ((bf16[64,16,2048]{2,1,0:T(8,128)(2,1)}), bf16[64,16,2048]{2,1,0:T(8,128)(2,1)}, u32[]{:S(2)}, u32[]{:S(2)}) async-start(bf16[64,16,2048]{2,1,0:T(8,128)(2,1)} %bitcast.32), calls=%async_computation.2 | async-start | bytes 8388608 | tf_op jit(solution)/shard_map/all_to_all | solution.py:365
  133.5 4.5 %collective-permute-start.3 = (bf16[512,2048]{1,0:T(8,128)(2,1)}, bf16[512,2048]{1,0:T(8,128)(2,1)S(1)}, u32[]{:S(2)}, u32[]{:S(2)}) collective-permute-start(bf16[512,2048]{1,0:T(8,128)(2,1)} %bitcast.15.x_ref.refs_1_), channel_id=1, source_target_pairs={{0,1},{1,0},{2,3},{3,2},{4,5},{5,4},{6,7},{7,6},{8,9},{9,8},{10,11... | collective-permute-start | bytes 6291464 | tf_op jit(solution)/shard_map/ppermute | solution.py:381
  138.0 1.4 copy-start.3
  146.9 7.9 %collective-permute-start.4 = (bf16[512,768]{1,0:T(8,128)(2,1)}, bf16[512,768]{1,0:T(8,128)(2,1)S(1)}, u32[]{:S(2)}, u32[]{:S(2)}) collective-permute-start(bf16[512,768]{1,0:T(8,128)(2,1)} %get-tuple-element.55.refs_7_), channel_id=1, source_target_pairs={{0,1},{1,0},{2,3},{3,2},{4,5},{5,4},{6,7},{7,6},{8,9},{9,8},{10,11... | collective-permute-start | bytes 2359304 | tf_op jit(solution)/shard_map/ppermute | solution.py:381
  154.8 0.9 copy-start.11
  187.5 38.2 %all-to-all-start.3 = ((bf16[64,8,2048]{2,1,0:T(8,128)(2,1)}), bf16[64,8,2048]{2,1,0:T(8,128)(2,1)S(1)}, u32[]{:S(2)}, u32[]{:S(2)}) async-start(bf16[64,8,2048]{2,1,0:T(8,128)(2,1)} %bitcast.33), calls=%async_computation.3 | async-start | bytes 4194304 | tf_op jit(solution)/shard_map/all_to_all | solution.py:365
  204.5 30.2 %copy-start.12 = (f32[128]{0:T(128)S(1)}, f32[128]{0:T(128)}, u32[]{:S(2)}) copy-start(f32[128]{0:T(128)} %param.13) | copy-start | bytes 1540
  225.7 1.3 copy-start.4
  231.0 6.2 %collective-permute-start.5 = (f32[128,2048]{1,0:T(8,128)}, f32[128,2048]{1,0:T(8,128)S(1)}, u32[]{:S(2)}, u32[]{:S(2)}) collective-permute-start(f32[128,2048]{1,0:T(8,128)} %combine.3.own_ref), channel_id=1, source_target_pairs={{0,1},{1,0},{2,3},{3,2},{4,5},{5,4},{6,7},{7,6},{8,9},{9,8},{10,11... | collective-permute-start | bytes 3145736 | tf_op jit(solution)/shard_map/ppermute | solution.py:381
  237.2 1.0 copy-start.5
  243.8 60.1 %all-to-all-start.4 = ((bf16[64,16,2048]{2,1,0:T(8,128)(2,1)}), bf16[64,16,2048]{2,1,0:T(8,128)(2,1)}, u32[]{:S(2)}, u32[]{:S(2)}) async-start(bf16[64,16,2048]{2,1,0:T(8,128)(2,1)} %bitcast.38), calls=%async_computation.4 | async-start | bytes 8388608 | tf_op jit(solution)/shard_map/all_to_all | solution.py:365
  303.9 18.2 %collective-permute-start.6 = (bf16[1024,2048]{1,0:T(8,128)(2,1)}, bf16[1024,2048]{1,0:T(8,128)(2,1)}, u32[]{:S(2)}, u32[]{:S(2)}) collective-permute-start(bf16[1024,2048]{1,0:T(8,128)(2,1)} %bitcast.21.q_ref.refs_0_), channel_id=1, source_target_pairs={{0,1},{1,0},{2,3},{3,2},{4,5},{5,4},{6,7},{7,6},{8,9},{9,8},{10,11... | collective-permute-start | bytes 12582920 | tf_op jit(solution)/shard_map/ppermute | solution.py:381
  305.7 39.8 %all-to-all-start.5 = ((bf16[64,8,2048]{2,1,0:T(8,128)(2,1)}), bf16[64,8,2048]{2,1,0:T(8,128)(2,1)S(1)}, u32[]{:S(2)}, u32[]{:S(2)}) async-start(bf16[64,8,2048]{2,1,0:T(8,128)(2,1)} %bitcast.35), calls=%async_computation.5 | async-start | bytes 4194304 | tf_op jit(solution)/shard_map/all_to_all | solution.py:365
  345.5 1.3 copy-start.2
  345.5 5.7 %collective-permute-start.7 = (bf16[512,2048]{1,0:T(8,128)(2,1)S(1)}, bf16[512,2048]{1,0:T(8,128)(2,1)}, u32[]{:S(2)}, u32[]{:S(2)}) collective-permute-start(bf16[512,2048]{1,0:T(8,128)(2,1)S(1)} %bitcast.29), channel_id=1, source_target_pairs={{0,1},{1,0},{2,3},{3,2},{4,5},{5,4},{6,7},{7,6},{8,9},{9,8},{10,11... | collective-permute-start | bytes 6291464 | tf_op jit(solution)/shard_map/ppermute | solution.py:381

commit v3 on v2

--- a/solution.py
+++ b/solution.py
@@ -8,9 +8,12 @@
 BF = jnp.bfloat16
 F32 = jnp.float32
 GROUP = ("dp", "expert")
-VMEM_LIMIT = 60 * 1024 * 1024
+VMEM_LIMIT = 63 * 1024 * 1024
 TILE = 256
-PIECE = 256
+PIECE = 512
+LAST_PIECE = 512
+ROWS = 512
+SLOTS = (1, 2)
 
 
 def params():
@@ -140,8 +143,8 @@
         us = sigma * (1.0 + gate * (1.0 - sigma)) * up
         ad_ref[:, :hidden] = (silu * up).astype(BF)
         ad_ref[:, hidden:] = (us * d_gate + silu * d_up).astype(BF)
-        silu_ref[...] = silu
-        us_ref[...] = us
+        silu_ref[...] = silu.astype(BF)
+        us_ref[...] = us.astype(BF)
 
     return pl.pallas_call(
         kernel,
@@ -154,8 +157,8 @@
         ],
         out_shape=[
             jax.ShapeDtypeStruct((count, 2 * hidden), BF),
-            jax.ShapeDtypeStruct((count, hidden), F32),
-            jax.ShapeDtypeStruct((count, hidden), F32),
+            jax.ShapeDtypeStruct((count, hidden), BF),
+            jax.ShapeDtypeStruct((count, hidden), BF),
         ],
         compiler_params=params(),
         cost_estimate=cost(8 * count * width * hidden, 2 * count * width + 12 * count * hidden),
@@ -187,58 +190,56 @@
     )(ad_own, ad_other, down_own, down_other)
 
 
-def split_gates(pos, gm, base, per):
-    weight = jnp.where(slot_match(pos, base, per), spread(gm, per), 0.0)
-    high = weight.astype(BF)
-    low = (weight - high.astype(F32)).astype(BF)
-    return high, low
-
-
-def combine(base, pos, gm, rows, start, per):
+def gate_matrix(base, pos, gm, per):
     experts, toks = pos.shape
-    width = rows.shape[1]
     step = TILE // per
-    steps = experts // step
-    first = start is None
-
-    def kernel(base_ref, pos_ref, gm_ref, rows_ref, *rest):
-        start_ref = None if first else rest[0]
-        out_ref, acc_ref = rest[-2:]
-        i = pl.program_id(0)
-        high, low = split_gates(pos_ref[...], gm_ref[...], base_ref[0], per)
-        term = mm_rows(jnp.concatenate([high, low], axis=1), rows_ref[...])
-
-        @pl.when(i == 0)
-        def _():
-            acc_ref[...] = term
-
-        @pl.when(i > 0)
-        def _():
-            acc_ref[...] += term
-
-        @pl.when(i == steps - 1)
-        def _():
-            total = acc_ref[:toks, :] + acc_ref[toks:, :]
-            out_ref[...] = total if first else total + start_ref[...]
-
-    extra = [] if first else [start]
-    return pl.pallas_call(
-        kernel,
-        grid=(steps,),
+
+    def kernel(base_ref, pos_ref, gm_ref, out_ref):
+        match = slot_match(pos_ref[...], base_ref[0], per)
+        weight = jnp.where(match, spread(gm_ref[...], per), 0.0).T
+        high = weight.astype(BF)
+        out_ref[:toks, :] = high
+        out_ref[toks:, :] = (weight - high.astype(F32)).astype(BF)
+
+    return pl.pallas_call(
+        kernel,
+        grid=(experts // step,),
         in_specs=[
             smem(),
             pl.BlockSpec((step, toks), lambda i: (i, 0)),
             pl.BlockSpec((step, toks), lambda i: (i, 0)),
-            pl.BlockSpec((TILE, width), lambda i: (i, 0)),
-        ]
-        + [fixed((toks, width)) for _ in extra],
-        out_specs=pl.BlockSpec((toks, width), lambda i: (0, 0)),
+        ],
+        out_specs=pl.BlockSpec((2 * toks, TILE), lambda i: (0, i)),
+        out_shape=jax.ShapeDtypeStruct((2 * toks, experts * per), BF),
+        compiler_params=params(),
+        cost_estimate=cost(4 * experts * per * toks, 4 * experts * per * toks),
+        name="gate_matrix",
+    )(base, pos, gm)
+
+
+def combine(matrix, rows, start):
+    count, width = rows.shape
+    toks = matrix.shape[0] // 2
+    piece = 1024
+
+    def kernel(matrix_ref, rows_ref, *rest):
+        both = mm(matrix_ref[...], rows_ref[...])
+        total = both[:toks] + both[toks:]
+        rest[-1][...] = total if start is None else total + rest[0][...]
+
+    extra = [] if start is None else [start]
+    column = pl.BlockSpec((toks, piece), lambda i: (0, i))
+    return pl.pallas_call(
+        kernel,
+        grid=(width // piece,),
+        in_specs=[fixed((2 * toks, count)), pl.BlockSpec((count, piece), lambda i: (0, i))]
+        + [column for _ in extra],
+        out_specs=column,
         out_shape=jax.ShapeDtypeStruct((toks, width), F32),
-        scratch_shapes=[pltpu.VMEM((2 * toks, width), F32)],
-        compiler_params=params(),
-        cost_estimate=cost(4 * experts * per * toks * width, 2 * experts * per * width),
+        compiler_params=params(),
+        cost_estimate=cost(4 * count * toks * width, 2 * count * width),
         name="combine",
-    )(base, pos, gm, rows, *extra)
+    )(matrix, rows, *extra)
 
 
 def weigh_pack(base, pos, gm, weight, own, other, per, half):
@@ -317,48 +318,131 @@
     )(q, silu, us, down)
 
 
-def outer_sums(own, other, start, factor, hidden):
+def phased_sums(own, other, down, factor):
     count, width = own[0].shape
+    hidden = down.shape[0]
+    tile = min(ROWS, count)
     piece = PIECE
+    tiles = count // tile
+    head = 2 * tiles
 
     def kernel(*refs):
-        gate_out, up_out, down_out = refs[-3:]
-        gate_up, down = 0.0, 0.0
-        for q_ref, x_ref, g_ref, act_ref in (refs[:4], refs[4:8]):
-            gate_up += mm_rows(x_ref[...], g_ref[...])
-            down += mm_rows(act_ref[...], q_ref[...])
-        terms = [gate_up[:, :hidden], gate_up[:, hidden:], down]
-        for out, term, begin in zip((gate_out, up_out, down_out), terms, refs[8:11] if start else [None] * 3):
-            out[0] = factor * term + begin[0] if start else factor * term
-
-    def specs():
+        sides = (refs[:5], refs[5:10])
+        down_ref = refs[10]
+        outs = refs[11:14]
+        g_ref, turned_ref, q_ref = refs[14:]
+        i = pl.program_id(0)
+
+        for side, (tile_ref, _, ad_ref, silu_ref, us_ref) in enumerate(sides):
+            for n in range(tiles):
+
+                @pl.when(i == side * tiles + n)
+                def _(side=side, n=n, tile_ref=tile_ref, ad_ref=ad_ref, silu_ref=silu_ref, us_ref=us_ref):
+                    rows = slice(side * count + n * tile, side * count + (n + 1) * tile)
+                    q = tile_ref[...]
+                    back = mm_t(q, down_ref[...])
+                    g_ref[rows, :hidden] = (back * us_ref[...]).astype(BF)
+                    g_ref[rows, hidden:] = (back * silu_ref[...]).astype(BF)
+                    turned_ref[:, rows] = ad_ref[...].T
+                    q_ref[rows, :] = q
+
+        @pl.when(i >= head)
+        def _():
+            cols = pl.ds(pl.multiple_of(jnp.maximum(i - head, 0) * piece, piece), piece)
+            gate_up = mm_rows(sides[0][1][...], g_ref[:count, :])
+            gate_up += mm_rows(sides[1][1][...], g_ref[count:, :])
+            outs[0][0] = factor * gate_up[:, :hidden]
+            outs[1][0] = factor * gate_up[:, hidden:]
+            outs[2][0] = factor * mm(turned_ref[...], q_ref[:, cols])
+
+    def later(i):
+        return jnp.maximum(i - head, 0)
+
+    def specs(first):
+        def at(i):
+            return jnp.clip(i - first, 0, tiles - 1)
+
         return [
-            pl.BlockSpec((count, piece), lambda i: (0, i)),
-            pl.BlockSpec((count, piece), lambda i: (0, i)),
-            fixed((count, 2 * hidden)),
-            pl.BlockSpec(
-                (count, hidden), lambda i: (0, 0), pipeline_mode=pl.Buffered(buffer_count=1)
-            ),
+            pl.BlockSpec((tile, width), lambda i: (at(i), 0)),
+            pl.BlockSpec((count, piece), lambda i: (0, later(i))),
+            pl.BlockSpec((tile, hidden), lambda i: (at(i), 0)),
+            pl.BlockSpec((tile, hidden), lambda i: (at(i), 0)),
+            pl.BlockSpec((tile, hidden), lambda i: (at(i), 0)),
         ]
 
-    def results():
-        return [
-            pl.BlockSpec((1, piece, hidden), lambda i: (0, i, 0)),
-            pl.BlockSpec((1, piece, hidden), lambda i: (0, i, 0)),
-            pl.BlockSpec((1, hidden, piece), lambda i: (0, 0, i)),
-        ]
-
     shapes = [(1, width, hidden), (1, width, hidden), (1, hidden, width)]
     return pl.pallas_call(
         kernel,
+        grid=(head + width // piece,),
+        in_specs=specs(0) + specs(tiles) + [fixed((hidden, width))],
+        out_specs=[
+            pl.BlockSpec((1, piece, hidden), lambda i: (0, later(i), 0)),
+            pl.BlockSpec((1, piece, hidden), lambda i: (0, later(i), 0)),
+            pl.BlockSpec((1, hidden, piece), lambda i: (0, 0, later(i))),
+        ],
+        out_shape=[jax.ShapeDtypeStruct(shape, F32) for shape in shapes],
+        scratch_shapes=[
+            pltpu.VMEM((2 * count, 2 * hidden), BF),
+            pltpu.VMEM((hidden, 2 * count), BF),
+            pltpu.VMEM((2 * count, width), BF),
+        ],
+        compiler_params=params(),
+        cost_estimate=cost(16 * count * width * hidden, 8 * count * width),
+        name="phased_sums",
+    )(*own, *other, down)
+
+
+def last_sums(own, other, silu, us, down, start, factor):
+    count, width = own[0].shape
+    hidden = down.shape[0]
+    piece = LAST_PIECE
+
+    def kernel(*refs):
+        q_ref, x_ref, g_ref, act_ref, q2_ref, x2_ref, act2_ref, silu_ref, us_ref, down_ref = refs[:10]
+        begins, outs = refs[10:13], refs[13:16]
+        g2_ref, turned_ref = refs[16:]
+        i = pl.program_id(0)
+
+        @pl.when(i == 0)
+        def _():
+            back = mm_t(q2_ref[...], down_ref[...])
+            g2_ref[:, :hidden] = (back * us_ref[...]).astype(BF)
+            g2_ref[:, hidden:] = (back * silu_ref[...]).astype(BF)
+            turned_ref[:, :count] = act_ref[...].T
+            turned_ref[:, count:] = act2_ref[...].T
+
+        cols = pl.ds(pl.multiple_of(i * piece, piece), piece)
+        gate_up = mm_rows(x_ref[...], g_ref[...]) + mm_rows(x2_ref[...], g2_ref[...])
+        below = mm(turned_ref[:, :count], q_ref[...]) + mm(turned_ref[:, count:], q2_ref[:, cols])
+        terms = (gate_up[:, :hidden], gate_up[:, hidden:], below)
+        for out, term, begin in zip(outs, terms, begins):
+            out[0] = factor * term + begin[0]
+
+    column = pl.BlockSpec((count, piece), lambda i: (0, i))
+    act = pl.BlockSpec((count, hidden), lambda i: (0, 0), pipeline_mode=pl.Buffered(buffer_count=1))
+    results = [
+        pl.BlockSpec((1, piece, hidden), lambda i: (0, i, 0)),
+        pl.BlockSpec((1, piece, hidden), lambda i: (0, i, 0)),
+        pl.BlockSpec((1, hidden, piece), lambda i: (0, 0, i)),
+    ]
+    shapes = [(1, width, hidden), (1, width, hidden), (1, hidden, width)]
+    return pl.pallas_call(
+        kernel,
         grid=(width // piece,),
-        in_specs=specs() + specs() + (results() if start else []),
-        out_specs=results(),
+        in_specs=[column, column, fixed((count, 2 * hidden)), act]
+        + [fixed((count, width)), column, act]
+        + [fixed((count, hidden)), fixed((count, hidden)), fixed((hidden, width))]
+        + results,
+        out_specs=results,
         out_shape=[jax.ShapeDtypeStruct(shape, F32) for shape in shapes],
-        compiler_params=params(),
-        cost_estimate=cost(12 * count * width * hidden, 8 * count * width),
-        name="outer_sums",
-    )(*own, *other, *start)
+        scratch_shapes=[
+            pltpu.VMEM((count, 2 * hidden), BF),
+            pltpu.VMEM((hidden, 2 * count), BF),
+        ],
+        compiler_params=params(),
+        cost_estimate=cost(14 * count * width * hidden, 8 * count * width),
+        name="last_sums",
+    )(*own, *other, silu, us, down, *start)
 
 
 def exchange(rows):
@@ -372,24 +456,30 @@
     cores = lax.axis_size("tensor")
     hidden = w_gate.shape[2]
     per_core = min(3 * toks * picks // experts, toks) // cores
-    per_a = 2 * per_core // 3
-    per_b = per_core - per_a
     core = lax.axis_index("tensor")
     factor = 1.0 / (toks * picks) ** 0.5
 
     def swap(rows):
         return lax.ppermute(rows, "tensor", [(0, 1), (1, 0)])
 
-    base_a = jnp.stack([core * per_core, core]).astype(jnp.int32)
-    base_b = jnp.stack([core * per_core + per_a, core]).astype(jnp.int32)
-
-    packed_a, pos, gm = route_pack(base_a, expert_ids.T, gates.T, tokens, experts, per_a)
-    x_a = exchange(packed_a)
-    packed_b = pack(base_b, pos, tokens, per_b)
+    chunks = []
+    start = 0
+    for per in SLOTS:
+        size = per * per_core // sum(SLOTS)
+        chunks.append((jnp.stack([core * per_core + start, core]).astype(jnp.int32), size))
+        start += size
+    count = len(chunks)
+
+    base, per = chunks[0]
+    packed, pos, gm = route_pack(base, expert_ids.T, gates.T, tokens, experts, per)
+    arrived = exchange(packed)
+    later = [pack(base, pos, tokens, per) for base, per in chunks[1:]]
     mats = jnp.concatenate([w_gate[0], w_up[0], v_gate[0], v_up[0]], axis=1)
     down_own = jnp.concatenate([v_down[0], w_down[0]], axis=0)
-    x_a, packed_b, mats, down_own = lax.optimization_barrier((x_a, packed_b, mats, down_own))
-    x_b = exchange(packed_b)
+    matrices = [gate_matrix(base, pos, gm, per) for base, per in chunks]
+    arrived, later, mats, down_own, matrices, weight = lax.optimization_barrier(
+        (arrived, later, mats, down_own, matrices, token_weight[:, None])
+    )
     down_other = swap(down_own)
 
     def run_forward(x_own):
@@ -399,34 +489,46 @@
         part = part_rows(mine[0], swap(theirs[0]), down_own, down_other)
         return part, (x_own, *mine), (x_other, *theirs)
 
-    part_a, mine_a, theirs_a = run_forward(x_a)
-    x_b, part_a = lax.optimization_barrier((x_b, part_a))
-    ret_a = exchange(part_a)
-    part_b, mine_b, theirs_b = run_forward(x_b)
-    ret_a, part_b = lax.optimization_barrier((ret_a, part_b))
-    ret_b = exchange(part_b)
-    own = combine(base_a, pos, gm, ret_a, None, per_a)
-    ret_b, own = lax.optimization_barrier((ret_b, own))
-    own = combine(base_b, pos, gm, ret_b, own, per_b)
+    own, returned, sides = None, None, []
+    for n in range(count):
+        coming = exchange(later[n]) if n + 1 < count else returned
+        part, mine, theirs = run_forward(arrived)
+        sides.append((mine, theirs))
+        if coming is not None:
+            coming, part = lax.optimization_barrier((coming, part))
+        if n + 1 < count:
+            arrived = coming
+            returned = exchange(part)
+    if count > 1:
+        own = combine(matrices[0], returned, None)
+    last = exchange(part)
+    if count > 1:
+        last, own = lax.optimization_barrier((last, own))
+    own = combine(matrices[-1], last, own)
     other = swap(own)
-    weight = token_weight[:, None]
-    send_a, tangent = weigh_pack(base_a, pos, gm, weight, own, other, per_a, width // cores)
-    q_a = exchange(send_a)
-    (send_b,) = weigh_pack(base_b, pos, gm, weight, own, other, per_b, 0)
-    q_a, send_b = lax.optimization_barrier((q_a, send_b))
-    q_b = exchange(send_b)
+    order = sorted(range(count), key=lambda n: -chunks[n][1])
+
+    base, per = chunks[order[0]]
+    send, tangent = weigh_pack(base, pos, gm, weight, own, other, per, width // cores)
+    q = exchange(send)
+    if count > 1:
+        base, per = chunks[order[1]]
+        (send,) = weigh_pack(base, pos, gm, weight, own, other, per, 0)
+        q, send = lax.optimization_barrier((q, send))
+        q_next = exchange(send)
     down = w_down[0]
 
-    def run_backward(q_own, mine, theirs, start):
-        q_other = swap(q_own)
-        sides = []
-        for q, (x, ad, silu, us) in ((q_own, mine), (q_other, theirs)):
-            sides.append((q, x, gradients(q, silu, us, down), ad))
-        return outer_sums(*sides, start, factor, hidden)
-
-    sums = run_backward(q_a, mine_a, theirs_a, ())
-    q_b, sums = lax.optimization_barrier((q_b, sums))
-    gv_gate, gv_up, gv_down = run_backward(q_b, mine_b, theirs_b, sums)
+    mine, theirs = sides[order[0]]
+    sums = phased_sums((q, *mine), (swap(q), *theirs), down, factor)
+    if count > 1:
+        q_next, sums = lax.optimization_barrier((q_next, sums))
+        mine, theirs = sides[order[1]]
+        q_other = swap(q_next)
+        x, ad, silu, us = mine
+        own_side = (q_next, x, gradients(q_next, silu, us, down), ad)
+        x, ad, silu, us = theirs
+        sums = last_sums(own_side, (q_other, x, ad), silu, us, down, sums, factor)
+    gv_gate, gv_up, gv_down = sums
     return gv_gate, gv_up, gv_down, tangent
 
 

time: 371 us -> 361 us (0.973)
  Pallas kernels: 136 us -> 128 us
  local copies, waits for them, and re-layouts: 8.39 us -> 2.08 us
  starting transfers between devices: 75.6 us -> 81.7 us
  waiting for transfers between devices: 143 us -> 139 us
    pallas_call x4 -> x1, Pallas kernels: 22.3 us -> 4.21 us  [gradients(): pl.pallas_call(kernel, grid=(count // tile,), in_specs=[pl.BlockSpec((til...]
    pallas_call x4 -> x6, Pallas kernels: 40.6 us -> 49.9 us  [the longest x1 22.7 us: phased_sums(): pl.pallas_call(kernel, grid=(head + width // piece,), in_specs=specs(0) +...]
    all_to_all x6, waiting for transfers between devices: 137 us -> 129 us  [exchange(): return lax.all_to_all(rows, GROUP, split_axis=0, concat_axis=0, tiled=True)]
    ppermute x8, starting transfers between devices: 10.2 us -> 16.9 us  [swap(): return lax.ppermute(rows, 'tensor', [(0, 1), (1, 0)])]
    unnamed x26 -> x12, local copies, waits for them, and re-layouts: 7.64 us -> 1.35 us
    ppermute x8, waiting for transfers between devices: 5.76 us -> 10.4 us  [swap(): return lax.ppermute(rows, 'tensor', [(0, 1), (1, 0)])]
  transfers between devices with their start and end apart: 14 -> 14, of which waited for: 6 -> 7; matrix products, arithmetic and copies ran while one was open for 2% -> 2% of each run, Pallas kernels for 28% -> 28%
where the time goes in v3:
time: 361 us; the launch traced here: 360 us
  waiting for transfers between devices  139 us (39%)
  Pallas kernels  128 us (35%)
  starting transfers between devices  81.7 us (23%)
  other arithmetic  8.53 us (2%)
    all_to_all x6, waiting for transfers between devices, exchange(): return lax.all_to_all(rows, GROUP, split_axis=0, concat_axis=0, tiled=True)  129 us
    all_to_all x6, starting transfers between devices, exchange(): return lax.all_to_all(rows, GROUP, split_axis=0, concat_axis=0, tiled=True)  64.8 us
    pallas_call x4, Pallas kernels, forward(): pl.pallas_call(kernel, grid=(count // TILE,), in_specs=[pl.BlockSpec((TIL...  37.4 us
    pallas_call x1, Pallas kernels, phased_sums(): pl.pallas_call(kernel, grid=(head + width // piece,), in_specs=specs(0) +...  22.7 us
    pallas_call x2, Pallas kernels, part_rows(): pl.pallas_call(kernel, grid=(count // TILE,), in_specs=[pl.BlockSpec((TIL...  19 us
    ppermute x8, starting transfers between devices, swap(): return lax.ppermute(rows, 'tensor', [(0, 1), (1, 0)])  16.9 us
    pallas_call x1, Pallas kernels, last_sums(): pl.pallas_call(kernel, grid=(width // piece,), in_specs=[column, column,...  14.6 us
    ppermute x8, waiting for transfers between devices, swap(): return lax.ppermute(rows, 'tensor', [(0, 1), (1, 0)])  10.4 us
  transfers between devices with their start and end apart: 14, of which 7 were waited for; matrix products, arithmetic and copies ran while one was open for 2% of the time, Pallas kernels for 28%

profile of v3, /device:TPU:1, one launch (start us, length us, event | category | flops | bytes accessed | tf_op | source)
XLA Modules:
  0.0 360.1 jit_solution(1751047246863636242)
XLA Ops:
  0.6 0.6 pad_add_fusion.1.base_ref
  1.2 3.1 route_pack.1
  4.3 12.2 %all-to-all-start = ((bf16[64,8,2048]{2,1,0:T(8,128)(2,1)}), bf16[64,8,2048]{2,1,0:T(8,128)(2,1)}, u32[]{:S(2)}, u32[]{:S(2)}) async-start(bf16[64,8,2048]{2,1,0:T(8,128)(2,1)} %bitcast.33), calls=%async_computation | async-start | bytes 4194304 | tf_op jit(solution)/shard_map/all_to_all | solution.py:449
  16.6 0.6 pad_add_fusion.base_ref
  17.2 1.7 gate_matrix.2.matrix_ref
  18.9 3.1 gate_matrix.3.matrix_ref
  22.0 4.6 %pack.1 = bf16[1024,2048]{1,0:T(8,128)(2,1)} custom-call(s32[2]{0:T(128)} %pad_add_fusion.base_ref, f32[64,128]{1,0:T(8,128)} %get-tuple-element.45.pos_ref, bf16[128,2048]{1,0:T(8,128)(2,1)} %tok_ref.3), custom_call_target="tpu_custom_call" | custom-call | flops 33554432 | bytes 262144 | tf_op jit(solution)/shard_map/pack/pallas_call | solution.py:120
  26.6 0.0 copy-start
  26.6 0.0 copy-start.1
  26.6 0.0 copy-start.2
  26.6 0.0 copy-start.3
  26.6 4.1 %pad_maximum_fusion.1.wa_ref = bf16[768,2048]{1,0:T(8,128)(2,1)} fusion(bf16[384,2048]{1,0:T(8,128)(2,1)} %bitcast.24, bf16[384,2048]{1,0:T(8,128)(2,1)} %bitcast.38), kind=kLoop, calls=%fused_computation.1 | loop fusion | flops 6291456 | bytes 6291456 | tf_op jit(solution)/shard_map/concatenate | solution.py:478
  30.7 0.0 copy-done
  30.7 0.0 copy-done.1
  30.7 0.0 copy-done.2
  30.7 0.5 copy-done.3
  31.2 3.2 pad_maximum_fusion.w_ref
  34.4 9.4 %all-to-all-done = bf16[64,8,2048]{2,1,0:T(8,128)(2,1)} async-done(((bf16[64,8,2048]{2,1,0:T(8,128)(2,1)}), bf16[64,8,2048]{2,1,0:T(8,128)(2,1)}, u32[]{:S(2)}, u32[]{:S(2)}) %all-to-all-start) | async-done | bytes 2097184 | tf_op jit(solution)/shard_map/all_to_all | solution.py:449
  43.8 6.8 %all-to-all-start.1 = ((bf16[64,16,2048]{2,1,0:T(8,128)(2,1)}), bf16[64,16,2048]{2,1,0:T(8,128)(2,1)}, u32[]{:S(2)}, u32[]{:S(2)}) async-start(bf16[64,16,2048]{2,1,0:T(8,128)(2,1)} %bitcast.28), calls=%async_computation.1 | async-start | bytes 8388608 | tf_op jit(solution)/shard_map/all_to_all | solution.py:449
  50.6 2.1 collective-permute-start.2
  52.7 0.1 collective-permute-start
  52.8 8.5 %collective-permute-done.x_ref.refs_5_ = bf16[512,2048]{1,0:T(8,128)(2,1)} collective-permute-done((bf16[512,2048]{1,0:T(8,128)(2,1)}, bf16[512,2048]{1,0:T(8,128)(2,1)}, u32[]{:S(2)}, u32[]{:S(2)}) %collective-permute-start) | collective-permute-done | bytes 2097184 | tf_op jit(solution)/shard_map/ppermute | solution.py:463
  61.3 7.5 %forward.5 = (bf16[512,768]{1,0:T(8,128)(2,1)}, bf16[512,384]{1,0:T(8,128)(2,1)}, bf16[512,384]{1,0:T(8,128)(2,1)}) custom-call(bf16[512,2048]{1,0:T(8,128)(2,1)} %collective-permute-done.x_ref.refs_5_, bf16[2048,1536]{1,0:T(8,128)(2,1)} %pad_maximum_fusion.w_ref), custom_call_target="tpu_custom_call" | custom-call | flops 201326592 | bytes 278528 | tf_op jit(solution)/shard_map/forward/pallas_call | solution.py:149
  68.9 0.4 collective-permute-start.1
  69.2 7.5 %forward.4 = (bf16[512,768]{1,0:T(8,128)(2,1)}, bf16[512,384]{1,0:T(8,128)(2,1)}, bf16[512,384]{1,0:T(8,128)(2,1)}) custom-call(bf16[512,2048]{1,0:T(8,128)(2,1)} %bitcast.6.x_ref.refs_1_, bf16[2048,1536]{1,0:T(8,128)(2,1)} %pad_maximum_fusion.w_ref), custom_call_target="tpu_custom_call" | custom-call | flops 201326592 | bytes 278528 | tf_op jit(solution)/shard_map/forward/pallas_call | solution.py:149
  76.8 0.0 collective-permute-done.1.b_ref
  76.8 0.0 copy-start.4
  76.8 0.0 collective-permute-done.2.wb_ref
  76.8 0.9 copy-done.4
  77.7 7.7 %part_rows.2 = bf16[512,2048]{1,0:T(8,128)(2,1)} custom-call(bf16[512,768]{1,0:T(8,128)(2,1)} %get-tuple-element.53.a_ref.refs_3_, bf16[512,768]{1,0:T(8,128)(2,1)} %copy-done.4, bf16[768,2048]{1,0:T(8,128)(2,1)} %pad_maximum_fusion.1.wa_ref, bf16[768,2048]{1,0:T(8,128)(2,1)} %collective-permute-done.2.wb_ref), custom_call_target="tpu_custom_call" | custom-call | flops 201326592 | bytes 524288 | tf_op jit(solution)/shard_map/part_rows/pallas_call | solution.py:176
  85.3 13.4 %all-to-all-done.1 = bf16[64,16,2048]{2,1,0:T(8,128)(2,1)} async-done(((bf16[64,16,2048]{2,1,0:T(8,128)(2,1)}), bf16[64,16,2048]{2,1,0:T(8,128)(2,1)}, u32[]{:S(2)}, u32[]{:S(2)}) %all-to-all-start.1) | async-done | bytes 4194336 | tf_op jit(solution)/shard_map/all_to_all | solution.py:449
  98.7 7.1 %collective-permute-start.3 = (bf16[1024,2048]{1,0:T(8,128)(2,1)}, bf16[1024,2048]{1,0:T(8,128)(2,1)}, u32[]{:S(2)}, u32[]{:S(2)}) collective-permute-start(bf16[1024,2048]{1,0:T(8,128)(2,1)} %bitcast.15.x_ref.refs_1_), channel_id=1, source_target_pairs={{0,1},{1,0},{2,3},{3,2},{4,5},{5,4},{6,7},{7,6},{8,9},{9,8},{10,11... | collective-permute-start | bytes 12582920 | tf_op jit(solution)/shard_map/ppermute | solution.py:463
  105.9 12.1 %all-to-all-start.2 = ((bf16[64,8,2048]{2,1,0:T(8,128)(2,1)}), bf16[64,8,2048]{2,1,0:T(8,128)(2,1)}, u32[]{:S(2)}, u32[]{:S(2)}) async-start(bf16[64,8,2048]{2,1,0:T(8,128)(2,1)} %bitcast.30), calls=%async_computation.2 | async-start | bytes 4194304 | tf_op jit(solution)/shard_map/all_to_all | solution.py:449
  117.9 0.0 collective-permute-done.3.x_ref.refs_6_
  117.9 11.2 %forward.7 = (bf16[1024,768]{1,0:T(8,128)(2,1)}, bf16[1024,384]{1,0:T(8,128)(2,1)}, bf16[1024,384]{1,0:T(8,128)(2,1)}) custom-call(bf16[1024,2048]{1,0:T(8,128)(2,1)} %collective-permute-done.3.x_ref.refs_6_, bf16[2048,1536]{1,0:T(8,128)(2,1)} %pad_maximum_fusion.w_ref), custom_call_target="tpu_custom_call" | custom-call | flops 402653184 | bytes 557056 | tf_op jit(solution)/shard_map/forward/pallas_call | solution.py:149
  129.2 0.3 collective-permute-start.4
  129.4 11.2 %forward.6 = (bf16[1024,768]{1,0:T(8,128)(2,1)}, bf16[1024,384]{1,0:T(8,128)(2,1)}, bf16[1024,384]{1,0:T(8,128)(2,1)}) custom-call(bf16[1024,2048]{1,0:T(8,128)(2,1)} %bitcast.15.x_ref.refs_1_, bf16[2048,1536]{1,0:T(8,128)(2,1)} %pad_maximum_fusion.w_ref), custom_call_target="tpu_custom_call" | custom-call | flops 402653184 | bytes 557056 | tf_op jit(solution)/shard_map/forward/pallas_call | solution.py:149
  140.6 0.0 collective-permute-done.4.b_ref
  140.6 11.3 %part_rows.3 = bf16[1024,2048]{1,0:T(8,128)(2,1)} custom-call(bf16[1024,768]{1,0:T(8,128)(2,1)} %get-tuple-element.58.a_ref.refs_2_, bf16[1024,768]{1,0:T(8,128)(2,1)} %collective-permute-done.4.b_ref, bf16[768,2048]{1,0:T(8,128)(2,1)} %pad_maximum_fusion.1.wa_ref, bf16[768,2048]{1,0:T(8,128)(2,1)} %collective-permute-done.2.wb_ref), custom_call_target="tpu_custom_call" | custom-call | flops 402653184 | bytes 655360 | tf_op jit(solution)/shard_map/part_rows/pallas_call | solution.py:176
  152.0 0.0 all-to-all-done.2
  152.0 10.2 %all-to-all-start.3 = ((bf16[64,16,2048]{2,1,0:T(8,128)(2,1)}), bf16[64,16,2048]{2,1,0:T(8,128)(2,1)}, u32[]{:S(2)}, u32[]{:S(2)}) async-start(bf16[64,16,2048]{2,1,0:T(8,128)(2,1)} %bitcast.29), calls=%async_computation.3 | async-start | bytes 8388608 | tf_op jit(solution)/shard_map/all_to_all | solution.py:449
  162.2 3.0 combine.2.rest_0_
  165.2 52.0 %all-to-all-done.3 = bf16[64,16,2048]{2,1,0:T(8,128)(2,1)} async-done(((bf16[64,16,2048]{2,1,0:T(8,128)(2,1)}), bf16[64,16,2048]{2,1,0:T(8,128)(2,1)}, u32[]{:S(2)}, u32[]{:S(2)}) %all-to-all-start.3) | async-done | bytes 4194336 | tf_op jit(solution)/shard_map/all_to_all | solution.py:449
  217.2 0.0 copy-start.5
  217.2 4.7 %combine.3.own_ref = f32[128,2048]{1,0:T(8,128)} custom-call(bf16[256,1024]{1,0:T(8,128)(2,1)} %gate_matrix.3.matrix_ref, bf16[1024,2048]{1,0:T(8,128)(2,1)} %bitcast.19.rows_ref, f32[128,2048]{1,0:T(8,128)} %combine.2.rest_0_), custom_call_target="tpu_custom_call" | custom-call | flops 67108864 | bytes 262144 | tf_op jit(solution)/shard_map/combine/pallas_call | solution.py:232
  221.9 1.9 collective-permute-start.5
  223.8 0.0 copy-done.5
  223.8 0.7 copy.14.tw_ref
  224.6 1.9 collective-permute-done.5.other_ref
  226.5 5.6 %weigh_pack.2 = (bf16[1024,2048]{1,0:T(8,128)(2,1)}, bf16[128,1024]{1,0:T(8,128)(2,1)}) custom-call(s32[2]{0:T(128)} %pad_add_fusion.base_ref, f32[64,128]{1,0:T(8,128)} %get-tuple-element.45.pos_ref, f32[64,128]{1,0:T(8,128)} %get-tuple-element.46.gm_ref, f32[128,1]{1,0:T(8,128)} %copy.14.tw_ref, f32[128,2048]{1,0:T(8,128)} %combine.3.own_ref, ...), custom_call_target="tpu_custom_call" | custom-call | flops 100663296 | bytes 262144 | tf_op jit(solution)/shard_map/weigh_pack/pallas_call | solution.py:274
  232.1 9.8 %all-to-all-start.4 = ((bf16[64,16,2048]{2,1,0:T(8,128)(2,1)}), bf16[64,16,2048]{2,1,0:T(8,128)(2,1)}, u32[]{:S(2)}, u32[]{:S(2)}) async-start(bf16[64,16,2048]{2,1,0:T(8,128)(2,1)} %bitcast.32), calls=%async_computation.4 | async-start | bytes 8388608 | tf_op jit(solution)/shard_map/all_to_all | solution.py:449
  241.9 3.9 %weigh_pack.3 = bf16[512,2048]{1,0:T(8,128)(2,1)} custom-call(s32[2]{0:T(128)} %pad_add_fusion.1.base_ref, f32[64,128]{1,0:T(8,128)} %get-tuple-element.45.pos_ref, f32[64,128]{1,0:T(8,128)} %get-tuple-element.46.gm_ref, f32[128,1]{1,0:T(8,128)} %copy.14.tw_ref, f32[128,2048]{1,0:T(8,128)} %combine.3.own_ref, f32[128,2048]{1,0:T(8,128)} %collective-permute-done.5.other_ref), custom_call_target="tpu_custom_call" | custom-call | flops 50331648 | bytes 131072 | tf_op jit(solution)/shard_map/weigh_pack/pallas_call | solution.py:274
  245.9 48.1 %all-to-all-done.4 = bf16[64,16,2048]{2,1,0:T(8,128)(2,1)} async-done(((bf16[64,16,2048]{2,1,0:T(8,128)(2,1)}), bf16[64,16,2048]{2,1,0:T(8,128)(2,1)}, u32[]{:S(2)}, u32[]{:S(2)}) %all-to-all-start.4) | async-done | bytes 4194336 | tf_op jit(solution)/shard_map/all_to_all | solution.py:449
  294.0 3.4 collective-permute-start.6
  297.4 13.7 %all-to-all-start.5 = ((bf16[64,8,2048]{2,1,0:T(8,128)(2,1)}), bf16[64,8,2048]{2,1,0:T(8,128)(2,1)}, u32[]{:S(2)}, u32[]{:S(2)}) async-start(bf16[64,8,2048]{2,1,0:T(8,128)(2,1)} %bitcast.31), calls=%async_computation.5 | async-start | bytes 4194304 | tf_op jit(solution)/shard_map/all_to_all | solution.py:449
  311.1 0.0 collective-permute-done.6.refs_5_
  311.1 22.7 %phased_sums.1 = (f32[1,2048,384]{2,1,0:T(8,128)}, f32[1,2048,384]{2,1,0:T(8,128)}, f32[1,384,2048]{2,1,0:T(8,128)}) custom-call(bf16[1024,2048]{1,0:T(8,128)(2,1)} %bitcast.21.refs_0_, bf16[1024,2048]{1,0:T(8,128)(2,1)} %bitcast.15.x_ref.refs_1_, bf16[1024,768]{1,0:T(8,128)(2,1)} %get-tuple-element.58.a_ref.refs_2_, ...), custom_call_target="tpu_custom_call" | custom-call | flops 805306368 | bytes 1048576 | tf_op jit(solution)/shard_map/phased_sums/pallas_call | solution.py:374
  333.9 5.7 %all-to-all-done.5 = bf16[64,8,2048]{2,1,0:T(8,128)(2,1)} async-done(((bf16[64,8,2048]{2,1,0:T(8,128)(2,1)}), bf16[64,8,2048]{2,1,0:T(8,128)(2,1)}, u32[]{:S(2)}, u32[]{:S(2)}) %all-to-all-start.5) | async-done | bytes 2097184 | tf_op jit(solution)/shard_map/all_to_all | solution.py:449
  339.6 1.6 collective-permute-start.7
  341.1 4.2 %gradients.1.refs_2_ = bf16[512,768]{1,0:T(8,128)(2,1)} custom-call(bf16[512,2048]{1,0:T(8,128)(2,1)} %bitcast.23.q_ref.refs_0_, bf16[512,384]{1,0:T(8,128)(2,1)} %get-tuple-element.75.silu_ref, bf16[512,384]{1,0:T(8,128)(2,1)} %get-tuple-element.76.us_ref, bf16[384,2048]{1,0:T(8,128)(2,1)} %bitcast.26), custom_call_target="tpu_custom_call" | custom-call | flops 50331648 | bytes 131072 | tf_op jit(solution)/shard_map/gradients/pallas_call | solution.py:304
  345.3 0.0 collective-permute-done.7.refs_4_
  345.3 14.6 %last_sums.1 = (f32[1,2048,384]{2,1,0:T(8,128)}, f32[1,2048,384]{2,1,0:T(8,128)}, f32[1,384,2048]{2,1,0:T(8,128)}) custom-call(bf16[512,2048]{1,0:T(8,128)(2,1)} %bitcast.23.q_ref.refs_0_, bf16[512,2048]{1,0:T(8,128)(2,1)} %bitcast.6.x_ref.refs_1_, bf16[512,768]{1,0:T(8,128)(2,1)} %gradients.1.refs_2_, bf16[512,768]{1,0:T(8,128)(2,1)} %get-tuple-element.53.a_ref.refs_3_, ...), custom_call_target="tpu_custom_call" | custom-call | flops 352321536 | bytes 524288 | tf_op jit(solution)/shard_map/last_sums/pallas_call | solution.py:429
Async XLA Ops:
  4.3 39.4 %all-to-all-start = ((bf16[64,8,2048]{2,1,0:T(8,128)(2,1)}), bf16[64,8,2048]{2,1,0:T(8,128)(2,1)}, u32[]{:S(2)}, u32[]{:S(2)}) async-start(bf16[64,8,2048]{2,1,0:T(8,128)(2,1)} %bitcast.33), calls=%async_computation | async-start | bytes 4194304 | tf_op jit(solution)/shard_map/all_to_all | solution.py:449
  26.6 4.1 %copy-start = (bf16[1,2048,384]{2,1,0:T(8,128)(2,1)S(1)}, bf16[1,2048,384]{2,1,0:T(8,128)(2,1)}, u32[]{:S(2)}) copy-start(bf16[1,2048,384]{2,1,0:T(8,128)(2,1)} %param.18) | copy-start | bytes 4718596
  26.6 4.1 %copy-start.1 = (bf16[1,2048,384]{2,1,0:T(8,128)(2,1)S(1)}, bf16[1,2048,384]{2,1,0:T(8,128)(2,1)}, u32[]{:S(2)}) copy-start(bf16[1,2048,384]{2,1,0:T(8,128)(2,1)} %param.17) | copy-start | bytes 4718596
  26.6 4.1 %copy-start.2 = (bf16[1,2048,384]{2,1,0:T(8,128)(2,1)S(1)}, bf16[1,2048,384]{2,1,0:T(8,128)(2,1)}, u32[]{:S(2)}) copy-start(bf16[1,2048,384]{2,1,0:T(8,128)(2,1)} %param.15) | copy-start | bytes 4718596
  26.6 4.6 %copy-start.3 = (bf16[1,2048,384]{2,1,0:T(8,128)(2,1)S(1)}, bf16[1,2048,384]{2,1,0:T(8,128)(2,1)}, u32[]{:S(2)}) copy-start(bf16[1,2048,384]{2,1,0:T(8,128)(2,1)} %param.14) | copy-start | bytes 4718596
  43.8 55.0 %all-to-all-start.1 = ((bf16[64,16,2048]{2,1,0:T(8,128)(2,1)}), bf16[64,16,2048]{2,1,0:T(8,128)(2,1)}, u32[]{:S(2)}, u32[]{:S(2)}) async-start(bf16[64,16,2048]{2,1,0:T(8,128)(2,1)} %bitcast.28), calls=%async_computation.1 | async-start | bytes 8388608 | tf_op jit(solution)/shard_map/all_to_all | solution.py:449
  50.6 26.2 %collective-permute-start.2 = (bf16[768,2048]{1,0:T(8,128)(2,1)}, bf16[768,2048]{1,0:T(8,128)(2,1)}, u32[]{:S(2)}, u32[]{:S(2)}) collective-permute-start(bf16[768,2048]{1,0:T(8,128)(2,1)} %pad_maximum_fusion.1.wa_ref), channel_id=1, source_target_pairs={{0,1},{1,0},{2,3},{3,2},{4,5},{5,4},{6,7},{7,6},{8,9},{9,8},{10,11... | collective-permute-start | bytes 9437192 | tf_op jit(solution)/shard_map/ppermute | solution.py:463
  52.7 8.6 %collective-permute-start = (bf16[512,2048]{1,0:T(8,128)(2,1)}, bf16[512,2048]{1,0:T(8,128)(2,1)}, u32[]{:S(2)}, u32[]{:S(2)}) collective-permute-start(bf16[512,2048]{1,0:T(8,128)(2,1)} %bitcast.6.x_ref.refs_1_), channel_id=1, source_target_pairs={{0,1},{1,0},{2,3},{3,2},{4,5},{5,4},{6,7},{7,6},{8,9},{9,8},{10,11... | collective-permute-start | bytes 6291464 | tf_op jit(solution)/shard_map/ppermute | solution.py:463
  68.9 7.9 %collective-permute-start.1 = (bf16[512,768]{1,0:T(8,128)(2,1)}, bf16[512,768]{1,0:T(8,128)(2,1)S(1)}, u32[]{:S(2)}, u32[]{:S(2)}) collective-permute-start(bf16[512,768]{1,0:T(8,128)(2,1)} %get-tuple-element.54.refs_6_), channel_id=1, source_target_pairs={{0,1},{1,0},{2,3},{3,2},{4,5},{5,4},{6,7},{7,6},{8,9},{9,8},{10,11... | collective-permute-start | bytes 2359304 | tf_op jit(solution)/shard_map/ppermute | solution.py:463
  76.8 0.9 copy-start.4
  98.7 19.2 %collective-permute-start.3 = (bf16[1024,2048]{1,0:T(8,128)(2,1)}, bf16[1024,2048]{1,0:T(8,128)(2,1)}, u32[]{:S(2)}, u32[]{:S(2)}) collective-permute-start(bf16[1024,2048]{1,0:T(8,128)(2,1)} %bitcast.15.x_ref.refs_1_), channel_id=1, source_target_pairs={{0,1},{1,0},{2,3},{3,2},{4,5},{5,4},{6,7},{7,6},{8,9},{9,8},{10,11... | collective-permute-start | bytes 12582920 | tf_op jit(solution)/shard_map/ppermute | solution.py:463
  105.9 46.1 %all-to-all-start.2 = ((bf16[64,8,2048]{2,1,0:T(8,128)(2,1)}), bf16[64,8,2048]{2,1,0:T(8,128)(2,1)}, u32[]{:S(2)}, u32[]{:S(2)}) async-start(bf16[64,8,2048]{2,1,0:T(8,128)(2,1)} %bitcast.30), calls=%async_computation.2 | async-start | bytes 4194304 | tf_op jit(solution)/shard_map/all_to_all | solution.py:449
  129.2 11.5 %collective-permute-start.4 = (bf16[1024,768]{1,0:T(8,128)(2,1)}, bf16[1024,768]{1,0:T(8,128)(2,1)}, u32[]{:S(2)}, u32[]{:S(2)}) collective-permute-start(bf16[1024,768]{1,0:T(8,128)(2,1)} %get-tuple-element.59.refs_7_), channel_id=1, source_target_pairs={{0,1},{1,0},{2,3},{3,2},{4,5},{5,4},{6,7},{7,6},{8,9},{9,8},{10,11... | collective-permute-start | bytes 4718600 | tf_op jit(solution)/shard_map/ppermute | solution.py:463
  152.0 65.3 %all-to-all-start.3 = ((bf16[64,16,2048]{2,1,0:T(8,128)(2,1)}), bf16[64,16,2048]{2,1,0:T(8,128)(2,1)}, u32[]{:S(2)}, u32[]{:S(2)}) async-start(bf16[64,16,2048]{2,1,0:T(8,128)(2,1)} %bitcast.29), calls=%async_computation.3 | async-start | bytes 8388608 | tf_op jit(solution)/shard_map/all_to_all | solution.py:449
  217.2 6.6 %copy-start.5 = (f32[128]{0:T(128)S(1)}, f32[128]{0:T(128)}, u32[]{:S(2)}) copy-start(f32[128]{0:T(128)} %param.13) | copy-start | bytes 1540
  221.9 4.5 %collective-permute-start.5 = (f32[128,2048]{1,0:T(8,128)}, f32[128,2048]{1,0:T(8,128)}, u32[]{:S(2)}, u32[]{:S(2)}) collective-permute-start(f32[128,2048]{1,0:T(8,128)} %combine.3.own_ref), channel_id=1, source_target_pairs={{0,1},{1,0},{2,3},{3,2},{4,5},{5,4},{6,7},{7,6},{8,9},{9,8},{10,11... | collective-permute-start | bytes 3145736 | tf_op jit(solution)/shard_map/ppermute | solution.py:463
  232.1 61.9 %all-to-all-start.4 = ((bf16[64,16,2048]{2,1,0:T(8,128)(2,1)}), bf16[64,16,2048]{2,1,0:T(8,128)(2,1)}, u32[]{:S(2)}, u32[]{:S(2)}) async-start(bf16[64,16,2048]{2,1,0:T(8,128)(2,1)} %bitcast.32), calls=%async_computation.4 | async-start | bytes 8388608 | tf_op jit(solution)/shard_map/all_to_all | solution.py:449
  294.0 17.1 %collective-permute-start.6 = (bf16[1024,2048]{1,0:T(8,128)(2,1)}, bf16[1024,2048]{1,0:T(8,128)(2,1)}, u32[]{:S(2)}, u32[]{:S(2)}) collective-permute-start(bf16[1024,2048]{1,0:T(8,128)(2,1)} %bitcast.21.refs_0_), channel_id=1, source_target_pairs={{0,1},{1,0},{2,3},{3,2},{4,5},{5,4},{6,7},{7,6},{8,9},{9,8},{10,11... | collective-permute-start | bytes 12582920 | tf_op jit(solution)/shard_map/ppermute | solution.py:463
  297.4 42.1 %all-to-all-start.5 = ((bf16[64,8,2048]{2,1,0:T(8,128)(2,1)}), bf16[64,8,2048]{2,1,0:T(8,128)(2,1)}, u32[]{:S(2)}, u32[]{:S(2)}) async-start(bf16[64,8,2048]{2,1,0:T(8,128)(2,1)} %bitcast.31), calls=%async_computation.5 | async-start | bytes 4194304 | tf_op jit(solution)/shard_map/all_to_all | solution.py:449
  339.6 5.8 %collective-permute-start.7 = (bf16[512,2048]{1,0:T(8,128)(2,1)}, bf16[512,2048]{1,0:T(8,128)(2,1)}, u32[]{:S(2)}, u32[]{:S(2)}) collective-permute-start(bf16[512,2048]{1,0:T(8,128)(2,1)} %bitcast.23.q_ref.refs_0_), channel_id=1, source_target_pairs={{0,1},{1,0},{2,3},{3,2},{4,5},{5,4},{6,7},{7,6},{8,9},{9,8},{10,11... | collective-permute-start | bytes 6291464 | tf_op jit(solution)/shard_map/ppermute | solution.py:463

commit v4 on v3

--- a/solution.py
+++ b/solution.py
@@ -11,9 +11,11 @@
 VMEM_LIMIT = 63 * 1024 * 1024
 TILE = 256
 PIECE = 512
-LAST_PIECE = 512
+LAST_PIECE = 1024
 ROWS = 512
 SLOTS = (1, 2)
+COMBINE = 1024
+WEIGH = 512
 
 
 def params():
@@ -217,78 +219,94 @@
     )(base, pos, gm)
 
 
-def combine(matrix, rows, start):
-    count, width = rows.shape
-    toks = matrix.shape[0] // 2
-    piece = 1024
-
-    def kernel(matrix_ref, rows_ref, *rest):
-        both = mm(matrix_ref[...], rows_ref[...])
-        total = both[:toks] + both[toks:]
-        rest[-1][...] = total if start is None else total + rest[0][...]
-
-    extra = [] if start is None else [start]
-    column = pl.BlockSpec((toks, piece), lambda i: (0, i))
-    return pl.pallas_call(
-        kernel,
-        grid=(width // piece,),
-        in_specs=[fixed((2 * toks, count)), pl.BlockSpec((count, piece), lambda i: (0, i))]
-        + [column for _ in extra],
-        out_specs=column,
+def combine(pairs):
+    width = pairs[0][1].shape[1]
+    toks = pairs[0][0].shape[0] // 2
+
+    def kernel(*refs):
+        both = None
+        for n in range(0, len(refs) - 1, 2):
+            term = mm(refs[n][...], refs[n + 1][...])
+            both = term if both is None else both + term
+        refs[-1][...] = both[:toks] + both[toks:]
+
+    in_specs = []
+    for matrix, rows in pairs:
+        in_specs += [
+            fixed(matrix.shape),
+            pl.BlockSpec((rows.shape[0], COMBINE), lambda i: (0, i)),
+        ]
+    count = sum(rows.shape[0] for _, rows in pairs)
+    return pl.pallas_call(
+        kernel,
+        grid=(width // COMBINE,),
+        in_specs=in_specs,
+        out_specs=pl.BlockSpec((toks, COMBINE), lambda i: (0, i)),
         out_shape=jax.ShapeDtypeStruct((toks, width), F32),
         compiler_params=params(),
         cost_estimate=cost(4 * count * toks * width, 2 * count * width),
         name="combine",
-    )(matrix, rows, *extra)
-
-
-def weigh_pack(base, pos, gm, weight, own, other, per, half):
+    )(*[array for pair in pairs for array in pair])
+
+
+def weigh_pack(bases, pers, pos, gm, weight, own, other, half):
     experts, toks = pos.shape
     width = own.shape[1]
-    step = TILE // per
-
-    def kernel(base_ref, pos_ref, gm_ref, tw_ref, own_ref, other_ref, q_ref, *rest):
-        split_ref = rest[-1]
-
-        @pl.when(pl.program_id(0) == 0)
+    chunks = len(pers)
+    tile = WEIGH
+    counts = [experts * per // tile for per in pers]
+    firsts = [sum(counts[:n]) for n in range(chunks)]
+
+    def kernel(*refs):
+        base_refs = refs[:chunks]
+        blocks = refs[chunks : 3 * chunks]
+        tw_ref, own_ref, other_ref = refs[3 * chunks : 3 * chunks + 3]
+        outs = refs[3 * chunks + 3 : -2]
+        tangent_ref, split_ref = refs[-2:]
+        i = pl.program_id(0)
+
+        @pl.when(i == 0)
         def _():
-            if half:
-                cols = pl.ds(pl.multiple_of(base_ref[1] * half, half), half)
-                rest[0][...] = (own_ref[:, cols] + other_ref[:, cols]).astype(BF)
-            scaled = tw_ref[...] * (own_ref[...] + other_ref[...])
+            cols = pl.ds(pl.multiple_of(base_refs[0][1] * half, half), half)
+            tangent_ref[...] = (own_ref[:, cols] + other_ref[:, cols]).astype(BF)
+            scale = jnp.broadcast_to(tw_ref[...], (toks, toks)).T[:, :1]
+            scaled = scale * (own_ref[...] + other_ref[...])
             high = scaled.astype(BF)
             split_ref[:toks, :] = high
             split_ref[toks:, :] = (scaled - high.astype(F32)).astype(BF)
 
-        match = slot_match(pos_ref[...], base_ref[0], per)
-        hot = jnp.where(match, 1.0, 0.0).astype(BF)
-        gate = jnp.sum(jnp.where(match, spread(gm_ref[...], per), 0.0), axis=1, keepdims=True)
-        row = mm(jnp.concatenate([hot, hot], axis=1), split_ref[...])
-        q_ref[...] = (gate * row).astype(BF)
-
-    out_specs = [pl.BlockSpec((TILE, width), lambda i: (i, 0))]
-    out_shape = [jax.ShapeDtypeStruct((experts * per, width), BF)]
-    if half:
-        out_specs.append(pl.BlockSpec((toks, half), lambda i: (0, 0)))
-        out_shape.append(jax.ShapeDtypeStruct((toks, half), BF))
-    return pl.pallas_call(
-        kernel,
-        grid=(experts // step,),
-        in_specs=[
-            smem(),
-            pl.BlockSpec((step, toks), lambda i: (i, 0)),
-            pl.BlockSpec((step, toks), lambda i: (i, 0)),
-            fixed((toks, 1)),
-            fixed((toks, width)),
-            fixed((toks, width)),
-        ],
-        out_specs=out_specs,
-        out_shape=out_shape,
+        for n in range(chunks):
+
+            @pl.when((i >= firsts[n]) & (i < firsts[n] + counts[n]))
+            def _(n=n):
+                match = slot_match(blocks[2 * n][...], base_refs[n][0], pers[n])
+                hot = jnp.where(match, 1.0, 0.0).astype(BF)
+                gates = spread(blocks[2 * n + 1][...], pers[n])
+                gate = jnp.sum(jnp.where(match, gates, 0.0), axis=1, keepdims=True)
+                row = mm(jnp.concatenate([hot, hot], axis=1), split_ref[...])
+                outs[n][...] = (gate * row).astype(BF)
+
+    def at(n):
+        return lambda i: (jnp.clip(i - firsts[n], 0, counts[n] - 1), 0)
+
+    pos_specs = []
+    for n, per in enumerate(pers):
+        pos_specs += [pl.BlockSpec((tile // per, toks), at(n))] * 2
+    return pl.pallas_call(
+        kernel,
+        grid=(sum(counts),),
+        in_specs=[smem() for _ in bases]
+        + pos_specs
+        + [fixed((1, toks)), fixed((toks, width)), fixed((toks, width))],
+        out_specs=[pl.BlockSpec((tile, width), at(n)) for n in range(chunks)]
+        + [pl.BlockSpec((toks, half), lambda i: (0, 0))],
+        out_shape=[jax.ShapeDtypeStruct((experts * per, width), BF) for per in pers]
+        + [jax.ShapeDtypeStruct((toks, half), BF)],
         scratch_shapes=[pltpu.VMEM((2 * toks, width), BF)],
         compiler_params=params(),
-        cost_estimate=cost(6 * experts * per * toks * width, 2 * experts * per * width),
+        cost_estimate=cost(4 * experts * sum(pers) * toks * width, 2 * experts * sum(pers) * width),
         name="weigh_pack",
-    )(base, pos, gm, weight, own, other)
+    )(*bases, *[array for _ in pers for array in (pos, gm)], weight, own, other)
 
 
 def gradients(q, silu, us, down):
@@ -468,7 +486,6 @@
         size = per * per_core // sum(SLOTS)
         chunks.append((jnp.stack([core * per_core + start, core]).astype(jnp.int32), size))
         start += size
-    count = len(chunks)
 
     base, per = chunks[0]
     packed, pos, gm = route_pack(base, expert_ids.T, gates.T, tokens, experts, per)
@@ -477,9 +494,10 @@
     mats = jnp.concatenate([w_gate[0], w_up[0], v_gate[0], v_up[0]], axis=1)
     down_own = jnp.concatenate([v_down[0], w_down[0]], axis=0)
     matrices = [gate_matrix(base, pos, gm, per) for base, per in chunks]
-    arrived, later, mats, down_own, matrices, weight = lax.optimization_barrier(
-        (arrived, later, mats, down_own, matrices, token_weight[:, None])
+    arrived, later, mats, down_own, matrices = lax.optimization_barrier(
+        (arrived, later, mats, down_own, matrices)
     )
+    weight = token_weight[None, :]
     down_other = swap(down_own)
 
     def run_forward(x_own):
@@ -489,46 +507,39 @@
         part = part_rows(mine[0], swap(theirs[0]), down_own, down_other)
         return part, (x_own, *mine), (x_other, *theirs)
 
-    own, returned, sides = None, None, []
-    for n in range(count):
-        coming = exchange(later[n]) if n + 1 < count else returned
-        part, mine, theirs = run_forward(arrived)
-        sides.append((mine, theirs))
-        if coming is not None:
-            coming, part = lax.optimization_barrier((coming, part))
-        if n + 1 < count:
-            arrived = coming
-            returned = exchange(part)
-    if count > 1:
-        own = combine(matrices[0], returned, None)
+    sides = []
+    x_large = exchange(later[0])
+    part, mine, theirs = run_forward(arrived)
+    sides.append((mine, theirs))
+    x_large, part = lax.optimization_barrier((x_large, part))
+    returned = exchange(part)
+    part, mine, theirs = run_forward(x_large)
+    sides.append((mine, theirs))
+    returned, part = lax.optimization_barrier((returned, part))
     last = exchange(part)
-    if count > 1:
-        last, own = lax.optimization_barrier((last, own))
-    own = combine(matrices[-1], last, own)
+    last, returned = lax.optimization_barrier((last, returned))
+    own = combine(list(zip(matrices, (returned, last))))
     other = swap(own)
-    order = sorted(range(count), key=lambda n: -chunks[n][1])
-
-    base, per = chunks[order[0]]
-    send, tangent = weigh_pack(base, pos, gm, weight, own, other, per, width // cores)
-    q = exchange(send)
-    if count > 1:
-        base, per = chunks[order[1]]
-        (send,) = weigh_pack(base, pos, gm, weight, own, other, per, 0)
-        q, send = lax.optimization_barrier((q, send))
-        q_next = exchange(send)
+
+    order = (1, 0)
+    bases, pers = zip(*[chunks[n] for n in order])
+    send_large, send_small, tangent = weigh_pack(
+        bases, pers, pos, gm, weight, own, other, width // cores
+    )
+    q_large = exchange(send_large)
+    q_large, send_small = lax.optimization_barrier((q_large, send_small))
+    q_small = exchange(send_small)
     down = w_down[0]
-
-    mine, theirs = sides[order[0]]
-    sums = phased_sums((q, *mine), (swap(q), *theirs), down, factor)
-    if count > 1:
-        q_next, sums = lax.optimization_barrier((q_next, sums))
-        mine, theirs = sides[order[1]]
-        q_other = swap(q_next)
-        x, ad, silu, us = mine
-        own_side = (q_next, x, gradients(q_next, silu, us, down), ad)
-        x, ad, silu, us = theirs
-        sums = last_sums(own_side, (q_other, x, ad), silu, us, down, sums, factor)
-    gv_gate, gv_up, gv_down = sums
+    mine, theirs = sides[1]
+    sums = phased_sums((q_large, *mine), (swap(q_large), *theirs), down, factor)
+    q_small, sums = lax.optimization_barrier((q_small, sums))
+    q_other = swap(q_small)
+    x, ad, silu, us = sides[0][0]
+    own_side = (q_small, x, gradients(q_small, silu, us, down), ad)
+    x, ad, silu, us = sides[0][1]
+    gv_gate, gv_up, gv_down = last_sums(
+        own_side, (q_other, x, ad), silu, us, down, sums, factor
+    )
     return gv_gate, gv_up, gv_down, tangent
 
 

time: 361 us -> 350 us (0.970)
  blocking collectives: 0 us -> 120 us
  waiting for transfers between devices: 139 us -> 39.8 us
  starting transfers between devices: 81.7 us -> 56.4 us
  Pallas kernels: 128 us -> 122 us
    all_to_all x0 -> x2, blocking collectives: none -> 120 us  [exchange(): return lax.all_to_all(rows, GROUP, split_axis=0, concat_axis=0, tiled=True)]
    all_to_all x6 -> x4, waiting for transfers between devices: 129 us -> 28.6 us  [exchange(): return lax.all_to_all(rows, GROUP, split_axis=0, concat_axis=0, tiled=True)]
    all_to_all x6 -> x4, starting transfers between devices: 64.8 us -> 39.8 us  [exchange(): return lax.all_to_all(rows, GROUP, split_axis=0, concat_axis=0, tiled=True)]
    pallas_call x4 -> x2, Pallas kernels: 17.2 us -> 11.8 us  [the longest x1 6.95 us: weigh_pack(): pl.pallas_call(kernel, grid=(sum(counts),), in_specs=[smem() for _ in bas...]
  transfers between devices with their start and end apart: 14 -> 12, of which waited for: 7 -> 5; matrix products, arithmetic and copies ran while one was open for 2% -> 2% of each run, Pallas kernels for 28% -> 27%
where the time goes in v4:
time: 350 us; the launch traced here: 349 us
  Pallas kernels  122 us (35%)
  blocking collectives  120 us (34%)
  starting transfers between devices  56.4 us (16%)
  waiting for transfers between devices  39.8 us (11%)
  other arithmetic  8.5 us (2%)
    all_to_all x2, blocking collectives, exchange(): return lax.all_to_all(rows, GROUP, split_axis=0, concat_axis=0, tiled=True)  120 us
    all_to_all x4, starting transfers between devices, exchange(): return lax.all_to_all(rows, GROUP, split_axis=0, concat_axis=0, tiled=True)  39.8 us
    pallas_call x4, Pallas kernels, forward(): pl.pallas_call(kernel, grid=(count // TILE,), in_specs=[pl.BlockSpec((TIL...  37.4 us
    all_to_all x4, waiting for transfers between devices, exchange(): return lax.all_to_all(rows, GROUP, split_axis=0, concat_axis=0, tiled=True)  28.6 us
    pallas_call x1, Pallas kernels, phased_sums(): pl.pallas_call(kernel, grid=(head + width // piece,), in_specs=specs(0) +...  22.8 us
    pallas_call x2, Pallas kernels, part_rows(): pl.pallas_call(kernel, grid=(count // TILE,), in_specs=[pl.BlockSpec((TIL...  19 us
    ppermute x8, starting transfers between devices, swap(): return lax.ppermute(rows, 'tensor', [(0, 1), (1, 0)])  16.5 us
    pallas_call x1, Pallas kernels, last_sums(): pl.pallas_call(kernel, grid=(width // piece,), in_specs=[column, column,...  14.4 us
  transfers between devices with their start and end apart: 12, of which 5 were waited for; matrix products, arithmetic and copies ran while one was open for 2% of the time, Pallas kernels for 27%

profile of v4, /device:TPU:1, one launch (start us, length us, event | category | flops | bytes accessed | tf_op | source)
XLA Modules:
  0.0 349.1 jit_solution(4141440661546465171)
XLA Ops:
  0.6 0.7 pad_add_fusion.1.base_ref.refs_1_
  1.3 3.1 route_pack.1
  4.4 12.2 %all-to-all-start = ((bf16[64,8,2048]{2,1,0:T(8,128)(2,1)}), bf16[64,8,2048]{2,1,0:T(8,128)(2,1)}, u32[]{:S(2)}, u32[]{:S(2)}) async-start(bf16[64,8,2048]{2,1,0:T(8,128)(2,1)} %bitcast.33), calls=%async_computation | async-start | bytes 4194304 | tf_op jit(solution)/shard_map/all_to_all | solution.py:467
  16.6 0.6 pad_add_fusion.base_ref.refs_0_
  17.2 1.7 gate_matrix.2.refs_0_
  18.9 3.1 gate_matrix.3.refs_2_
  22.0 4.6 %pack.1 = bf16[1024,2048]{1,0:T(8,128)(2,1)} custom-call(s32[2]{0:T(128)} %pad_add_fusion.base_ref.refs_0_, f32[64,128]{1,0:T(8,128)} %get-tuple-element.46.pos_ref.refs_2_.refs_4_, bf16[128,2048]{1,0:T(8,128)(2,1)} %tok_ref.3), custom_call_target="tpu_custom_call" | custom-call | flops 33554432 | bytes 262144 | tf_op jit(solution)/shard_map/pack/pallas_call | solution.py:122
  26.6 0.0 copy-start
  26.6 0.0 copy-start.1
  26.6 0.0 copy-start.2
  26.6 0.0 copy-start.3
  26.6 4.1 %pad_maximum_fusion.1.wa_ref = bf16[768,2048]{1,0:T(8,128)(2,1)} fusion(bf16[384,2048]{1,0:T(8,128)(2,1)} %bitcast.24, bf16[384,2048]{1,0:T(8,128)(2,1)} %bitcast.38), kind=kLoop, calls=%fused_computation.1 | loop fusion | flops 6291456 | bytes 6291456 | tf_op jit(solution)/shard_map/concatenate | solution.py:495
  30.7 0.0 copy-done
  30.7 0.0 copy-done.1
  30.7 0.0 copy-done.2
  30.7 0.5 copy-done.3
  31.2 3.1 pad_maximum_fusion.w_ref
  34.3 9.5 %all-to-all-done = bf16[64,8,2048]{2,1,0:T(8,128)(2,1)} async-done(((bf16[64,8,2048]{2,1,0:T(8,128)(2,1)}), bf16[64,8,2048]{2,1,0:T(8,128)(2,1)}, u32[]{:S(2)}, u32[]{:S(2)}) %all-to-all-start) | async-done | bytes 2097184 | tf_op jit(solution)/shard_map/all_to_all | solution.py:467
  43.8 6.8 %all-to-all-start.1 = ((bf16[64,16,2048]{2,1,0:T(8,128)(2,1)}), bf16[64,16,2048]{2,1,0:T(8,128)(2,1)}, u32[]{:S(2)}, u32[]{:S(2)}) async-start(bf16[64,16,2048]{2,1,0:T(8,128)(2,1)} %bitcast.28), calls=%async_computation.1 | async-start | bytes 8388608 | tf_op jit(solution)/shard_map/all_to_all | solution.py:467
  50.6 2.1 collective-permute-start.2
  52.8 0.1 collective-permute-start
  52.9 8.5 %collective-permute-done.x_ref.refs_5_ = bf16[512,2048]{1,0:T(8,128)(2,1)} collective-permute-done((bf16[512,2048]{1,0:T(8,128)(2,1)}, bf16[512,2048]{1,0:T(8,128)(2,1)}, u32[]{:S(2)}, u32[]{:S(2)}) %collective-permute-start) | collective-permute-done | bytes 2097184 | tf_op jit(solution)/shard_map/ppermute | solution.py:481
  61.4 7.5 %forward.5 = (bf16[512,768]{1,0:T(8,128)(2,1)}, bf16[512,384]{1,0:T(8,128)(2,1)}, bf16[512,384]{1,0:T(8,128)(2,1)}) custom-call(bf16[512,2048]{1,0:T(8,128)(2,1)} %collective-permute-done.x_ref.refs_5_, bf16[2048,1536]{1,0:T(8,128)(2,1)} %pad_maximum_fusion.w_ref), custom_call_target="tpu_custom_call" | custom-call | flops 201326592 | bytes 278528 | tf_op jit(solution)/shard_map/forward/pallas_call | solution.py:151
  68.9 0.4 collective-permute-start.1
  69.3 7.5 %forward.4 = (bf16[512,768]{1,0:T(8,128)(2,1)}, bf16[512,384]{1,0:T(8,128)(2,1)}, bf16[512,384]{1,0:T(8,128)(2,1)}) custom-call(bf16[512,2048]{1,0:T(8,128)(2,1)} %bitcast.7.x_ref.refs_1_, bf16[2048,1536]{1,0:T(8,128)(2,1)} %pad_maximum_fusion.w_ref), custom_call_target="tpu_custom_call" | custom-call | flops 201326592 | bytes 278528 | tf_op jit(solution)/shard_map/forward/pallas_call | solution.py:151
  76.8 0.0 collective-permute-done.1.b_ref
  76.8 0.0 copy-start.4
  76.9 0.0 collective-permute-done.2.wb_ref
  76.9 0.9 copy-done.4
  77.7 7.7 %part_rows.2 = bf16[512,2048]{1,0:T(8,128)(2,1)} custom-call(bf16[512,768]{1,0:T(8,128)(2,1)} %get-tuple-element.53.a_ref.refs_3_, bf16[512,768]{1,0:T(8,128)(2,1)} %copy-done.4, bf16[768,2048]{1,0:T(8,128)(2,1)} %pad_maximum_fusion.1.wa_ref, bf16[768,2048]{1,0:T(8,128)(2,1)} %collective-permute-done.2.wb_ref), custom_call_target="tpu_custom_call" | custom-call | flops 201326592 | bytes 524288 | tf_op jit(solution)/shard_map/part_rows/pallas_call | solution.py:178
  85.4 13.4 %all-to-all-done.1 = bf16[64,16,2048]{2,1,0:T(8,128)(2,1)} async-done(((bf16[64,16,2048]{2,1,0:T(8,128)(2,1)}), bf16[64,16,2048]{2,1,0:T(8,128)(2,1)}, u32[]{:S(2)}, u32[]{:S(2)}) %all-to-all-start.1) | async-done | bytes 4194336 | tf_op jit(solution)/shard_map/all_to_all | solution.py:467
  98.8 7.2 %collective-permute-start.3 = (bf16[1024,2048]{1,0:T(8,128)(2,1)}, bf16[1024,2048]{1,0:T(8,128)(2,1)}, u32[]{:S(2)}, u32[]{:S(2)}) collective-permute-start(bf16[1024,2048]{1,0:T(8,128)(2,1)} %bitcast.15.x_ref.refs_1_), channel_id=1, source_target_pairs={{0,1},{1,0},{2,3},{3,2},{4,5},{5,4},{6,7},{7,6},{8,9},{9,8},{10,11... | collective-permute-start | bytes 12582920 | tf_op jit(solution)/shard_map/ppermute | solution.py:481
  106.0 12.3 %all-to-all-start.2 = ((bf16[64,8,2048]{2,1,0:T(8,128)(2,1)}), bf16[64,8,2048]{2,1,0:T(8,128)(2,1)}, u32[]{:S(2)}, u32[]{:S(2)}) async-start(bf16[64,8,2048]{2,1,0:T(8,128)(2,1)} %bitcast.31), calls=%async_computation.2 | async-start | bytes 4194304 | tf_op jit(solution)/shard_map/all_to_all | solution.py:467
  118.2 0.0 collective-permute-done.3.x_ref.refs_6_
  118.2 11.2 %forward.7 = (bf16[1024,768]{1,0:T(8,128)(2,1)}, bf16[1024,384]{1,0:T(8,128)(2,1)}, bf16[1024,384]{1,0:T(8,128)(2,1)}) custom-call(bf16[1024,2048]{1,0:T(8,128)(2,1)} %collective-permute-done.3.x_ref.refs_6_, bf16[2048,1536]{1,0:T(8,128)(2,1)} %pad_maximum_fusion.w_ref), custom_call_target="tpu_custom_call" | custom-call | flops 402653184 | bytes 557056 | tf_op jit(solution)/shard_map/forward/pallas_call | solution.py:151
  129.4 0.3 collective-permute-start.4
  129.7 11.2 %forward.6 = (bf16[1024,768]{1,0:T(8,128)(2,1)}, bf16[1024,384]{1,0:T(8,128)(2,1)}, bf16[1024,384]{1,0:T(8,128)(2,1)}) custom-call(bf16[1024,2048]{1,0:T(8,128)(2,1)} %bitcast.15.x_ref.refs_1_, bf16[2048,1536]{1,0:T(8,128)(2,1)} %pad_maximum_fusion.w_ref), custom_call_target="tpu_custom_call" | custom-call | flops 402653184 | bytes 557056 | tf_op jit(solution)/shard_map/forward/pallas_call | solution.py:151
  140.9 0.0 collective-permute-done.4.b_ref
  140.9 11.3 %part_rows.3 = bf16[1024,2048]{1,0:T(8,128)(2,1)} custom-call(bf16[1024,768]{1,0:T(8,128)(2,1)} %get-tuple-element.58.a_ref.refs_2_, bf16[1024,768]{1,0:T(8,128)(2,1)} %collective-permute-done.4.b_ref, bf16[768,2048]{1,0:T(8,128)(2,1)} %pad_maximum_fusion.1.wa_ref, bf16[768,2048]{1,0:T(8,128)(2,1)} %collective-permute-done.2.wb_ref), custom_call_target="tpu_custom_call" | custom-call | flops 402653184 | bytes 655360 | tf_op jit(solution)/shard_map/part_rows/pallas_call | solution.py:178
  152.2 0.0 all-to-all-done.2
  152.2 61.3 %all_to_all.72 = bf16[64,16,2048]{2,1,0:T(8,128)(2,1)} all-to-all(bf16[64,16,2048]{2,1,0:T(8,128)(2,1)} %bitcast.29), channel_id=1, replica_groups=mesh['dp'=4,'expert'=16,'tensor'=2] {'dp','expert'}, dimensions={0} | all-to-all | bytes 8388608 | tf_op jit(solution)/shard_map/all_to_all | solution.py:467
  213.5 4.9 %combine.1.refs_7_ = f32[128,2048]{1,0:T(8,128)} custom-call(bf16[256,512]{1,0:T(8,128)(2,1)} %gate_matrix.2.refs_0_, bf16[512,2048]{1,0:T(8,128)(2,1)} %bitcast.17.refs_1_, bf16[256,1024]{1,0:T(8,128)(2,1)} %gate_matrix.3.refs_2_, bf16[1024,2048]{1,0:T(8,128)(2,1)} %bitcast.30), custom_call_target="tpu_custom_call" | custom-call | flops 100663296 | bytes 393216 | tf_op jit(solution)/shard_map/combine/pallas_call | solution.py:240
  218.4 1.8 collective-permute-start.5
  220.2 2.6 collective-permute-done.5.refs_8_
  222.8 6.9 %weigh_pack.1 = (bf16[1024,2048]{1,0:T(8,128)(2,1)}, bf16[512,2048]{1,0:T(8,128)(2,1)}, bf16[128,1024]{1,0:T(8,128)(2,1)}) custom-call(s32[2]{0:T(128)} %pad_add_fusion.base_ref.refs_0_, s32[2]{0:T(128)} %pad_add_fusion.1.base_ref.refs_1_, f32[64,128]{1,0:T(8,128)} %get-tuple-element.46.pos_ref.refs_2_.refs_4_, ...), custom_call_target="tpu_custom_call" | custom-call | flops 100663296 | bytes 393216 | tf_op jit(solution)/shard_map/weigh_pack/pallas_call | solution.py:295
  229.8 59.0 %all_to_all.73 = bf16[64,16,2048]{2,1,0:T(8,128)(2,1)} all-to-all(bf16[64,16,2048]{2,1,0:T(8,128)(2,1)} %bitcast.32), channel_id=1, replica_groups=mesh['dp'=4,'expert'=16,'tensor'=2] {'dp','expert'}, dimensions={0} | all-to-all | bytes 8388608 | tf_op jit(solution)/shard_map/all_to_all | solution.py:467
  288.8 3.1 collective-permute-start.6
  292.0 8.5 %all-to-all-start.5 = ((bf16[64,8,2048]{2,1,0:T(8,128)(2,1)}), bf16[64,8,2048]{2,1,0:T(8,128)(2,1)}, u32[]{:S(2)}, u32[]{:S(2)}) async-start(bf16[64,8,2048]{2,1,0:T(8,128)(2,1)} %bitcast.22), calls=%async_computation.5 | async-start | bytes 4194304 | tf_op jit(solution)/shard_map/all_to_all | solution.py:467
  300.5 0.0 collective-permute-done.6.refs_5_
  300.5 22.8 %phased_sums.1 = (f32[1,2048,384]{2,1,0:T(8,128)}, f32[1,2048,384]{2,1,0:T(8,128)}, f32[1,384,2048]{2,1,0:T(8,128)}) custom-call(bf16[1024,2048]{1,0:T(8,128)(2,1)} %bitcast.21.refs_0_, bf16[1024,2048]{1,0:T(8,128)(2,1)} %bitcast.15.x_ref.refs_1_, bf16[1024,768]{1,0:T(8,128)(2,1)} %get-tuple-element.58.a_ref.refs_2_, ...), custom_call_target="tpu_custom_call" | custom-call | flops 805306368 | bytes 1048576 | tf_op jit(solution)/shard_map/phased_sums/pallas_call | solution.py:392
  323.3 5.7 %all-to-all-done.5 = bf16[64,8,2048]{2,1,0:T(8,128)(2,1)} async-done(((bf16[64,8,2048]{2,1,0:T(8,128)(2,1)}), bf16[64,8,2048]{2,1,0:T(8,128)(2,1)}, u32[]{:S(2)}, u32[]{:S(2)}) %all-to-all-start.5) | async-done | bytes 2097184 | tf_op jit(solution)/shard_map/all_to_all | solution.py:467
  329.0 1.5 collective-permute-start.7
  330.5 4.2 %gradients.1.refs_2_ = bf16[512,768]{1,0:T(8,128)(2,1)} custom-call(bf16[512,2048]{1,0:T(8,128)(2,1)} %bitcast.23.q_ref.refs_0_, bf16[512,384]{1,0:T(8,128)(2,1)} %get-tuple-element.77.silu_ref, bf16[512,384]{1,0:T(8,128)(2,1)} %get-tuple-element.78.us_ref, bf16[384,2048]{1,0:T(8,128)(2,1)} %bitcast.26), custom_call_target="tpu_custom_call" | custom-call | flops 50331648 | bytes 131072 | tf_op jit(solution)/shard_map/gradients/pallas_call | solution.py:322
  334.7 0.0 collective-permute-done.7.refs_4_
  334.7 14.4 %last_sums.1 = (f32[1,2048,384]{2,1,0:T(8,128)}, f32[1,2048,384]{2,1,0:T(8,128)}, f32[1,384,2048]{2,1,0:T(8,128)}) custom-call(bf16[512,2048]{1,0:T(8,128)(2,1)} %bitcast.23.q_ref.refs_0_, bf16[512,2048]{1,0:T(8,128)(2,1)} %bitcast.7.x_ref.refs_1_, bf16[512,768]{1,0:T(8,128)(2,1)} %gradients.1.refs_2_, bf16[512,768]{1,0:T(8,128)(2,1)} %get-tuple-element.53.a_ref.refs_3_, ...), custom_call_target="tpu_custom_call" | custom-call | flops 352321536 | bytes 524288 | tf_op jit(solution)/shard_map/last_sums/pallas_call | solution.py:447
Async XLA Ops:
  4.4 39.4 %all-to-all-start = ((bf16[64,8,2048]{2,1,0:T(8,128)(2,1)}), bf16[64,8,2048]{2,1,0:T(8,128)(2,1)}, u32[]{:S(2)}, u32[]{:S(2)}) async-start(bf16[64,8,2048]{2,1,0:T(8,128)(2,1)} %bitcast.33), calls=%async_computation | async-start | bytes 4194304 | tf_op jit(solution)/shard_map/all_to_all | solution.py:467
  26.6 4.1 %copy-start = (bf16[1,2048,384]{2,1,0:T(8,128)(2,1)S(1)}, bf16[1,2048,384]{2,1,0:T(8,128)(2,1)}, u32[]{:S(2)}) copy-start(bf16[1,2048,384]{2,1,0:T(8,128)(2,1)} %param.18) | copy-start | bytes 4718596
  26.6 4.1 %copy-start.1 = (bf16[1,2048,384]{2,1,0:T(8,128)(2,1)S(1)}, bf16[1,2048,384]{2,1,0:T(8,128)(2,1)}, u32[]{:S(2)}) copy-start(bf16[1,2048,384]{2,1,0:T(8,128)(2,1)} %param.17) | copy-start | bytes 4718596
  26.6 4.1 %copy-start.2 = (bf16[1,2048,384]{2,1,0:T(8,128)(2,1)S(1)}, bf16[1,2048,384]{2,1,0:T(8,128)(2,1)}, u32[]{:S(2)}) copy-start(bf16[1,2048,384]{2,1,0:T(8,128)(2,1)} %param.15) | copy-start | bytes 4718596
  26.6 4.6 %copy-start.3 = (bf16[1,2048,384]{2,1,0:T(8,128)(2,1)S(1)}, bf16[1,2048,384]{2,1,0:T(8,128)(2,1)}, u32[]{:S(2)}) copy-start(bf16[1,2048,384]{2,1,0:T(8,128)(2,1)} %param.14) | copy-start | bytes 4718596
  43.8 55.0 %all-to-all-start.1 = ((bf16[64,16,2048]{2,1,0:T(8,128)(2,1)}), bf16[64,16,2048]{2,1,0:T(8,128)(2,1)}, u32[]{:S(2)}, u32[]{:S(2)}) async-start(bf16[64,16,2048]{2,1,0:T(8,128)(2,1)} %bitcast.28), calls=%async_computation.1 | async-start | bytes 8388608 | tf_op jit(solution)/shard_map/all_to_all | solution.py:467
  50.6 26.2 %collective-permute-start.2 = (bf16[768,2048]{1,0:T(8,128)(2,1)}, bf16[768,2048]{1,0:T(8,128)(2,1)}, u32[]{:S(2)}, u32[]{:S(2)}) collective-permute-start(bf16[768,2048]{1,0:T(8,128)(2,1)} %pad_maximum_fusion.1.wa_ref), channel_id=1, source_target_pairs={{0,1},{1,0},{2,3},{3,2},{4,5},{5,4},{6,7},{7,6},{8,9},{9,8},{10,11... | collective-permute-start | bytes 9437192 | tf_op jit(solution)/shard_map/ppermute | solution.py:481
  52.8 8.6 %collective-permute-start = (bf16[512,2048]{1,0:T(8,128)(2,1)}, bf16[512,2048]{1,0:T(8,128)(2,1)}, u32[]{:S(2)}, u32[]{:S(2)}) collective-permute-start(bf16[512,2048]{1,0:T(8,128)(2,1)} %bitcast.7.x_ref.refs_1_), channel_id=1, source_target_pairs={{0,1},{1,0},{2,3},{3,2},{4,5},{5,4},{6,7},{7,6},{8,9},{9,8},{10,11... | collective-permute-start | bytes 6291464 | tf_op jit(solution)/shard_map/ppermute | solution.py:481
  68.9 7.9 %collective-permute-start.1 = (bf16[512,768]{1,0:T(8,128)(2,1)}, bf16[512,768]{1,0:T(8,128)(2,1)S(1)}, u32[]{:S(2)}, u32[]{:S(2)}) collective-permute-start(bf16[512,768]{1,0:T(8,128)(2,1)} %get-tuple-element.54.refs_6_), channel_id=1, source_target_pairs={{0,1},{1,0},{2,3},{3,2},{4,5},{5,4},{6,7},{7,6},{8,9},{9,8},{10,11... | collective-permute-start | bytes 2359304 | tf_op jit(solution)/shard_map/ppermute | solution.py:481
  76.8 0.9 copy-start.4
  98.8 19.5 %collective-permute-start.3 = (bf16[1024,2048]{1,0:T(8,128)(2,1)}, bf16[1024,2048]{1,0:T(8,128)(2,1)}, u32[]{:S(2)}, u32[]{:S(2)}) collective-permute-start(bf16[1024,2048]{1,0:T(8,128)(2,1)} %bitcast.15.x_ref.refs_1_), channel_id=1, source_target_pairs={{0,1},{1,0},{2,3},{3,2},{4,5},{5,4},{6,7},{7,6},{8,9},{9,8},{10,11... | collective-permute-start | bytes 12582920 | tf_op jit(solution)/shard_map/ppermute | solution.py:481
  106.0 46.3 %all-to-all-start.2 = ((bf16[64,8,2048]{2,1,0:T(8,128)(2,1)}), bf16[64,8,2048]{2,1,0:T(8,128)(2,1)}, u32[]{:S(2)}, u32[]{:S(2)}) async-start(bf16[64,8,2048]{2,1,0:T(8,128)(2,1)} %bitcast.31), calls=%async_computation.2 | async-start | bytes 4194304 | tf_op jit(solution)/shard_map/all_to_all | solution.py:467
  129.4 11.5 %collective-permute-start.4 = (bf16[1024,768]{1,0:T(8,128)(2,1)}, bf16[1024,768]{1,0:T(8,128)(2,1)}, u32[]{:S(2)}, u32[]{:S(2)}) collective-permute-start(bf16[1024,768]{1,0:T(8,128)(2,1)} %get-tuple-element.59.refs_7_), channel_id=1, source_target_pairs={{0,1},{1,0},{2,3},{3,2},{4,5},{5,4},{6,7},{7,6},{8,9},{9,8},{10,11... | collective-permute-start | bytes 4718600 | tf_op jit(solution)/shard_map/ppermute | solution.py:481
  218.4 4.4 %collective-permute-start.5 = (f32[128,2048]{1,0:T(8,128)}, f32[128,2048]{1,0:T(8,128)}, u32[]{:S(2)}, u32[]{:S(2)}) collective-permute-start(f32[128,2048]{1,0:T(8,128)} %combine.1.refs_7_), channel_id=1, source_target_pairs={{0,1},{1,0},{2,3},{3,2},{4,5},{5,4},{6,7},{7,6},{8,9},{9,8},{10,11... | collective-permute-start | bytes 3145736 | tf_op jit(solution)/shard_map/ppermute | solution.py:481
  288.8 11.7 %collective-permute-start.6 = (bf16[1024,2048]{1,0:T(8,128)(2,1)}, bf16[1024,2048]{1,0:T(8,128)(2,1)}, u32[]{:S(2)}, u32[]{:S(2)}) collective-permute-start(bf16[1024,2048]{1,0:T(8,128)(2,1)} %bitcast.21.refs_0_), channel_id=1, source_target_pairs={{0,1},{1,0},{2,3},{3,2},{4,5},{5,4},{6,7},{7,6},{8,9},{9,8},{10,11... | collective-permute-start | bytes 12582920 | tf_op jit(solution)/shard_map/ppermute | solution.py:481
  292.0 37.0 %all-to-all-start.5 = ((bf16[64,8,2048]{2,1,0:T(8,128)(2,1)}), bf16[64,8,2048]{2,1,0:T(8,128)(2,1)}, u32[]{:S(2)}, u32[]{:S(2)}) async-start(bf16[64,8,2048]{2,1,0:T(8,128)(2,1)} %bitcast.22), calls=%async_computation.5 | async-start | bytes 4194304 | tf_op jit(solution)/shard_map/all_to_all | solution.py:467
  329.0 5.8 %collective-permute-start.7 = (bf16[512,2048]{1,0:T(8,128)(2,1)}, bf16[512,2048]{1,0:T(8,128)(2,1)}, u32[]{:S(2)}, u32[]{:S(2)}) collective-permute-start(bf16[512,2048]{1,0:T(8,128)(2,1)} %bitcast.23.q_ref.refs_0_), channel_id=1, source_target_pairs={{0,1},{1,0},{2,3},{3,2},{4,5},{5,4},{6,7},{7,6},{8,9},{9,8},{10,11... | collective-permute-start | bytes 6291464 | tf_op jit(solution)/shard_map/ppermute | solution.py:481

commit v5 on v4

--- a/solution.py
+++ b/solution.py
@@ -131,65 +131,75 @@
     )(base, pos, tokens)
 
 
-def forward(rows, mats, hidden):
+def forward(rows, mats_own, mats_other, down_own, down_other):
     count, width = rows.shape
-
-    def kernel(x_ref, w_ref, ad_ref, silu_ref, us_ref):
-        pre = mm(x_ref[...], w_ref[...])
-        gate = pre[:, :hidden]
-        up = pre[:, hidden : 2 * hidden]
-        d_gate = pre[:, 2 * hidden : 3 * hidden]
-        d_up = pre[:, 3 * hidden :]
-        sigma = jax.nn.sigmoid(gate)
-        silu = gate * sigma
-        us = sigma * (1.0 + gate * (1.0 - sigma)) * up
-        ad_ref[:, :hidden] = (silu * up).astype(BF)
-        ad_ref[:, hidden:] = (us * d_gate + silu * d_up).astype(BF)
-        silu_ref[...] = silu.astype(BF)
-        us_ref[...] = us.astype(BF)
-
+    hidden = mats_own.shape[1] // 4
+
+    def kernel(x_ref, *refs):
+        sources = refs[:4]
+        part_ref, own_ref, other_ref = refs[4:7]
+        held, sems = refs[7:11], refs[11]
+        first = pl.program_id(0) == 0
+        copies = [
+            pltpu.make_async_copy(source, target, sems.at[n])
+            for n, (source, target) in enumerate(zip(sources, held))
+        ]
+
+        @pl.when(first)
+        def _():
+            for copy in copies:
+                copy.start()
+
+        def ready(n):
+            @pl.when(first)
+            def _():
+                copies[n].wait()
+
+        def side(n, aux_ref):
+            ready(n)
+            pre = mm(x_ref[...], held[n][...])
+            gate = pre[:, :hidden]
+            up = pre[:, hidden : 2 * hidden]
+            d_gate = pre[:, 2 * hidden : 3 * hidden]
+            d_up = pre[:, 3 * hidden :]
+            sigma = jax.nn.sigmoid(gate)
+            silu = gate * sigma
+            us = sigma * (1.0 + gate * (1.0 - sigma)) * up
+            act = (silu * up).astype(BF)
+            aux_ref[:, :hidden] = act
+            aux_ref[:, hidden : 2 * hidden] = silu.astype(BF)
+            aux_ref[:, 2 * hidden :] = us.astype(BF)
+            d_act = (us * d_gate + silu * d_up).astype(BF)
+            return jnp.concatenate([act, d_act], axis=1)
+
+        left = side(0, own_ref)
+        right = side(1, other_ref)
+        ready(2)
+        ready(3)
+        part_ref[...] = (mm(left, held[2][...]) + mm(right, held[3][...])).astype(BF)
+
+    weights = [mats_own, mats_other, down_own, down_other]
     return pl.pallas_call(
         kernel,
         grid=(count // TILE,),
-        in_specs=[pl.BlockSpec((TILE, width), lambda i: (i, 0)), fixed((width, 4 * hidden))],
+        in_specs=[pl.BlockSpec((TILE, width), lambda i: (i, 0))]
+        + [pl.BlockSpec(memory_space=pl.ANY) for _ in weights],
         out_specs=[
-            pl.BlockSpec((TILE, 2 * hidden), lambda i: (i, 0)),
-            pl.BlockSpec((TILE, hidden), lambda i: (i, 0)),
-            pl.BlockSpec((TILE, hidden), lambda i: (i, 0)),
+            pl.BlockSpec((TILE, width), lambda i: (i, 0)),
+            pl.BlockSpec((TILE, 3 * hidden), lambda i: (i, 0)),
+            pl.BlockSpec((TILE, 3 * hidden), lambda i: (i, 0)),
         ],
         out_shape=[
-            jax.ShapeDtypeStruct((count, 2 * hidden), BF),
-            jax.ShapeDtypeStruct((count, hidden), BF),
-            jax.ShapeDtypeStruct((count, hidden), BF),
-        ],
-        compiler_params=params(),
-        cost_estimate=cost(8 * count * width * hidden, 2 * count * width + 12 * count * hidden),
+            jax.ShapeDtypeStruct((count, width), BF),
+            jax.ShapeDtypeStruct((count, 3 * hidden), BF),
+            jax.ShapeDtypeStruct((count, 3 * hidden), BF),
+        ],
+        scratch_shapes=[pltpu.VMEM(w.shape, BF) for w in weights]
+        + [pltpu.SemaphoreType.DMA((len(weights),))],
+        compiler_params=params(),
+        cost_estimate=cost(24 * count * width * hidden, 8 * count * width),
         name="forward",
-    )(rows, mats)
-
-
-def part_rows(ad_own, ad_other, down_own, down_other):
-    count, inner = ad_own.shape
-    width = down_own.shape[1]
-
-    def kernel(a_ref, b_ref, wa_ref, wb_ref, out_ref):
-        out_ref[...] = (mm(a_ref[...], wa_ref[...]) + mm(b_ref[...], wb_ref[...])).astype(BF)
-
-    return pl.pallas_call(
-        kernel,
-        grid=(count // TILE,),
-        in_specs=[
-            pl.BlockSpec((TILE, inner), lambda i: (i, 0)),
-            pl.BlockSpec((TILE, inner), lambda i: (i, 0)),
-            fixed((inner, width)),
-            fixed((inner, width)),
-        ],
-        out_specs=pl.BlockSpec((TILE, width), lambda i: (i, 0)),
-        out_shape=jax.ShapeDtypeStruct((count, width), BF),
-        compiler_params=params(),
-        cost_estimate=cost(4 * count * width * inner, 2 * count * width + 4 * inner * width),
-        name="part_rows",
-    )(ad_own, ad_other, down_own, down_other)
+    )(rows, *weights)
 
 
 def gate_matrix(base, pos, gm, per):
@@ -309,7 +319,7 @@
     )(*bases, *[array for _ in pers for array in (pos, gm)], weight, own, other)
 
 
-def gradients(q, silu, us, down):
+def gradients(q, aux, down):
     count, width = q.shape
     hidden = down.shape[0]
     tile = min(TILE, count)
@@ -324,8 +334,8 @@
         grid=(count // tile,),
         in_specs=[
             pl.BlockSpec((tile, width), lambda i: (i, 0)),
-            pl.BlockSpec((tile, hidden), lambda i: (i, 0)),
-            pl.BlockSpec((tile, hidden), lambda i: (i, 0)),
+            pl.BlockSpec((tile, hidden), lambda i: (i, 1)),
+            pl.BlockSpec((tile, hidden), lambda i: (i, 2)),
             fixed((hidden, width)),
         ],
         out_specs=pl.BlockSpec((tile, 2 * hidden), lambda i: (i, 0)),
@@ -333,7 +343,7 @@
         compiler_params=params(),
         cost_estimate=cost(2 * count * width * hidden, 2 * count * width),
         name="gradients",
-    )(q, silu, us, down)
+    )(q, aux, aux, down)
 
 
 def phased_sums(own, other, down, factor):
@@ -384,8 +394,8 @@
             pl.BlockSpec((tile, width), lambda i: (at(i), 0)),
             pl.BlockSpec((count, piece), lambda i: (0, later(i))),
             pl.BlockSpec((tile, hidden), lambda i: (at(i), 0)),
-            pl.BlockSpec((tile, hidden), lambda i: (at(i), 0)),
-            pl.BlockSpec((tile, hidden), lambda i: (at(i), 0)),
+            pl.BlockSpec((tile, hidden), lambda i: (at(i), 1)),
+            pl.BlockSpec((tile, hidden), lambda i: (at(i), 2)),
         ]
 
     shapes = [(1, width, hidden), (1, width, hidden), (1, hidden, width)]
@@ -407,10 +417,10 @@
         compiler_params=params(),
         cost_estimate=cost(16 * count * width * hidden, 8 * count * width),
         name="phased_sums",
-    )(*own, *other, down)
-
-
-def last_sums(own, other, silu, us, down, start, factor):
+    )(*own, own[2], own[2], *other, other[2], other[2], down)
+
+
+def last_sums(own, other, down, start, factor):
     count, width = own[0].shape
     hidden = down.shape[0]
     piece = LAST_PIECE
@@ -437,7 +447,11 @@
             out[0] = factor * term + begin[0]
 
     column = pl.BlockSpec((count, piece), lambda i: (0, i))
-    act = pl.BlockSpec((count, hidden), lambda i: (0, 0), pipeline_mode=pl.Buffered(buffer_count=1))
+
+    def third(n):
+        once = pl.Buffered(buffer_count=1)
+        return pl.BlockSpec((count, hidden), lambda i: (0, n), pipeline_mode=once)
+
     results = [
         pl.BlockSpec((1, piece, hidden), lambda i: (0, i, 0)),
         pl.BlockSpec((1, piece, hidden), lambda i: (0, i, 0)),
@@ -447,9 +461,9 @@
     return pl.pallas_call(
         kernel,
         grid=(width // piece,),
-        in_specs=[column, column, fixed((count, 2 * hidden)), act]
-        + [fixed((count, width)), column, act]
-        + [fixed((count, hidden)), fixed((count, hidden)), fixed((hidden, width))]
+        in_specs=[column, column, fixed((count, 2 * hidden)), third(0)]
+        + [fixed((count, width)), column, third(0)]
+        + [third(1), third(2), fixed((hidden, width))]
         + results,
         out_specs=results,
         out_shape=[jax.ShapeDtypeStruct(shape, F32) for shape in shapes],
@@ -460,7 +474,7 @@
         compiler_params=params(),
         cost_estimate=cost(14 * count * width * hidden, 8 * count * width),
         name="last_sums",
-    )(*own, *other, silu, us, down, *start)
+    )(*own, *other, other[2], other[2], down, *start)
 
 
 def exchange(rows):
@@ -492,30 +506,23 @@
     arrived = exchange(packed)
     later = [pack(base, pos, tokens, per) for base, per in chunks[1:]]
     mats = jnp.concatenate([w_gate[0], w_up[0], v_gate[0], v_up[0]], axis=1)
-    down_own = jnp.concatenate([v_down[0], w_down[0]], axis=0)
+    downs = jnp.concatenate([v_down[0], w_down[0]], axis=0)
     matrices = [gate_matrix(base, pos, gm, per) for base, per in chunks]
-    arrived, later, mats, down_own, matrices = lax.optimization_barrier(
-        (arrived, later, mats, down_own, matrices)
+    arrived, later, mats, downs, matrices = lax.optimization_barrier(
+        (arrived, later, mats, downs, matrices)
     )
     weight = token_weight[None, :]
-    down_other = swap(down_own)
-
-    def run_forward(x_own):
-        x_other = swap(x_own)
-        mine = forward(x_own, mats, hidden)
-        theirs = forward(x_other, mats, hidden)
-        part = part_rows(mine[0], swap(theirs[0]), down_own, down_other)
-        return part, (x_own, *mine), (x_other, *theirs)
-
-    sides = []
     x_large = exchange(later[0])
-    part, mine, theirs = run_forward(arrived)
-    sides.append((mine, theirs))
-    x_large, part = lax.optimization_barrier((x_large, part))
+    mats_other, downs_other = swap(mats), swap(downs)
+
+    x_small = arrived
+    part, aux_small, sent = forward(x_small, mats, mats_other, downs, downs_other)
+    theirs_small = swap(x_small), swap(sent)
+    x_large, part, theirs_small = lax.optimization_barrier((x_large, part, theirs_small))
     returned = exchange(part)
-    part, mine, theirs = run_forward(x_large)
-    sides.append((mine, theirs))
-    returned, part = lax.optimization_barrier((returned, part))
+    x_their = swap(x_large)
+    part, aux_large, sent = forward(x_large, mats, mats_other, downs, downs_other)
+    returned, part, x_their = lax.optimization_barrier((returned, part, x_their))
     last = exchange(part)
     last, returned = lax.optimization_barrier((last, returned))
     own = combine(list(zip(matrices, (returned, last))))
@@ -527,19 +534,16 @@
         bases, pers, pos, gm, weight, own, other, width // cores
     )
     q_large = exchange(send_large)
-    q_large, send_small = lax.optimization_barrier((q_large, send_small))
+    q_large, send_small, sent = lax.optimization_barrier((q_large, send_small, sent))
     q_small = exchange(send_small)
     down = w_down[0]
-    mine, theirs = sides[1]
-    sums = phased_sums((q_large, *mine), (swap(q_large), *theirs), down, factor)
+    sums = phased_sums(
+        (q_large, x_large, aux_large), (swap(q_large), x_their, swap(sent)), down, factor
+    )
     q_small, sums = lax.optimization_barrier((q_small, sums))
     q_other = swap(q_small)
-    x, ad, silu, us = sides[0][0]
-    own_side = (q_small, x, gradients(q_small, silu, us, down), ad)
-    x, ad, silu, us = sides[0][1]
-    gv_gate, gv_up, gv_down = last_sums(
-        own_side, (q_other, x, ad), silu, us, down, sums, factor
-    )
+    own_side = (q_small, x_small, gradients(q_small, aux_small, down), aux_small)
+    gv_gate, gv_up, gv_down = last_sums(own_side, (q_other, *theirs_small), down, sums, factor)
     return gv_gate, gv_up, gv_down, tangent
 
 

time: 350 us -> 344 us (0.983)
  waiting for transfers between devices: 39.8 us -> 53.2 us
  Pallas kernels: 122 us -> 109 us
  blocking collectives: 120 us -> 114 us
    pallas_call x2 -> x0, Pallas kernels: 19 us -> none  [part_rows(): pl.pallas_call(kernel, grid=(count // TILE,), in_specs=[pl.BlockSpec((TIL...]
    all_to_all x4, waiting for transfers between devices: 28.6 us -> 39.9 us  [exchange(): return lax.all_to_all(rows, GROUP, split_axis=0, concat_axis=0, tiled=True)]
    all_to_all x2, blocking collectives: 120 us -> 114 us  [exchange(): return lax.all_to_all(rows, GROUP, split_axis=0, concat_axis=0, tiled=True)]
    pallas_call x4 -> x2, Pallas kernels: 37.4 us -> 42.8 us  [forward(): pl.pallas_call(kernel, grid=(count // TILE,), in_specs=[pl.BlockSpec((TIL...]
    ppermute x8 -> x9, waiting for transfers between devices: 11.2 us -> 13.2 us  [swap(): return lax.ppermute(rows, 'tensor', [(0, 1), (1, 0)])]
    ppermute x8 -> x9, starting transfers between devices: 16.5 us -> 16.4 us  [swap(): return lax.ppermute(rows, 'tensor', [(0, 1), (1, 0)])]
  transfers between devices with their start and end apart: 12 -> 13, of which waited for: 5 -> 8; matrix products, arithmetic and copies ran while one was open for 2% -> 2% of each run, Pallas kernels for 27% -> 23%
where the time goes in v5:
time: 344 us; the launch traced here: 343 us
  blocking collectives  114 us (33%)
  Pallas kernels  109 us (32%)
  starting transfers between devices  56 us (16%)
  waiting for transfers between devices  53.2 us (15%)
  other arithmetic  6.67 us (2%)
    all_to_all x2, blocking collectives, exchange(): return lax.all_to_all(rows, GROUP, split_axis=0, concat_axis=0, tiled=True)  114 us
    pallas_call x2, Pallas kernels, forward(): pl.pallas_call(kernel, grid=(count // TILE,), in_specs=[pl.BlockSpec((TIL...  42.8 us
    all_to_all x4, waiting for transfers between devices, exchange(): return lax.all_to_all(rows, GROUP, split_axis=0, concat_axis=0, tiled=True)  39.9 us
    all_to_all x4, starting transfers between devices, exchange(): return lax.all_to_all(rows, GROUP, split_axis=0, concat_axis=0, tiled=True)  39.6 us
    pallas_call x1, Pallas kernels, phased_sums(): pl.pallas_call(kernel, grid=(head + width // piece,), in_specs=specs(0) +...  23.4 us
    ppermute x9, starting transfers between devices, swap(): return lax.ppermute(rows, 'tensor', [(0, 1), (1, 0)])  16.4 us
    pallas_call x1, Pallas kernels, last_sums(): pl.pallas_call(kernel, grid=(width // piece,), in_specs=[column, column,...  14.4 us
    ppermute x9, waiting for transfers between devices, swap(): return lax.ppermute(rows, 'tensor', [(0, 1), (1, 0)])  13.2 us
  transfers between devices with their start and end apart: 13, of which 8 were waited for; matrix products, arithmetic and copies ran while one was open for 2% of the time, Pallas kernels for 23%

profile of v5, /device:TPU:1, one launch (start us, length us, event | category | flops | bytes accessed | tf_op | source)
XLA Modules:
  0.0 342.6 jit_solution(18137999229554858250)
XLA Ops:
  0.6 0.7 pad_add_fusion.1.base_ref.refs_1_
  1.3 3.1 route_pack.1
  4.4 12.2 %all-to-all-start = ((bf16[64,8,2048]{2,1,0:T(8,128)(2,1)}), bf16[64,8,2048]{2,1,0:T(8,128)(2,1)}, u32[]{:S(2)}, u32[]{:S(2)}) async-start(bf16[64,8,2048]{2,1,0:T(8,128)(2,1)} %bitcast.33), calls=%async_computation | async-start | bytes 4194304 | tf_op jit(solution)/shard_map/all_to_all | solution.py:481
  16.6 0.7 pad_add_fusion.base_ref.refs_0_
  17.3 1.7 gate_matrix.2.refs_0_
  19.0 3.1 gate_matrix.3.refs_2_
  22.1 4.6 %pack.1 = bf16[1024,2048]{1,0:T(8,128)(2,1)} custom-call(s32[2]{0:T(128)} %pad_add_fusion.base_ref.refs_0_, f32[64,128]{1,0:T(8,128)} %get-tuple-element.44.pos_ref.refs_2_.refs_4_, bf16[128,2048]{1,0:T(8,128)(2,1)} %tok_ref.3), custom_call_target="tpu_custom_call" | custom-call | flops 33554432 | bytes 262144 | tf_op jit(solution)/shard_map/pack/pallas_call | solution.py:122
  26.6 0.0 copy-start.1
  26.6 0.0 copy-start.2
  26.6 0.0 copy-start.3
  26.6 0.0 copy-start.4
  26.7 2.3 pad_maximum_fusion.1.refs_2_
  28.9 0.0 copy-start
  28.9 0.1 copy-done.1
  29.0 0.5 copy-done.2
  29.5 0.6 copy-done.3
  30.1 1.5 copy-done.4
  31.6 3.1 pad_maximum_fusion.refs_0_
  34.7 9.1 %all-to-all-done = bf16[64,8,2048]{2,1,0:T(8,128)(2,1)} async-done(((bf16[64,8,2048]{2,1,0:T(8,128)(2,1)}), bf16[64,8,2048]{2,1,0:T(8,128)(2,1)}, u32[]{:S(2)}, u32[]{:S(2)}) %all-to-all-start) | async-done | bytes 2097184 | tf_op jit(solution)/shard_map/all_to_all | solution.py:481
  43.8 3.2 collective-permute-start
  47.0 0.0 copy-done
  47.0 0.0 collective-permute-start.1
  47.0 5.7 %all-to-all-start.1 = ((bf16[64,16,2048]{2,1,0:T(8,128)(2,1)}), bf16[64,16,2048]{2,1,0:T(8,128)(2,1)}, u32[]{:S(2)}, u32[]{:S(2)}) async-start(bf16[64,16,2048]{2,1,0:T(8,128)(2,1)} %bitcast.28), calls=%async_computation.1 | async-start | bytes 8388608 | tf_op jit(solution)/shard_map/all_to_all | solution.py:481
  52.7 0.6 collective-permute-start.2
  53.3 8.6 %collective-permute-done.1.refs_3_ = bf16[768,2048]{1,0:T(8,128)(2,1)} collective-permute-done((bf16[768,2048]{1,0:T(8,128)(2,1)S(1)}, bf16[768,2048]{1,0:T(8,128)(2,1)}, u32[]{:S(2)}, u32[]{:S(2)}) %collective-permute-start.1) | collective-permute-done | bytes 3145760 | tf_op jit(solution)/shard_map/ppermute | solution.py:495
  61.9 0.0 collective-permute-done.refs_1_
  61.9 15.9 %forward.2 = (bf16[512,2048]{1,0:T(8,128)(2,1)}, bf16[512,1152]{1,0:T(8,128)(2,1)}, bf16[512,1152]{1,0:T(8,128)(2,1)}) custom-call(bf16[512,2048]{1,0:T(8,128)(2,1)} %bitcast.7.x_ref.refs_1_, bf16[2048,1536]{1,0:T(8,128)(2,1)} %pad_maximum_fusion.refs_0_, bf16[2048,1536]{1,0:T(8,128)(2,1)} %collective-permute-done.refs_1_, bf16[768,2048]{1,0:T(8,128)(2,1)} %copy-done, ...), custom_call_target="tpu_custom_call" | custom-call | flops 603979776 | bytes 524288 | tf_op jit(solution)/shard_map/forward/pallas_call | solution.py:182
  77.8 0.2 collective-permute-start.3
  78.1 0.0 collective-permute-done.2.refs_5_
  78.1 27.4 %all-to-all-done.1 = bf16[64,16,2048]{2,1,0:T(8,128)(2,1)} async-done(((bf16[64,16,2048]{2,1,0:T(8,128)(2,1)}), bf16[64,16,2048]{2,1,0:T(8,128)(2,1)}, u32[]{:S(2)}, u32[]{:S(2)}) %all-to-all-start.1) | async-done | bytes 4194336 | tf_op jit(solution)/shard_map/all_to_all | solution.py:481
  105.5 0.0 collective-permute-done.3.refs_6_.refs_7_.refs_8_
  105.5 2.9 collective-permute-start.4
  108.4 13.1 %all-to-all-start.2 = ((bf16[64,8,2048]{2,1,0:T(8,128)(2,1)}), bf16[64,8,2048]{2,1,0:T(8,128)(2,1)}, u32[]{:S(2)}, u32[]{:S(2)}) async-start(bf16[64,8,2048]{2,1,0:T(8,128)(2,1)} %bitcast.32), calls=%async_computation.2 | async-start | bytes 4194304 | tf_op jit(solution)/shard_map/all_to_all | solution.py:481
  121.5 26.8 %forward.3 = (bf16[1024,2048]{1,0:T(8,128)(2,1)}, bf16[1024,1152]{1,0:T(8,128)(2,1)}, bf16[1024,1152]{1,0:T(8,128)(2,1)}) custom-call(bf16[1024,2048]{1,0:T(8,128)(2,1)} %bitcast.15.x_ref.refs_1_, bf16[2048,1536]{1,0:T(8,128)(2,1)} %pad_maximum_fusion.refs_0_, bf16[2048,1536]{1,0:T(8,128)(2,1)} %collective-permute-done.refs_1_, bf16[768,2048]{1,0:T(8,128)(2,1)} %copy-done, ...), custom_call_target="tpu_custom_call" | custom-call | flops 1207959552 | bytes 1048576 | tf_op jit(solution)/shard_map/forward/pallas_call | solution.py:182
  148.3 1.6 all-to-all-done.2
  149.9 0.0 collective-permute-done.4.refs_6_
  149.9 58.0 %all_to_all.72 = bf16[64,16,2048]{2,1,0:T(8,128)(2,1)} all-to-all(bf16[64,16,2048]{2,1,0:T(8,128)(2,1)} %bitcast.30), channel_id=1, replica_groups=mesh['dp'=4,'expert'=16,'tensor'=2] {'dp','expert'}, dimensions={0} | all-to-all | bytes 8388608 | tf_op jit(solution)/shard_map/all_to_all | solution.py:481
  207.9 5.0 %combine.1.refs_7_ = f32[128,2048]{1,0:T(8,128)} custom-call(bf16[256,512]{1,0:T(8,128)(2,1)} %gate_matrix.2.refs_0_, bf16[512,2048]{1,0:T(8,128)(2,1)} %bitcast.17.refs_1_, bf16[256,1024]{1,0:T(8,128)(2,1)} %gate_matrix.3.refs_2_, bf16[1024,2048]{1,0:T(8,128)(2,1)} %bitcast.29), custom_call_target="tpu_custom_call" | custom-call | flops 100663296 | bytes 393216 | tf_op jit(solution)/shard_map/combine/pallas_call | solution.py:250
  212.9 3.4 collective-permute-start.5
  216.2 2.6 collective-permute-done.5.refs_8_
  218.8 7.0 %weigh_pack.1 = (bf16[1024,2048]{1,0:T(8,128)(2,1)}, bf16[512,2048]{1,0:T(8,128)(2,1)}, bf16[128,1024]{1,0:T(8,128)(2,1)}) custom-call(s32[2]{0:T(128)} %pad_add_fusion.base_ref.refs_0_, s32[2]{0:T(128)} %pad_add_fusion.1.base_ref.refs_1_, f32[64,128]{1,0:T(8,128)} %get-tuple-element.44.pos_ref.refs_2_.refs_4_, ...), custom_call_target="tpu_custom_call" | custom-call | flops 100663296 | bytes 393216 | tf_op jit(solution)/shard_map/weigh_pack/pallas_call | solution.py:305
  225.8 0.0 copy-start.5
  225.8 56.3 %all_to_all.73 = bf16[64,16,2048]{2,1,0:T(8,128)(2,1)} all-to-all(bf16[64,16,2048]{2,1,0:T(8,128)(2,1)} %bitcast.31), channel_id=1, replica_groups=mesh['dp'=4,'expert'=16,'tensor'=2] {'dp','expert'}, dimensions={0} | all-to-all | bytes 8388608 | tf_op jit(solution)/shard_map/all_to_all | solution.py:481
  282.1 3.1 collective-permute-start.6
  285.2 0.0 copy-done.5
  285.2 0.0 collective-permute-start.7
  285.2 8.5 %all-to-all-start.5 = ((bf16[64,8,2048]{2,1,0:T(8,128)(2,1)}), bf16[64,8,2048]{2,1,0:T(8,128)(2,1)}, u32[]{:S(2)}, u32[]{:S(2)}) async-start(bf16[64,8,2048]{2,1,0:T(8,128)(2,1)} %bitcast.22), calls=%async_computation.5 | async-start | bytes 4194304 | tf_op jit(solution)/shard_map/all_to_all | solution.py:481
  293.8 1.6 collective-permute-done.7.refs_7_.refs_8_.refs_9_
  295.4 0.3 collective-permute-done.6.refs_5_
  295.7 23.4 %phased_sums.1 = (f32[1,2048,384]{2,1,0:T(8,128)}, f32[1,2048,384]{2,1,0:T(8,128)}, f32[1,384,2048]{2,1,0:T(8,128)}) custom-call(bf16[1024,2048]{1,0:T(8,128)(2,1)} %bitcast.21.refs_0_, bf16[1024,2048]{1,0:T(8,128)(2,1)} %bitcast.15.x_ref.refs_1_, bf16[1024,1152]{1,0:T(8,128)(2,1)} %get-tuple-element.67.refs_2_.refs_3_.refs_4_, ...), custom_call_target="tpu_custom_call" | custom-call | flops 805306368 | bytes 1048576 | tf_op jit(solution)/shard_map/phased_sums/pallas_call | solution.py:402
  319.1 1.7 all-to-all-done.5
  320.8 3.1 collective-permute-start.8
  323.9 4.2 %gradients.1.refs_2_ = bf16[512,768]{1,0:T(8,128)(2,1)} custom-call(bf16[512,2048]{1,0:T(8,128)(2,1)} %bitcast.23.q_ref.refs_0_, bf16[512,1152]{1,0:T(8,128)(2,1)} %get-tuple-element.74.silu_ref.us_ref.refs_3_, bf16[512,1152]{1,0:T(8,128)(2,1)} %get-tuple-element.74.silu_ref.us_ref.refs_3_, bf16[384,2048]{1,0:T(8,128)(2,1)} %bitcast.26), custom_call_target="tpu_custom_call" | custom-call | flops 50331648 | bytes 131072 | tf_op jit(solution)/shard_map/gradients/pallas_call | solution.py:332
  328.1 0.0 collective-permute-done.8.refs_4_
  328.1 14.4 %last_sums.1 = (f32[1,2048,384]{2,1,0:T(8,128)}, f32[1,2048,384]{2,1,0:T(8,128)}, f32[1,384,2048]{2,1,0:T(8,128)}) custom-call(bf16[512,2048]{1,0:T(8,128)(2,1)} %bitcast.23.q_ref.refs_0_, bf16[512,2048]{1,0:T(8,128)(2,1)} %bitcast.7.x_ref.refs_1_, bf16[512,768]{1,0:T(8,128)(2,1)} %gradients.1.refs_2_, ...), custom_call_target="tpu_custom_call" | custom-call | flops 352321536 | bytes 524288 | tf_op jit(solution)/shard_map/last_sums/pallas_call | solution.py:461
Async XLA Ops:
  4.4 39.4 %all-to-all-start = ((bf16[64,8,2048]{2,1,0:T(8,128)(2,1)}), bf16[64,8,2048]{2,1,0:T(8,128)(2,1)}, u32[]{:S(2)}, u32[]{:S(2)}) async-start(bf16[64,8,2048]{2,1,0:T(8,128)(2,1)} %bitcast.33), calls=%async_computation | async-start | bytes 4194304 | tf_op jit(solution)/shard_map/all_to_all | solution.py:481
  26.6 2.4 copy-start.1
  26.6 2.8 copy-start.2
  26.6 3.4 %copy-start.3 = (bf16[1,2048,384]{2,1,0:T(8,128)(2,1)S(1)}, bf16[1,2048,384]{2,1,0:T(8,128)(2,1)}, u32[]{:S(2)}) copy-start(bf16[1,2048,384]{2,1,0:T(8,128)(2,1)} %param.15) | copy-start | bytes 4718596
  26.6 4.9 %copy-start.4 = (bf16[1,2048,384]{2,1,0:T(8,128)(2,1)S(1)}, bf16[1,2048,384]{2,1,0:T(8,128)(2,1)}, u32[]{:S(2)}) copy-start(bf16[1,2048,384]{2,1,0:T(8,128)(2,1)} %param.14) | copy-start | bytes 4718596
  28.9 18.1 %copy-start = (bf16[768,2048]{1,0:T(8,128)(2,1)}, bf16[768,2048]{1,0:T(8,128)(2,1)S(1)}, u32[]{:S(2)}) copy-start(bf16[768,2048]{1,0:T(8,128)(2,1)S(1)} %pad_maximum_fusion.1.refs_2_) | copy-start | bytes 9437188
  43.8 18.1 %collective-permute-start = (bf16[2048,1536]{1,0:T(8,128)(2,1)}, bf16[2048,1536]{1,0:T(8,128)(2,1)}, u32[]{:S(2)}, u32[]{:S(2)}) collective-permute-start(bf16[2048,1536]{1,0:T(8,128)(2,1)} %pad_maximum_fusion.refs_0_), channel_id=1, source_target_pairs={{0,1},{1,0},{2,3},{3,2},{4,5},{5,4},{6,7},{7,6},{8,9},{9,8},{10,11... | collective-permute-start | bytes 18874376 | tf_op jit(solution)/shard_map/ppermute | solution.py:495
  47.0 14.9 %collective-permute-start.1 = (bf16[768,2048]{1,0:T(8,128)(2,1)S(1)}, bf16[768,2048]{1,0:T(8,128)(2,1)}, u32[]{:S(2)}, u32[]{:S(2)}) collective-permute-start(bf16[768,2048]{1,0:T(8,128)(2,1)S(1)} %pad_maximum_fusion.1.refs_2_), channel_id=1, source_target_pairs={{0,1},{1,0},{2,3},{3,2},{4,5},{5,4},{6,7},{7,6},{8,9},{9,8},{10,11... | collective-permute-start | bytes 9437192 | tf_op jit(solution)/shard_map/ppermute | solution.py:495
  47.0 58.5 %all-to-all-start.1 = ((bf16[64,16,2048]{2,1,0:T(8,128)(2,1)}), bf16[64,16,2048]{2,1,0:T(8,128)(2,1)}, u32[]{:S(2)}, u32[]{:S(2)}) async-start(bf16[64,16,2048]{2,1,0:T(8,128)(2,1)} %bitcast.28), calls=%async_computation.1 | async-start | bytes 8388608 | tf_op jit(solution)/shard_map/all_to_all | solution.py:481
  52.7 25.4 %collective-permute-start.2 = (bf16[512,2048]{1,0:T(8,128)(2,1)}, bf16[512,2048]{1,0:T(8,128)(2,1)}, u32[]{:S(2)}, u32[]{:S(2)}) collective-permute-start(bf16[512,2048]{1,0:T(8,128)(2,1)} %bitcast.7.x_ref.refs_1_), channel_id=1, source_target_pairs={{0,1},{1,0},{2,3},{3,2},{4,5},{5,4},{6,7},{7,6},{8,9},{9,8},{10,11... | collective-permute-start | bytes 6291464 | tf_op jit(solution)/shard_map/ppermute | solution.py:495
  77.8 27.7 %collective-permute-start.3 = (bf16[512,1152]{1,0:T(8,128)(2,1)}, bf16[512,1152]{1,0:T(8,128)(2,1)}, u32[]{:S(2)}, u32[]{:S(2)}) collective-permute-start(bf16[512,1152]{1,0:T(8,128)(2,1)} %get-tuple-element.53), channel_id=1, source_target_pairs={{0,1},{1,0},{2,3},{3,2},{4,5},{5,4},{6,7},{7,6},{8,9},{9,8},{10,11... | collective-permute-start | bytes 3538952 | tf_op jit(solution)/shard_map/ppermute | solution.py:495
  105.5 44.4 %collective-permute-start.4 = (bf16[1024,2048]{1,0:T(8,128)(2,1)}, bf16[1024,2048]{1,0:T(8,128)(2,1)}, u32[]{:S(2)}, u32[]{:S(2)}) collective-permute-start(bf16[1024,2048]{1,0:T(8,128)(2,1)} %bitcast.15.x_ref.refs_1_), channel_id=1, source_target_pairs={{0,1},{1,0},{2,3},{3,2},{4,5},{5,4},{6,7},{7,6},{8,9},{9,8},{10,11... | collective-permute-start | bytes 12582920 | tf_op jit(solution)/shard_map/ppermute | solution.py:495
  108.4 41.6 %all-to-all-start.2 = ((bf16[64,8,2048]{2,1,0:T(8,128)(2,1)}), bf16[64,8,2048]{2,1,0:T(8,128)(2,1)}, u32[]{:S(2)}, u32[]{:S(2)}) async-start(bf16[64,8,2048]{2,1,0:T(8,128)(2,1)} %bitcast.32), calls=%async_computation.2 | async-start | bytes 4194304 | tf_op jit(solution)/shard_map/all_to_all | solution.py:481
  212.9 6.0 %collective-permute-start.5 = (f32[128,2048]{1,0:T(8,128)}, f32[128,2048]{1,0:T(8,128)}, u32[]{:S(2)}, u32[]{:S(2)}) collective-permute-start(f32[128,2048]{1,0:T(8,128)} %combine.1.refs_7_), channel_id=1, source_target_pairs={{0,1},{1,0},{2,3},{3,2},{4,5},{5,4},{6,7},{7,6},{8,9},{9,8},{10,11... | collective-permute-start | bytes 3145736 | tf_op jit(solution)/shard_map/ppermute | solution.py:495
  225.8 59.4 %copy-start.5 = (bf16[1024,1152]{1,0:T(8,128)(2,1)S(1)}, bf16[1024,1152]{1,0:T(8,128)(2,1)}, u32[]{:S(2)}) copy-start(bf16[1024,1152]{1,0:T(8,128)(2,1)} %get-tuple-element.69) | copy-start | bytes 7077892
  282.1 13.6 %collective-permute-start.6 = (bf16[1024,2048]{1,0:T(8,128)(2,1)}, bf16[1024,2048]{1,0:T(8,128)(2,1)}, u32[]{:S(2)}, u32[]{:S(2)}) collective-permute-start(bf16[1024,2048]{1,0:T(8,128)(2,1)} %bitcast.21.refs_0_), channel_id=1, source_target_pairs={{0,1},{1,0},{2,3},{3,2},{4,5},{5,4},{6,7},{7,6},{8,9},{9,8},{10,11... | collective-permute-start | bytes 12582920 | tf_op jit(solution)/shard_map/ppermute | solution.py:495
  285.2 10.2 %collective-permute-start.7 = (bf16[1024,1152]{1,0:T(8,128)(2,1)S(1)}, bf16[1024,1152]{1,0:T(8,128)(2,1)}, u32[]{:S(2)}, u32[]{:S(2)}) collective-permute-start(bf16[1024,1152]{1,0:T(8,128)(2,1)S(1)} %copy-done.5), channel_id=1, source_target_pairs={{0,1},{1,0},{2,3},{3,2},{4,5},{5,4},{6,7},{7,6},{8,9},{9,8},{10,11... | collective-permute-start | bytes 7077896 | tf_op jit(solution)/shard_map/ppermute | solution.py:495
  285.2 35.6 %all-to-all-start.5 = ((bf16[64,8,2048]{2,1,0:T(8,128)(2,1)}), bf16[64,8,2048]{2,1,0:T(8,128)(2,1)}, u32[]{:S(2)}, u32[]{:S(2)}) async-start(bf16[64,8,2048]{2,1,0:T(8,128)(2,1)} %bitcast.22), calls=%async_computation.5 | async-start | bytes 4194304 | tf_op jit(solution)/shard_map/all_to_all | solution.py:481
  320.8 7.3 %collective-permute-start.8 = (bf16[512,2048]{1,0:T(8,128)(2,1)}, bf16[512,2048]{1,0:T(8,128)(2,1)}, u32[]{:S(2)}, u32[]{:S(2)}) collective-permute-start(bf16[512,2048]{1,0:T(8,128)(2,1)} %bitcast.23.q_ref.refs_0_), channel_id=1, source_target_pairs={{0,1},{1,0},{2,3},{3,2},{4,5},{5,4},{6,7},{7,6},{8,9},{9,8},{10,11... | collective-permute-start | bytes 6291464 | tf_op jit(solution)/shard_map/ppermute | solution.py:495

commit v6 on v5

--- a/solution.py
+++ b/solution.py
@@ -9,9 +9,9 @@
 F32 = jnp.float32
 GROUP = ("dp", "expert")
 VMEM_LIMIT = 63 * 1024 * 1024
-TILE = 256
+TILE = 512
 PIECE = 512
-LAST_PIECE = 1024
+LAST_PIECE = 512
 ROWS = 512
 SLOTS = (1, 2)
 COMBINE = 1024
@@ -379,9 +379,9 @@
             cols = pl.ds(pl.multiple_of(jnp.maximum(i - head, 0) * piece, piece), piece)
             gate_up = mm_rows(sides[0][1][...], g_ref[:count, :])
             gate_up += mm_rows(sides[1][1][...], g_ref[count:, :])
-            outs[0][0] = factor * gate_up[:, :hidden]
-            outs[1][0] = factor * gate_up[:, hidden:]
-            outs[2][0] = factor * mm(turned_ref[...], q_ref[:, cols])
+            outs[0][0] = (factor * gate_up[:, :hidden]).astype(BF)
+            outs[1][0] = (factor * gate_up[:, hidden:]).astype(BF)
+            outs[2][0] = (factor * mm(turned_ref[...], q_ref[:, cols])).astype(BF)
 
     def later(i):
         return jnp.maximum(i - head, 0)
@@ -408,7 +408,7 @@
             pl.BlockSpec((1, piece, hidden), lambda i: (0, later(i), 0)),
             pl.BlockSpec((1, hidden, piece), lambda i: (0, 0, later(i))),
         ],
-        out_shape=[jax.ShapeDtypeStruct(shape, F32) for shape in shapes],
+        out_shape=[jax.ShapeDtypeStruct(shape, BF) for shape in shapes],
         scratch_shapes=[
             pltpu.VMEM((2 * count, 2 * hidden), BF),
             pltpu.VMEM((hidden, 2 * count), BF),
@@ -444,7 +444,7 @@
         below = mm(turned_ref[:, :count], q_ref[...]) + mm(turned_ref[:, count:], q2_ref[:, cols])
         terms = (gate_up[:, :hidden], gate_up[:, hidden:], below)
         for out, term, begin in zip(outs, terms, begins):
-            out[0] = factor * term + begin[0]
+            out[0] = factor * term + begin[0].astype(F32)
 
     column = pl.BlockSpec((count, piece), lambda i: (0, i))
 

time: 344 us -> 343 us (level)
  no operation moved by 1% of the time
where the time goes in v6:
time: 343 us; the launch traced here: 342 us
  blocking collectives  114 us (33%)
  Pallas kernels  106 us (31%)
  waiting for transfers between devices  56.3 us (16%)
  starting transfers between devices  55.6 us (16%)
  other arithmetic  6.64 us (2%)
    all_to_all x2, blocking collectives, exchange(): return lax.all_to_all(rows, GROUP, split_axis=0, concat_axis=0, tiled=True)  114 us
    all_to_all x4, waiting for transfers between devices, exchange(): return lax.all_to_all(rows, GROUP, split_axis=0, concat_axis=0, tiled=True)  42.8 us
    pallas_call x2, Pallas kernels, forward(): pl.pallas_call(kernel, grid=(count // TILE,), in_specs=[pl.BlockSpec((TIL...  42.6 us
    all_to_all x4, starting transfers between devices, exchange(): return lax.all_to_all(rows, GROUP, split_axis=0, concat_axis=0, tiled=True)  39.1 us
    pallas_call x1, Pallas kernels, phased_sums(): pl.pallas_call(kernel, grid=(head + width // piece,), in_specs=specs(0) +...  23 us
    ppermute x9, starting transfers between devices, swap(): return lax.ppermute(rows, 'tensor', [(0, 1), (1, 0)])  16.4 us
    ppermute x9, waiting for transfers between devices, swap(): return lax.ppermute(rows, 'tensor', [(0, 1), (1, 0)])  13.4 us
    pallas_call x1, Pallas kernels, last_sums(): pl.pallas_call(kernel, grid=(width // piece,), in_specs=[column, column,...  13.4 us
  transfers between devices with their start and end apart: 13, of which 8 were waited for; matrix products, arithmetic and copies ran while one was open for 2% of the time, Pallas kernels for 23%

profile of v6, /device:TPU:1, one launch (start us, length us, event | category | flops | bytes accessed | tf_op | source)
XLA Modules:
  0.0 341.8 jit_solution(4851814786262896206)
XLA Ops:
  0.6 0.7 pad_add_fusion.1.base_ref.refs_1_
  1.3 3.2 route_pack.1
  4.5 12.2 %all-to-all-start = ((bf16[64,8,2048]{2,1,0:T(8,128)(2,1)}), bf16[64,8,2048]{2,1,0:T(8,128)(2,1)}, u32[]{:S(2)}, u32[]{:S(2)}) async-start(bf16[64,8,2048]{2,1,0:T(8,128)(2,1)} %bitcast.33), calls=%async_computation | async-start | bytes 4194304 | tf_op jit(solution)/shard_map/all_to_all | solution.py:481
  16.8 0.6 pad_add_fusion.base_ref.refs_0_
  17.4 1.6 gate_matrix.2.refs_0_
  19.0 1.8 gate_matrix.3.refs_2_
  20.8 3.8 %pack.1 = bf16[1024,2048]{1,0:T(8,128)(2,1)} custom-call(s32[2]{0:T(128)} %pad_add_fusion.base_ref.refs_0_, f32[64,128]{1,0:T(8,128)} %get-tuple-element.44.pos_ref.refs_2_.refs_4_, bf16[128,2048]{1,0:T(8,128)(2,1)} %tok_ref.3), custom_call_target="tpu_custom_call" | custom-call | flops 33554432 | bytes 262144 | tf_op jit(solution)/shard_map/pack/pallas_call | solution.py:122
  24.6 0.0 copy-start.1
  24.6 0.0 copy-start.2
  24.6 0.0 copy-start.3
  24.6 0.0 copy-start.4
  24.7 2.3 pad_maximum_fusion.1.refs_2_
  26.9 0.0 copy-start
  26.9 0.1 copy-done.1
  27.0 0.5 copy-done.2
  27.5 0.6 copy-done.3
  28.1 1.5 copy-done.4
  29.5 3.1 pad_maximum_fusion.refs_0_
  32.7 11.3 %all-to-all-done = bf16[64,8,2048]{2,1,0:T(8,128)(2,1)} async-done(((bf16[64,8,2048]{2,1,0:T(8,128)(2,1)}), bf16[64,8,2048]{2,1,0:T(8,128)(2,1)}, u32[]{:S(2)}, u32[]{:S(2)}) %all-to-all-start) | async-done | bytes 2097184 | tf_op jit(solution)/shard_map/all_to_all | solution.py:481
  44.0 3.2 collective-permute-start
  47.2 0.0 copy-done
  47.2 0.0 collective-permute-start.1
  47.2 5.7 %all-to-all-start.1 = ((bf16[64,16,2048]{2,1,0:T(8,128)(2,1)}), bf16[64,16,2048]{2,1,0:T(8,128)(2,1)}, u32[]{:S(2)}, u32[]{:S(2)}) async-start(bf16[64,16,2048]{2,1,0:T(8,128)(2,1)} %bitcast.28), calls=%async_computation.1 | async-start | bytes 8388608 | tf_op jit(solution)/shard_map/all_to_all | solution.py:481
  52.9 0.6 collective-permute-start.2
  53.5 8.6 %collective-permute-done.1.refs_3_ = bf16[768,2048]{1,0:T(8,128)(2,1)} collective-permute-done((bf16[768,2048]{1,0:T(8,128)(2,1)S(1)}, bf16[768,2048]{1,0:T(8,128)(2,1)}, u32[]{:S(2)}, u32[]{:S(2)}) %collective-permute-start.1) | collective-permute-done | bytes 3145760 | tf_op jit(solution)/shard_map/ppermute | solution.py:495
  62.1 0.0 collective-permute-done.refs_1_
  62.1 16.0 %forward.2 = (bf16[512,2048]{1,0:T(8,128)(2,1)}, bf16[512,1152]{1,0:T(8,128)(2,1)}, bf16[512,1152]{1,0:T(8,128)(2,1)}) custom-call(bf16[512,2048]{1,0:T(8,128)(2,1)} %bitcast.7.x_ref.refs_1_, bf16[2048,1536]{1,0:T(8,128)(2,1)} %pad_maximum_fusion.refs_0_, bf16[2048,1536]{1,0:T(8,128)(2,1)} %collective-permute-done.refs_1_, bf16[768,2048]{1,0:T(8,128)(2,1)} %copy-done, ...), custom_call_target="tpu_custom_call" | custom-call | flops 603979776 | bytes 524288 | tf_op jit(solution)/shard_map/forward/pallas_call | solution.py:182
  78.1 0.2 collective-permute-start.3
  78.3 0.0 collective-permute-done.2.refs_5_
  78.3 27.4 %all-to-all-done.1 = bf16[64,16,2048]{2,1,0:T(8,128)(2,1)} async-done(((bf16[64,16,2048]{2,1,0:T(8,128)(2,1)}), bf16[64,16,2048]{2,1,0:T(8,128)(2,1)}, u32[]{:S(2)}, u32[]{:S(2)}) %all-to-all-start.1) | async-done | bytes 4194336 | tf_op jit(solution)/shard_map/all_to_all | solution.py:481
  105.7 0.0 collective-permute-done.3.refs_6_.refs_7_.refs_8_
  105.7 2.9 collective-permute-start.4
  108.5 12.9 %all-to-all-start.2 = ((bf16[64,8,2048]{2,1,0:T(8,128)(2,1)}), bf16[64,8,2048]{2,1,0:T(8,128)(2,1)}, u32[]{:S(2)}, u32[]{:S(2)}) async-start(bf16[64,8,2048]{2,1,0:T(8,128)(2,1)} %bitcast.32), calls=%async_computation.2 | async-start | bytes 4194304 | tf_op jit(solution)/shard_map/all_to_all | solution.py:481
  121.5 26.6 %forward.3 = (bf16[1024,2048]{1,0:T(8,128)(2,1)}, bf16[1024,1152]{1,0:T(8,128)(2,1)}, bf16[1024,1152]{1,0:T(8,128)(2,1)}) custom-call(bf16[1024,2048]{1,0:T(8,128)(2,1)} %bitcast.15.x_ref.refs_1_, bf16[2048,1536]{1,0:T(8,128)(2,1)} %pad_maximum_fusion.refs_0_, bf16[2048,1536]{1,0:T(8,128)(2,1)} %collective-permute-done.refs_1_, bf16[768,2048]{1,0:T(8,128)(2,1)} %copy-done, ...), custom_call_target="tpu_custom_call" | custom-call | flops 1207959552 | bytes 1048576 | tf_op jit(solution)/shard_map/forward/pallas_call | solution.py:182
  148.1 2.0 all-to-all-done.2
  150.1 0.0 collective-permute-done.4.refs_6_
  150.1 57.8 %all_to_all.72 = bf16[64,16,2048]{2,1,0:T(8,128)(2,1)} all-to-all(bf16[64,16,2048]{2,1,0:T(8,128)(2,1)} %bitcast.30), channel_id=1, replica_groups=mesh['dp'=4,'expert'=16,'tensor'=2] {'dp','expert'}, dimensions={0} | all-to-all | bytes 8388608 | tf_op jit(solution)/shard_map/all_to_all | solution.py:481
  207.9 4.9 %combine.1.refs_7_ = f32[128,2048]{1,0:T(8,128)} custom-call(bf16[256,512]{1,0:T(8,128)(2,1)} %gate_matrix.2.refs_0_, bf16[512,2048]{1,0:T(8,128)(2,1)} %bitcast.17.refs_1_, bf16[256,1024]{1,0:T(8,128)(2,1)} %gate_matrix.3.refs_2_, bf16[1024,2048]{1,0:T(8,128)(2,1)} %bitcast.29), custom_call_target="tpu_custom_call" | custom-call | flops 100663296 | bytes 393216 | tf_op jit(solution)/shard_map/combine/pallas_call | solution.py:250
  212.8 3.3 collective-permute-start.5
  216.2 2.6 collective-permute-done.5.refs_8_
  218.8 7.0 %weigh_pack.1 = (bf16[1024,2048]{1,0:T(8,128)(2,1)}, bf16[512,2048]{1,0:T(8,128)(2,1)}, bf16[128,1024]{1,0:T(8,128)(2,1)}) custom-call(s32[2]{0:T(128)} %pad_add_fusion.base_ref.refs_0_, s32[2]{0:T(128)} %pad_add_fusion.1.base_ref.refs_1_, f32[64,128]{1,0:T(8,128)} %get-tuple-element.44.pos_ref.refs_2_.refs_4_, ...), custom_call_target="tpu_custom_call" | custom-call | flops 100663296 | bytes 393216 | tf_op jit(solution)/shard_map/weigh_pack/pallas_call | solution.py:305
  225.8 0.0 copy-start.5
  225.8 56.3 %all_to_all.73 = bf16[64,16,2048]{2,1,0:T(8,128)(2,1)} all-to-all(bf16[64,16,2048]{2,1,0:T(8,128)(2,1)} %bitcast.31), channel_id=1, replica_groups=mesh['dp'=4,'expert'=16,'tensor'=2] {'dp','expert'}, dimensions={0} | all-to-all | bytes 8388608 | tf_op jit(solution)/shard_map/all_to_all | solution.py:481
  282.1 3.1 collective-permute-start.6
  285.2 0.0 copy-done.5
  285.2 0.0 collective-permute-start.7
  285.2 8.3 %all-to-all-start.5 = ((bf16[64,8,2048]{2,1,0:T(8,128)(2,1)}), bf16[64,8,2048]{2,1,0:T(8,128)(2,1)}, u32[]{:S(2)}, u32[]{:S(2)}) async-start(bf16[64,8,2048]{2,1,0:T(8,128)(2,1)} %bitcast.22), calls=%async_computation.5 | async-start | bytes 4194304 | tf_op jit(solution)/shard_map/all_to_all | solution.py:481
  293.5 1.8 collective-permute-done.7.refs_7_.refs_8_.refs_9_
  295.3 0.3 collective-permute-done.6.refs_5_
  295.7 23.0 %phased_sums.1 = (bf16[1,2048,384]{2,1,0:T(8,128)(2,1)}, bf16[1,2048,384]{2,1,0:T(8,128)(2,1)}, bf16[1,384,2048]{2,1,0:T(8,128)(2,1)}) custom-call(bf16[1024,2048]{1,0:T(8,128)(2,1)} %bitcast.21.refs_0_, bf16[1024,2048]{1,0:T(8,128)(2,1)} %bitcast.15.x_ref.refs_1_, bf16[1024,1152]{1,0:T(8,128)(2,1)} %get-tuple-element.67.refs_2_.refs_3_.refs_4_, ...), custom_call_target="tpu_custom_call" | custom-call | flops 805306368 | bytes 1048576 | tf_op jit(solution)/shard_map/phased_sums/pallas_call | solution.py:402
  318.7 2.1 all-to-all-done.5
  320.8 3.1 collective-permute-start.8
  323.9 4.5 %gradients.1.refs_2_ = bf16[512,768]{1,0:T(8,128)(2,1)} custom-call(bf16[512,2048]{1,0:T(8,128)(2,1)} %bitcast.23.q_ref.refs_0_, bf16[512,1152]{1,0:T(8,128)(2,1)} %get-tuple-element.74.silu_ref.us_ref.refs_3_, bf16[512,1152]{1,0:T(8,128)(2,1)} %get-tuple-element.74.silu_ref.us_ref.refs_3_, bf16[384,2048]{1,0:T(8,128)(2,1)} %bitcast.26), custom_call_target="tpu_custom_call" | custom-call | flops 50331648 | bytes 131072 | tf_op jit(solution)/shard_map/gradients/pallas_call | solution.py:332
  328.4 0.0 collective-permute-done.8.refs_4_
  328.4 13.4 %last_sums.1 = (f32[1,2048,384]{2,1,0:T(8,128)}, f32[1,2048,384]{2,1,0:T(8,128)}, f32[1,384,2048]{2,1,0:T(8,128)}) custom-call(bf16[512,2048]{1,0:T(8,128)(2,1)} %bitcast.23.q_ref.refs_0_, bf16[512,2048]{1,0:T(8,128)(2,1)} %bitcast.7.x_ref.refs_1_, bf16[512,768]{1,0:T(8,128)(2,1)} %gradients.1.refs_2_, ...), custom_call_target="tpu_custom_call" | custom-call | flops 352321536 | bytes 524288 | tf_op jit(solution)/shard_map/last_sums/pallas_call | solution.py:461
Async XLA Ops:
  4.5 39.4 %all-to-all-start = ((bf16[64,8,2048]{2,1,0:T(8,128)(2,1)}), bf16[64,8,2048]{2,1,0:T(8,128)(2,1)}, u32[]{:S(2)}, u32[]{:S(2)}) async-start(bf16[64,8,2048]{2,1,0:T(8,128)(2,1)} %bitcast.33), calls=%async_computation | async-start | bytes 4194304 | tf_op jit(solution)/shard_map/all_to_all | solution.py:481
  24.6 2.4 copy-start.1
  24.6 2.8 copy-start.2
  24.6 3.4 %copy-start.3 = (bf16[1,2048,384]{2,1,0:T(8,128)(2,1)S(1)}, bf16[1,2048,384]{2,1,0:T(8,128)(2,1)}, u32[]{:S(2)}) copy-start(bf16[1,2048,384]{2,1,0:T(8,128)(2,1)} %param.15) | copy-start | bytes 4718596
  24.6 4.9 %copy-start.4 = (bf16[1,2048,384]{2,1,0:T(8,128)(2,1)S(1)}, bf16[1,2048,384]{2,1,0:T(8,128)(2,1)}, u32[]{:S(2)}) copy-start(bf16[1,2048,384]{2,1,0:T(8,128)(2,1)} %param.14) | copy-start | bytes 4718596
  26.9 20.3 %copy-start = (bf16[768,2048]{1,0:T(8,128)(2,1)}, bf16[768,2048]{1,0:T(8,128)(2,1)S(1)}, u32[]{:S(2)}) copy-start(bf16[768,2048]{1,0:T(8,128)(2,1)S(1)} %pad_maximum_fusion.1.refs_2_) | copy-start | bytes 9437188
  44.0 18.1 %collective-permute-start = (bf16[2048,1536]{1,0:T(8,128)(2,1)}, bf16[2048,1536]{1,0:T(8,128)(2,1)}, u32[]{:S(2)}, u32[]{:S(2)}) collective-permute-start(bf16[2048,1536]{1,0:T(8,128)(2,1)} %pad_maximum_fusion.refs_0_), channel_id=1, source_target_pairs={{0,1},{1,0},{2,3},{3,2},{4,5},{5,4},{6,7},{7,6},{8,9},{9,8},{10,11... | collective-permute-start | bytes 18874376 | tf_op jit(solution)/shard_map/ppermute | solution.py:495
  47.2 14.9 %collective-permute-start.1 = (bf16[768,2048]{1,0:T(8,128)(2,1)S(1)}, bf16[768,2048]{1,0:T(8,128)(2,1)}, u32[]{:S(2)}, u32[]{:S(2)}) collective-permute-start(bf16[768,2048]{1,0:T(8,128)(2,1)S(1)} %pad_maximum_fusion.1.refs_2_), channel_id=1, source_target_pairs={{0,1},{1,0},{2,3},{3,2},{4,5},{5,4},{6,7},{7,6},{8,9},{9,8},{10,11... | collective-permute-start | bytes 9437192 | tf_op jit(solution)/shard_map/ppermute | solution.py:495
  47.2 58.5 %all-to-all-start.1 = ((bf16[64,16,2048]{2,1,0:T(8,128)(2,1)}), bf16[64,16,2048]{2,1,0:T(8,128)(2,1)}, u32[]{:S(2)}, u32[]{:S(2)}) async-start(bf16[64,16,2048]{2,1,0:T(8,128)(2,1)} %bitcast.28), calls=%async_computation.1 | async-start | bytes 8388608 | tf_op jit(solution)/shard_map/all_to_all | solution.py:481
  52.9 25.4 %collective-permute-start.2 = (bf16[512,2048]{1,0:T(8,128)(2,1)}, bf16[512,2048]{1,0:T(8,128)(2,1)}, u32[]{:S(2)}, u32[]{:S(2)}) collective-permute-start(bf16[512,2048]{1,0:T(8,128)(2,1)} %bitcast.7.x_ref.refs_1_), channel_id=1, source_target_pairs={{0,1},{1,0},{2,3},{3,2},{4,5},{5,4},{6,7},{7,6},{8,9},{9,8},{10,11... | collective-permute-start | bytes 6291464 | tf_op jit(solution)/shard_map/ppermute | solution.py:495
  78.1 27.6 %collective-permute-start.3 = (bf16[512,1152]{1,0:T(8,128)(2,1)}, bf16[512,1152]{1,0:T(8,128)(2,1)}, u32[]{:S(2)}, u32[]{:S(2)}) collective-permute-start(bf16[512,1152]{1,0:T(8,128)(2,1)} %get-tuple-element.53), channel_id=1, source_target_pairs={{0,1},{1,0},{2,3},{3,2},{4,5},{5,4},{6,7},{7,6},{8,9},{9,8},{10,11... | collective-permute-start | bytes 3538952 | tf_op jit(solution)/shard_map/ppermute | solution.py:495
  105.7 44.4 %collective-permute-start.4 = (bf16[1024,2048]{1,0:T(8,128)(2,1)}, bf16[1024,2048]{1,0:T(8,128)(2,1)}, u32[]{:S(2)}, u32[]{:S(2)}) collective-permute-start(bf16[1024,2048]{1,0:T(8,128)(2,1)} %bitcast.15.x_ref.refs_1_), channel_id=1, source_target_pairs={{0,1},{1,0},{2,3},{3,2},{4,5},{5,4},{6,7},{7,6},{8,9},{9,8},{10,11... | collective-permute-start | bytes 12582920 | tf_op jit(solution)/shard_map/ppermute | solution.py:495
  108.5 41.5 %all-to-all-start.2 = ((bf16[64,8,2048]{2,1,0:T(8,128)(2,1)}), bf16[64,8,2048]{2,1,0:T(8,128)(2,1)}, u32[]{:S(2)}, u32[]{:S(2)}) async-start(bf16[64,8,2048]{2,1,0:T(8,128)(2,1)} %bitcast.32), calls=%async_computation.2 | async-start | bytes 4194304 | tf_op jit(solution)/shard_map/all_to_all | solution.py:481
  212.8 5.9 %collective-permute-start.5 = (f32[128,2048]{1,0:T(8,128)}, f32[128,2048]{1,0:T(8,128)}, u32[]{:S(2)}, u32[]{:S(2)}) collective-permute-start(f32[128,2048]{1,0:T(8,128)} %combine.1.refs_7_), channel_id=1, source_target_pairs={{0,1},{1,0},{2,3},{3,2},{4,5},{5,4},{6,7},{7,6},{8,9},{9,8},{10,11... | collective-permute-start | bytes 3145736 | tf_op jit(solution)/shard_map/ppermute | solution.py:495
  225.8 59.4 %copy-start.5 = (bf16[1024,1152]{1,0:T(8,128)(2,1)S(1)}, bf16[1024,1152]{1,0:T(8,128)(2,1)}, u32[]{:S(2)}) copy-start(bf16[1024,1152]{1,0:T(8,128)(2,1)} %get-tuple-element.69) | copy-start | bytes 7077892
  282.1 13.6 %collective-permute-start.6 = (bf16[1024,2048]{1,0:T(8,128)(2,1)}, bf16[1024,2048]{1,0:T(8,128)(2,1)}, u32[]{:S(2)}, u32[]{:S(2)}) collective-permute-start(bf16[1024,2048]{1,0:T(8,128)(2,1)} %bitcast.21.refs_0_), channel_id=1, source_target_pairs={{0,1},{1,0},{2,3},{3,2},{4,5},{5,4},{6,7},{7,6},{8,9},{9,8},{10,11... | collective-permute-start | bytes 12582920 | tf_op jit(solution)/shard_map/ppermute | solution.py:495
  285.2 10.2 %collective-permute-start.7 = (bf16[1024,1152]{1,0:T(8,128)(2,1)S(1)}, bf16[1024,1152]{1,0:T(8,128)(2,1)}, u32[]{:S(2)}, u32[]{:S(2)}) collective-permute-start(bf16[1024,1152]{1,0:T(8,128)(2,1)S(1)} %copy-done.5), channel_id=1, source_target_pairs={{0,1},{1,0},{2,3},{3,2},{4,5},{5,4},{6,7},{7,6},{8,9},{9,8},{10,11... | collective-permute-start | bytes 7077896 | tf_op jit(solution)/shard_map/ppermute | solution.py:495
  285.2 35.6 %all-to-all-start.5 = ((bf16[64,8,2048]{2,1,0:T(8,128)(2,1)}), bf16[64,8,2048]{2,1,0:T(8,128)(2,1)}, u32[]{:S(2)}, u32[]{:S(2)}) async-start(bf16[64,8,2048]{2,1,0:T(8,128)(2,1)} %bitcast.22), calls=%async_computation.5 | async-start | bytes 4194304 | tf_op jit(solution)/shard_map/all_to_all | solution.py:481
  320.8 7.6 %collective-permute-start.8 = (bf16[512,2048]{1,0:T(8,128)(2,1)}, bf16[512,2048]{1,0:T(8,128)(2,1)}, u32[]{:S(2)}, u32[]{:S(2)}) collective-permute-start(bf16[512,2048]{1,0:T(8,128)(2,1)} %bitcast.23.q_ref.refs_0_), channel_id=1, source_target_pairs={{0,1},{1,0},{2,3},{3,2},{4,5},{5,4},{6,7},{7,6},{8,9},{9,8},{10,11... | collective-permute-start | bytes 6291464 | tf_op jit(solution)/shard_map/ppermute | solution.py:495
